TPU v7x, 32 devices: a whole 2x2x4 slice. The times are simulated.
32 devices in a mesh: cfg: 2 (over y), ta: 4 (over z), gz: 2 (over x), gy: 2 (over core).
Axes of the slice: x: 2, y: 2, z: 4, core: 2. Of those that a mesh axis runs over, the one named last changes fastest.
Arguments:
- eigen_store: bfloat16 [20, 3, 2, 24, 6, 256], P(None, None, None, ('cfg', 'ta'), 'gz', 'gy'), parts along dimension 3, may hold values from -6 to 6
- fat_links: bfloat16 [2, 4, 3, 3, 2, 24, 6, 256], P(None, None, None, None, None, ('cfg', 'ta'), 'gz', 'gy'), parts along dimension 5, may hold values from -0.59765625 to 0.59765625
- long_links: bfloat16 [2, 4, 3, 3, 2, 24, 6, 256], P(None, None, None, None, None, ('cfg', 'ta'), 'gz', 'gy'), parts along dimension 5, may hold values from -0.29882812 to 0.29882812
- chosen: int32 [32], P('cfg'), parts along dimension 0, may hold values from 0 to 19, as said below
- momenta: int32 [8, 3], replicated, may hold values from -2 to 2
- current_dirs: int32 [4], replicated, may hold values from 1 to 3
- taste_masks: int32 [4], replicated, may hold values from 0 to 7
Outputs:
- odd_vectors: bfloat16 [16, 3, 2, 24, 6, 256], P(None, None, None, ('cfg', 'ta'), 'gz', 'gy'), parts along dimension 3
- meson_fields: float32 [32, 24, 2, 16, 16], P(('gz', 'gy'), ('cfg', 'ta')), parts along dimension 1
There are 2 independent parts, one for each index of `cfg`. A program takes and returns all parts, laid end to end along the dimension named above; an argument that names none is the same for every part. Nothing has to cross between parts.
Inputs may be any that keep to these rules, and one draw needn't show every extreme that they name: `chosen`: the 16 indices are distinct.
All inputs are finite; a program needn't handle non-finite values.
Results may differ from a plain program's by a relative error of at most 0.001.
Values may be sent and summed in bfloat16 or wider, within the bound.
No kernel may reach another device: no remote copies, remote signals or barrier semaphores. Data moves between devices by JAX's collectives and lax.ppermute only.
A program may use at most 128 MiB of HBM per device.

v0:
```python
import functools
import math

import jax
import jax.numpy as jnp
from jax import lax
from jax.experimental import pallas as pl
from jax.experimental.pallas import tpu as pltpu
from jax.sharding import PartitionSpec as P

NX = 64
HALF = NX // 2
LANES = 128
F32 = jnp.float32
BF16 = jnp.bfloat16
VM = pl.BlockSpec(memory_space=pltpu.VMEM)
SM = pl.BlockSpec(memory_space=pltpu.SMEM)
HB = pl.BlockSpec(memory_space=pl.ANY)


def call(body, outs, ins, scratch, flops, bytes_accessed):
    return pl.pallas_call(
        body,
        out_shape=outs,
        in_specs=ins,
        out_specs=[VM] * len(outs),
        scratch_shapes=scratch,
        compiler_params=pltpu.CompilerParams(vmem_limit_bytes=40 * 1024 * 1024),
        cost_estimate=pl.CostEstimate(
            flops=flops, bytes_accessed=bytes_accessed, transcendentals=0
        ),
    )


def gather_kernel(chosen, store, out, wide, turned):
    vectors = chosen.shape[0]
    rows = out.shape[0] // vectors
    wide[: store.shape[0], :] = store[...].astype(F32)
    full = rows // 8
    rest = rows - 8 * full
    for n in range(vectors):
        start = chosen[n] * rows
        for q in range(full):
            turned[pl.ds(q * 8 * vectors + n, 8, stride=vectors), :] = wide[
                pl.ds(start + 8 * q, 8), :
            ]
        if rest:
            turned[pl.ds(full * 8 * vectors + n, rest, stride=vectors), :] = wide[
                pl.ds(start + 8 * full, rest), :
            ]
    out[...] = turned[...].astype(BF16)


class Links:
    def __init__(self, ref, times, depth):
        self.ref, self.times, self.depth = ref, times, depth

    def row(self, w, mu, a, b, t, z, ri):
        at = (((((w * 4 + mu) * 3 + a) * 3 + b) * self.times + t) * self.depth + z) * 2 + ri
        return self.ref[at : at + 1, :]


def add_hop(acc, links, w, mu, t, z, vec, minus):
    for a in range(3):
        for b in range(3):
            lr = links.row(w, mu, a, b, t, z, 0)
            li = links.row(w, mu, a, b, t, z, 1)
            vr, vi = vec[b]
            if minus:
                acc[a][0] = (acc[a][0] - lr * vr) + li * vi
                acc[a][1] = (acc[a][1] - lr * vi) - li * vr
            else:
                acc[a][0] = (acc[a][0] + lr * vr) - li * vi
                acc[a][1] = (acc[a][1] + lr * vi) + li * vr


def zeros(vectors):
    return [[jnp.zeros((vectors, LANES), F32) for _ in range(2)] for _ in range(3)]


def read(ref, t, z):
    return [[ref[a, t, z, ri].astype(F32) for ri in range(2)] for a in range(3)]


def write(ref, t, z, acc):
    for a in range(3):
        for ri in range(2):
            ref[a, t, z, ri] = acc[a][ri].astype(ref.dtype)


def subtract(acc, other):
    for a in range(3):
        for ri in range(2):
            acc[a][ri] = acc[a][ri] - other[a][ri]


def split_hops(product, vectors, count):
    out = []
    for h in range(count):
        cols = product[:, h * LANES : (h + 1) * LANES]
        out.append(
            [
                [cols[(a * 2 + ri) * vectors : (a * 2 + ri + 1) * vectors] for ri in range(2)]
                for a in range(3)
            ]
        )
    return out


OFFSETS = (1, -1, 3, -3)


def x_permutation(e):
    src = lax.broadcasted_iota(jnp.int32, (LANES, 4 * LANES), 0)
    col = lax.broadcasted_iota(jnp.int32, (LANES, 4 * LANES), 1)
    h = col // LANES
    dst = col % LANES
    y = dst // HALF
    k = dst % HALF
    s = (e + y) % 2
    lead = jnp.where(h == 0, 1, jnp.where(h == 1, 0, jnp.where(h == 2, 2, -1)))
    want = y * HALF + (k + lead - s + HALF) % HALF
    return jnp.where(src == want, 1.0, 0.0).astype(BF16)


def y_permutation():
    rows = LANES // HALF
    src = lax.broadcasted_iota(jnp.int32, (2 * LANES, 4 * LANES), 0)
    col = lax.broadcasted_iota(jnp.int32, (2 * LANES, 4 * LANES), 1)
    h = col // LANES
    dst = col % LANES
    y = dst // HALF
    k = dst % HALF
    d = jnp.where(h == 0, 1, jnp.where(h == 1, -1, jnp.where(h == 2, 3, -3)))
    want = ((y + d + 2 * rows) % (2 * rows)) * HALF + k
    return jnp.where(src == want, 1.0, 0.0).astype(BF16)


def local_kernel(times, depth, field, fat, long, dacc, back_x, fatf, longf, perm):
    vectors = field.shape[4]
    fatf[...] = fat[...].astype(F32)
    longf[...] = long[...].astype(F32)
    fat_l, long_l = Links(fatf, times, depth), Links(longf, times, depth)
    origin = lax.axis_index("ta") * times + lax.axis_index("gz") * depth
    for e in range(2):
        perm[e] = x_permutation(origin + e)
    for t in range(times):
        for z in range(depth):
            here = field[:, t, z].reshape(6 * vectors, LANES)
            moved = jnp.dot(here, perm[(t + z) % 2], preferred_element_type=F32)
            plus1, minus1, plus3, minus3 = split_hops(moved, vectors, 4)
            acc = zeros(vectors)
            add_hop(acc, fat_l, 1, 3, t, z, minus1, False)
            write(back_x, t, z, acc)
            for a in range(3):
                for ri in range(2):
                    acc[a][ri] = -acc[a][ri]
            add_hop(acc, fat_l, 0, 3, t, z, plus1, False)
            add_hop(acc, long_l, 0, 3, t, z, plus3, False)
            add_hop(acc, long_l, 1, 3, t, z, minus3, True)
            if t + 1 < times:
                add_hop(acc, fat_l, 0, 0, t, z, read(field, t + 1, z), False)
            if t >= 1:
                add_hop(acc, fat_l, 1, 0, t, z, read(field, t - 1, z), True)
            if z + 1 < depth:
                add_hop(acc, fat_l, 0, 1, t, z, read(field, t, z + 1), False)
            write(dacc, t, z, acc)


def turn_split(value):
    high = value.astype(BF16)
    low = (value - high.astype(F32)).astype(BF16)
    return high, low


def sincos_turns(turns):
    quarters = 4.0 * (turns - jnp.floor(turns + 0.5))
    near = jnp.floor(quarters + 0.5)
    x = (quarters - near) * (0.5 * math.pi)
    x2 = x * x
    s = x * (1.0 + x2 * (-1.0 / 6 + x2 * (1.0 / 120 + x2 * (-1.0 / 5040 + x2 / 362880))))
    c = 1.0 + x2 * (-0.5 + x2 * (1.0 / 24 + x2 * (-1.0 / 720 + x2 * (1.0 / 40320))))
    which = near.astype(jnp.int32) & 3
    odd = (which & 1) == 1
    cosine = jnp.where(odd, s, c)
    sine = jnp.where(odd, c, s)
    cosine = jnp.where((which == 1) | (which == 2), -cosine, cosine)
    sine = jnp.where(which >= 2, -sine, sine)
    return cosine, sine


def side_kernel(
    times, depth, sizes, rotate,
    momenta, dirs, masks, field, yfield, zprev, znext, fat, long, dacc_in, back_x,
    dacc, left_hi, left_lo, weights, fatf, longf, perm, back,
):
    vectors = field.shape[4]
    total_y, total_z, scale = sizes
    fatf[...] = fat[...].astype(F32)
    longf[...] = long[...].astype(F32)
    fat_l, long_l = Links(fatf, times, depth), Links(longf, times, depth)
    perm[...] = y_permutation()
    lane = lax.broadcasted_iota(jnp.int32, (8, LANES), 1)
    sub = lax.broadcasted_iota(jnp.int32, (8, LANES), 0)
    k = lane % HALF
    y_glob = lax.axis_index("gy") * (LANES // HALF) + lane // HALF
    quarters = [jnp.zeros((8, LANES), F32) for _ in range(3)]
    for p in range(8):
        for axis in range(3):
            quarters[axis] = jnp.where(sub == p, momenta[axis, p].astype(F32), quarters[axis])
    slots = dirs.shape[0]
    if rotate:
        gz, gy = lax.axis_index("gz"), lax.axis_index("gy")
        current_of = [((gz + d // 2) % 2) * 2 + (gy + d % 2) % 2 for d in range(slots)]
    else:
        current_of = list(range(slots))
    for t in range(times):
        for z in range(depth):
            here = jnp.concatenate(
                [
                    field[:, t, z].reshape(6 * vectors, LANES),
                    yfield[:, t, z].reshape(6 * vectors, LANES),
                ],
                axis=1,
            )
            moved = jnp.dot(here, perm[...], preferred_element_type=F32)
            plus1, minus1, plus3, minus3 = split_hops(moved, vectors, 4)
            back_y, back_z = zeros(vectors), zeros(vectors)
            add_hop(back_y, fat_l, 1, 2, t, z, minus1, False)
            for a in range(3):
                for ri in range(2):
                    back[1, a, t, z, ri] = back_y[a][ri]
                    back[2, a, t, z, ri] = back_x[a, t, z, ri]
            acc = read(dacc_in, t, z)
            subtract(acc, back_y)
            source = read(field, t, z - 1) if z >= 1 else read(zprev, t, depth - 1)
            add_hop(back_z, fat_l, 1, 1, t, z, source, False)
            for a in range(3):
                for ri in range(2):
                    back[0, a, t, z, ri] = back_z[a][ri]
            subtract(acc, back_z)
            add_hop(acc, fat_l, 0, 2, t, z, plus1, False)
            add_hop(acc, long_l, 0, 2, t, z, plus3, False)
            add_hop(acc, long_l, 1, 2, t, z, minus3, True)
            if z + 1 == depth:
                add_hop(acc, fat_l, 0, 1, t, z, read(znext, t, 0), False)
            add_hop(acc, long_l, 0, 1, t, z, read(znext, t, z), False)
            add_hop(acc, long_l, 1, 1, t, z, read(zprev, t, z), True)
            write(dacc, t, z, acc)

            t_glob = lax.axis_index("ta") * times + t
            z_glob = lax.axis_index("gz") * depth + z
            x_glob = 2 * k + 1 - (t_glob + z_glob + y_glob) % 2
            turns = (
                quarters[0] * (x_glob.astype(F32) * (1.0 / NX))
                + quarters[1] * (y_glob.astype(F32) * (1.0 / total_y))
                + quarters[2] * (z_glob.astype(F32) * (1.0 / total_z))
            )
            cosine, sine = sincos_turns(turns)
            weights[t * depth + z, 0:8] = cosine * scale
            weights[t * depth + z, 8:16] = sine * scale

            x_row, y_row = x_glob[0:1], y_glob[0:1]
            for slot in range(slots):
                current = current_of[slot]
                direction = dirs[current] - 1
                mask = masks[current]
                exponent = (
                    (mask & 1) * x_row + ((mask >> 1) & 1) * y_row + ((mask >> 2) & 1) * z_glob
                )
                sign = (1 - 2 * (exponent & 1)).astype(F32)
                for a in range(3):
                    real_h, real_l = turn_split(back[direction, a, t, z, 0] * sign)
                    imag_h, imag_l = turn_split(back[direction, a, t, z, 1] * sign)
                    col = (z * 3 + a) * 2 * LANES
                    first = slice(col, col + LANES)
                    other = slice(col + LANES, col + 2 * LANES)
                    top = slice(slot * 2 * vectors, slot * 2 * vectors + vectors)
                    low = slice(slot * 2 * vectors + vectors, (slot + 1) * 2 * vectors)
                    for ref, re, im in (
                        (left_hi, real_h, imag_h),
                        (left_lo, real_l, imag_l),
                    ):
                        ref[t, top, first] = re
                        ref[t, top, other] = im
                        ref[t, low, first] = -im
                        ref[t, low, other] = re


NT_DIMS = (((1,), (1,)), ((), ()))


def last_kernel(
    times, depth,
    dacc, afield, bfield, fat, long, weights, left_hi_hbm, left_lo_hbm,
    dirac16, *rest,
):
    pieces = rest[:4]
    fatf, longf, dirac, left_hi, left_lo, right_hi, right_lo, sems = rest[4:]
    vectors = dacc.shape[4]
    copies = [
        pltpu.make_async_copy(left_hi_hbm, left_hi, sems.at[0]),
        pltpu.make_async_copy(left_lo_hbm, left_lo, sems.at[1]),
    ]
    for copy in copies:
        copy.start()
    fatf[...] = fat[...].astype(F32)
    longf[...] = long[...].astype(F32)
    fat_l, long_l = Links(fatf, times, depth), Links(longf, times, depth)

    def hops(after, before):
        for t in range(times):
            for z in range(depth):
                acc = read(dacc, t, z)
                add_hop(acc, long_l, 0, 0, t, z, read(after, t, z), False)
                add_hop(acc, long_l, 1, 0, t, z, read(before, t, z), True)
                if t + 1 == times:
                    add_hop(acc, fat_l, 0, 0, t, z, read(after, 0, z), False)
                if t == 0:
                    add_hop(acc, fat_l, 1, 0, t, z, read(before, times - 1, z), True)
                write(dirac, t, z, acc)

    even = lax.axis_index("ta") % 2 == 0

    @pl.when(even)
    def _():
        hops(afield, bfield)

    @pl.when(jnp.logical_not(even))
    def _():
        hops(bfield, afield)

    dirac16[...] = dirac[...].astype(BF16)
    for copy in copies:
        copy.wait()
    rows = 2 * vectors
    for t in range(times):
        for z in range(depth):
            for a in range(3):
                for ri in range(2):
                    col = ((z * 3 + a) * 2 + ri) * LANES
                    value = dirac[a, t, z, ri]
                    for w in range(16):
                        high, low = turn_split(value * weights[t * depth + z, w : w + 1, :])
                        right_hi[w * vectors : (w + 1) * vectors, col : col + LANES] = high
                        right_lo[w * vectors : (w + 1) * vectors, col : col + LANES] = low
        lh, ll = left_hi[t], left_lo[t]
        rh, rl = right_hi[...], right_lo[...]
        total = lax.dot_general(lh, rh, NT_DIMS, preferred_element_type=F32)
        total = total + lax.dot_general(ll, rh, NT_DIMS, preferred_element_type=F32)
        total = total + lax.dot_general(lh, rl, NT_DIMS, preferred_element_type=F32)
        half = 8 * vectors
        for slot, piece in enumerate(pieces):
            plain = total[slot * rows : slot * rows + vectors]
            turned = total[slot * rows + vectors : (slot + 1) * rows]
            piece[t, 0] = plain[:, :half] + turned[:, half:]
            piece[t, 1] = turned[:, :half] - plain[:, half:]


def spread_kernel(dirac16, out, wide):
    rows, vectors = dirac16.shape[0], dirac16.shape[1]
    for r in range(rows):
        wide[pl.ds(r, vectors, stride=rows), :] = dirac16[r].astype(F32)
    out[...] = wide[...].astype(BF16)


def final_kernel(kept, arrived, other, out):
    times = kept.shape[0]
    for t in range(times):
        for ri in range(2):
            total = kept[t, ri] + arrived[t, ri] + other[t, ri]
            for p in range(out.shape[0]):
                width = out.shape[4]
                out[p, t, ri] = total[:, p * width : (p + 1) * width]


def exchange(value, axis):
    size = lax.axis_size(axis)
    up = [(i, (i + 1) % size) for i in range(size)]
    down = [(j, i) for i, j in up]
    before = lax.ppermute(value, axis, up)
    if size == 2:
        return before, before
    return before, lax.ppermute(value, axis, down)


def on_device(eigen_store, fat_links, long_links, chosen, momenta, current_dirs, taste_masks):
    stored, _, _, times, depth, _ = eigen_store.shape
    vectors = chosen.shape[0]
    per_vector = 6 * times * depth
    n_ta, n_gz, n_gy = (lax.axis_size(a) for a in ("ta", "gz", "gy"))
    total_y = (LANES // HALF) * n_gy
    total_z = depth * n_gz

    store = eigen_store.transpose(0, 1, 3, 4, 2, 5).reshape(stored * per_vector, LANES)
    fat = fat_links.transpose(0, 1, 2, 3, 5, 6, 4, 7).reshape(-1, LANES)
    long = long_links.transpose(0, 1, 2, 3, 5, 6, 4, 7).reshape(-1, LANES)
    link_rows = fat.shape[0]
    link_scratch = [pltpu.VMEM((link_rows, LANES), F32)] * 2
    shape6 = (3, times, depth, 2, vectors, LANES)
    field_f32 = jax.ShapeDtypeStruct(shape6, F32)

    (packed,) = call(
        gather_kernel,
        [jax.ShapeDtypeStruct((per_vector * vectors, LANES), BF16)],
        [SM, VM],
        [
            pltpu.VMEM((stored * per_vector, LANES), F32),
            pltpu.VMEM((per_vector * vectors, LANES), F32),
        ],
        10000,
        500000,
    )(chosen, store)
    near = [(i, i ^ 1) for i in range(n_ta)]
    far = [((i + 1) % n_ta, ((i ^ 1) + 1) % n_ta) for i in range(n_ta)]
    afield = lax.ppermute(packed, "ta", near)
    bfield = lax.ppermute(packed, "ta", far)
    zprev, znext = exchange(packed, "gz")
    yfield, _ = exchange(packed, "gy")
    field, afield, bfield, zprev, znext, yfield = (
        f.reshape(shape6) for f in (packed, afield, bfield, zprev, znext, yfield)
    )

    dacc, back_x = call(
        functools.partial(local_kernel, times, depth),
        [field_f32, field_f32],
        [VM] * 3,
        link_scratch + [pltpu.VMEM((2, LANES, 4 * LANES), BF16)],
        20000000,
        3000000,
    )(field, fat, long)

    slots = current_dirs.shape[0]
    momentum_count = momenta.shape[0]
    width = depth * 6 * LANES
    left_rows = slots * 2 * vectors
    left = jax.ShapeDtypeStruct((times, left_rows, width), BF16)
    rotate = n_gz == 2 and n_gy == 2
    scale = 1.0 / math.sqrt(NX * total_y * total_z / 2)
    dacc, left_hi, left_lo, weights = call(
        functools.partial(side_kernel, times, depth, (total_y, total_z, scale), rotate),
        [
            field_f32,
            left,
            left,
            jax.ShapeDtypeStruct((times * depth, 2 * momentum_count, LANES), F32),
        ],
        [SM] * 3 + [VM] * 8,
        link_scratch
        + [
            pltpu.VMEM((2 * LANES, 4 * LANES), BF16),
            pltpu.VMEM((3,) + shape6, F32),
        ],
        20000000,
        6000000,
    )(
        momenta.T, current_dirs, taste_masks,
        field, yfield, zprev, znext, fat, long, dacc, back_x,
    )

    piece = jax.ShapeDtypeStruct((times, 2, vectors, momentum_count * vectors), F32)
    dirac16, *pieces = call(
        functools.partial(last_kernel, times, depth),
        [jax.ShapeDtypeStruct(shape6, BF16)] + [piece] * slots,
        [VM] * 6 + [HB] * 2,
        link_scratch
        + [
            pltpu.VMEM(shape6, F32),
            pltpu.VMEM((times, left_rows, width), BF16),
            pltpu.VMEM((times, left_rows, width), BF16),
            pltpu.VMEM((2 * momentum_count * vectors, width), BF16),
            pltpu.VMEM((2 * momentum_count * vectors, width), BF16),
            pltpu.SemaphoreType.DMA((2,)),
        ],
        400000000,
        6000000,
    )(dacc, afield, bfield, fat, long, weights, left_hi, left_lo)

    (odd_rows,) = call(
        spread_kernel,
        [jax.ShapeDtypeStruct((vectors * per_vector, LANES), BF16)],
        [VM],
        [pltpu.VMEM((vectors * per_vector, LANES), F32)],
        10000,
        500000,
    )(dirac16.reshape(per_vector, vectors, LANES))
    odd_vectors = odd_rows.reshape(vectors, 3, times, depth, 2, LANES).transpose(0, 1, 4, 2, 3, 5)

    if rotate:
        swap = [(0, 1), (1, 0)]
        got = lax.ppermute(jnp.stack([pieces[1], pieces[3]]), "gy", swap)
        other = lax.ppermute(pieces[2] + got[1], "gz", swap)
        (meson_fields,) = call(
            final_kernel,
            [jax.ShapeDtypeStruct((momentum_count, times, 2, vectors, vectors), F32)],
            [VM] * 3,
            [],
            100000,
            600000,
        )(pieces[0], got[0], other)
    else:
        whole = jnp.stack(pieces).reshape(slots, times, 2, vectors, momentum_count, vectors)
        whole = whole.transpose(0, 4, 1, 2, 3, 5).reshape(
            slots * momentum_count, times, 2, vectors, vectors
        )
        meson_fields = lax.psum_scatter(whole, ("gz", "gy"), scatter_dimension=0, tiled=True)
    return odd_vectors, meson_fields


def solution(mesh):
    in_specs = (
        P(None, None, None, ("cfg", "ta"), "gz", "gy"),
        P(None, None, None, None, None, ("cfg", "ta"), "gz", "gy"),
        P(None, None, None, None, None, ("cfg", "ta"), "gz", "gy"),
        P("cfg"),
        P(),
        P(),
        P(),
    )
    out_specs = (
        P(None, None, None, ("cfg", "ta"), "gz", "gy"),
        P(("gz", "gy"), ("cfg", "ta"), None, None, None),
    )
    return jax.shard_map(
        on_device, mesh=mesh, in_specs=in_specs, out_specs=out_specs, check_vma=False
    )
```

profile of v0, /device:TPU:0, one launch (start us, length us, event | category | flops | bytes accessed | tf_op | source)
XLA Modules:
  0.0 32.5 jit_solution(222423280794078026)
XLA Ops:
  0.6 0.0 copy-start.4
  0.6 0.9 %copy-done.4 = bf16[20,3,2,3,3,128]{5,2,4,3,1,0:T(2,128)(2,1)S(1)} copy-done((bf16[20,3,2,3,3,128]{5,2,4,3,1,0:T(2,128)(2,1)S(1)}, bf16[20,3,2,3,3,128]{5,2,4,3,1,0:T(2,128)(2,1)}, u32[]{:S(2)}) %copy-start.4) | copy-done | bytes 276504
  1.6 0.0 copy-start.6
  1.6 0.7 %copy-done.6 = s32[16]{0:T(128)S(1)} copy-done((s32[16]{0:T(128)S(1)}, s32[16]{0:T(128)}, u32[]{:S(2)}) %copy-start.6) | copy-done | bytes 88
  2.2 0.0 copy-start.1
  2.2 0.8 %shard_map.86 = bf16[864,128]{1,0:T(8,128)(2,1)S(1)} custom-call(s32[16]{0:T(128)S(1)} %copy-done.6, bf16[1080,128]{1,0:T(8,128)(2,1)S(1)} %bitcast.37), custom_call_target="tpu_custom_call" | custom-call | flops 10000 | bytes 500000 | tf_op jit(solution)/shard_map/pallas_call | solution.py:403
  3.1 0.5 %collective-permute-start = (bf16[864,128]{1,0:T(8,128)(2,1)S(1)}, bf16[864,128]{1,0:T(8,128)(2,1)S(1)}, u32[]{:S(2)}, u32[]{:S(2)}) collective-permute-start(bf16[864,128]{1,0:T(8,128)(2,1)S(1)} %shard_map.86), channel_id=1, source_target_pairs={{0,1},{1,0},{2,3},{3,2},{4,5},{5,4},{6,7},{7,6},{8,9},{9,8},{10,11... | collective-permute-start | bytes 663560 | tf_op jit(solution)/shard_map/ppermute | solution.py:381
  3.6 2.6 %collective-permute-start.1 = (bf16[864,128]{1,0:T(8,128)(2,1)S(1)}, bf16[864,128]{1,0:T(8,128)(2,1)S(1)}, u32[]{:S(2)}, u32[]{:S(2)}) collective-permute-start(bf16[864,128]{1,0:T(8,128)(2,1)S(1)} %shard_map.86), channel_id=1, source_target_pairs={{0,2},{2,0},{1,3},{3,1},{4,6},{6,4},{5,7},{7,5},{8,10},{10,8},{9,1... | collective-permute-start | bytes 663560 | tf_op jit(solution)/shard_map/ppermute | solution.py:381
  6.1 1.6 %collective-permute-start.2 = (bf16[864,128]{1,0:T(8,128)(2,1)S(1)}, bf16[864,128]{1,0:T(8,128)(2,1)S(1)}, u32[]{:S(2)}, u32[]{:S(2)}) collective-permute-start(bf16[864,128]{1,0:T(8,128)(2,1)S(1)} %shard_map.86), channel_id=1, source_target_pairs={{0,4},{4,0},{8,12},{12,8},{1,5},{5,1},{9,13},{13,9},{2,6},{6,2},{1... | collective-permute-start | bytes 663560 | tf_op jit(solution)/shard_map/ppermute | solution.py:416
  7.7 2.5 %collective-permute-start.3 = (bf16[864,128]{1,0:T(8,128)(2,1)S(1)}, bf16[864,128]{1,0:T(8,128)(2,1)S(1)}, u32[]{:S(2)}, u32[]{:S(2)}) collective-permute-start(bf16[864,128]{1,0:T(8,128)(2,1)S(1)} %shard_map.86), channel_id=1, source_target_pairs={{4,8},{8,4},{12,0},{0,12},{5,9},{9,5},{13,1},{1,13},{6,10},{10,6},... | collective-permute-start | bytes 663560 | tf_op jit(solution)/shard_map/ppermute | solution.py:417
  10.2 0.0 copy-start
  10.2 1.0 %copy-done = bf16[2,4,3,3,2,3,3,128]{7,4,6,5,3,2,1,0:T(2,128)(2,1)S(1)} copy-done((bf16[2,4,3,3,2,3,3,128]{7,4,6,5,3,2,1,0:T(2,128)(2,1)S(1)}, bf16[2,4,3,3,2,3,3,128]{7,4,6,5,3,2,1,0:T(2,128)(2,1)}, u32[]{:S(2)}) %copy-start) | copy-done | bytes 331800
  11.2 0.0 copy-start.2
  11.2 1.0 %copy-done.2 = bf16[2,4,3,3,2,3,3,128]{7,4,6,5,3,2,1,0:T(2,128)(2,1)S(1)} copy-done((bf16[2,4,3,3,2,3,3,128]{7,4,6,5,3,2,1,0:T(2,128)(2,1)S(1)}, bf16[2,4,3,3,2,3,3,128]{7,4,6,5,3,2,1,0:T(2,128)(2,1)}, u32[]{:S(2)}) %copy-start.2) | copy-done | bytes 331800
  12.1 0.0 copy-start.3
  12.1 1.5 %shard_map.87 = (f32[3,3,3,2,16,128]{5,4,3,2,1,0:T(8,128)S(1)}, f32[3,3,3,2,16,128]{5,4,3,2,1,0:T(8,128)S(1)}) custom-call(bf16[3,3,3,2,16,128]{5,4,3,2,1,0:T(8,128)(2,1)S(1)} %bitcast.33, bf16[1296,128]{1,0:T(8,128)(2,1)S(1)} %bitcast.27, bf16[1296,128]{1,0:T(8,128)(2,1)S(1)} %bitcast.30), custom_call_target="tpu_custom_call" | custom-call | flops 20000000 | bytes 3000000 | tf_op jit(solution)/shard_map/pallas_call | solution.py:424
  13.7 0.0 collective-permute-done
  13.7 0.0 collective-permute-done.1
  13.7 0.0 copy-start.5
  13.7 0.7 %copy-done.5 = s32[8,3]{0,1:T(4,128)S(1)} copy-done((s32[8,3]{0,1:T(4,128)S(1)}, s32[8,3]{0,1:T(4,128)}, u32[]{:S(2)}) %copy-start.5) | copy-done | bytes 120
  14.4 0.0 copy-start.7
  14.4 0.7 %copy-done.7 = s32[4]{0:T(128)S(1)} copy-done((s32[4]{0:T(128)S(1)}, s32[4]{0:T(128)}, u32[]{:S(2)}) %copy-start.7) | copy-done | bytes 40
  15.0 0.0 copy-start.8
  15.0 0.7 %copy-done.8 = s32[4]{0:T(128)S(1)} copy-done((s32[4]{0:T(128)S(1)}, s32[4]{0:T(128)}, u32[]{:S(2)}) %copy-start.8) | copy-done | bytes 40
  15.7 3.0 %shard_map.88 = (f32[3,3,3,2,16,128]{5,4,3,2,1,0:T(8,128)S(1)}, bf16[3,128,2304]{2,1,0:T(8,128)(2,1)S(1)}, bf16[3,128,2304]{2,1,0:T(8,128)(2,1)S(1)}, f32[9,16,128]{2,1,0:T(8,128)S(1)}) custom-call(s32[3,8]{1,0:T(4,128)S(1)} %bitcast.44, s32[4]{0:T(128)S(1)} %copy-done.7, s32[4]{0:T(128)S(1)} %copy-done.8, bf16[3,3,3,2,16,128]{5,4,3,2,1,0:T(8,128)(2,1)S(1)} %bitcast.34, ...), custom_call_target="tpu_custom_call" | custom-call | flops 20000000 | bytes 6000000 | tf_op jit(solution)/shard_map/pallas_call | solution.py:440
  18.7 0.0 collective-permute-done.2
  18.7 1.8 %collective-permute-done.3 = bf16[864,128]{1,0:T(8,128)(2,1)S(1)} collective-permute-done((bf16[864,128]{1,0:T(8,128)(2,1)S(1)}, bf16[864,128]{1,0:T(8,128)(2,1)S(1)}, u32[]{:S(2)}, u32[]{:S(2)}) %collective-permute-start.3) | collective-permute-done | bytes 221216 | tf_op jit(solution)/shard_map/ppermute | solution.py:417
  20.5 0.0 copy-done.1
  20.5 0.0 copy-done.3
  20.5 5.5 %shard_map.89 = (bf16[3,3,3,2,16,128]{5,4,3,2,1,0:T(8,128)(2,1)S(1)}, f32[3,2,16,128]{3,2,1,0:T(8,128)S(1)}, f32[3,2,16,128]{3,2,1,0:T(8,128)S(1)}, f32[3,2,16,128]{3,2,1,0:T(8,128)S(1)}, f32[3,2,16,128]{3,2,1,0:T(8,128)S(1)}) custom-call(f32[3,3,3,2,16,128]{5,4,3,2,1,0:T(8,128)S(1)} %get-tuple-element.15.dacc, bf16[3,3,3,2,16,128]{5,4,3,2,1,0:T(8,128)(2,1)S(1)} %bitcast.40, ...), custom_call_target="tpu_custom_call" | custom-call | flops 400000000 | bytes 6000000 | tf_op jit(solution)/shard_map/pallas_call | solution.py:462
  26.0 0.1 collective-permute-start.4
  26.1 0.7 %shard_map.90 = bf16[864,128]{1,0:T(8,128)(2,1)} custom-call(bf16[54,16,128]{2,1,0:T(8,128)(2,1)S(1)} %bitcast.39), custom_call_target="tpu_custom_call" | custom-call | flops 10000 | bytes 500000 | tf_op jit(solution)/shard_map/pallas_call | solution.py:479
  26.8 0.5 %collective-permute-done.4 = f32[2,3,2,16,128]{4,3,2,1,0:T(8,128)S(1)} collective-permute-done((f32[2,3,2,16,128]{4,3,2,1,0:T(8,128)S(1)}, f32[2,3,2,16,128]{4,3,2,1,0:T(8,128)S(1)}, u32[]{:S(2)}, u32[]{:S(2)}) %collective-permute-start.4) | collective-permute-done | bytes 98336 | tf_op jit(solution)/shard_map/ppermute | solution.py:491
  27.4 0.6 %collective-permute-start.5 = (f32[3,2,16,128]{3,2,1,0:T(8,128)S(1)}, f32[3,2,16,128]{3,2,1,0:T(8,128)S(1)}, u32[]{:S(2)}, u32[]{:S(2)}) collective-permute-start(f32[3,2,16,128]{3,2,1,0:T(8,128)S(1)} %fusion), channel_id=1, source_target_pairs={{0,2},{2,0},{1,3},{3,1},{4,6},{6,4},{5,7},{7,5},{8,10},{10,8},{9,1... | collective-permute-start | bytes 147464 | tf_op jit(solution)/shard_map/ppermute | solution.py:492
  28.0 3.5 %collective-permute-done.5.other = f32[3,2,16,128]{3,2,1,0:T(8,128)S(1)} collective-permute-done((f32[3,2,16,128]{3,2,1,0:T(8,128)S(1)}, f32[3,2,16,128]{3,2,1,0:T(8,128)S(1)}, u32[]{:S(2)}, u32[]{:S(2)}) %collective-permute-start.5) | collective-permute-done | bytes 49184 | tf_op jit(solution)/shard_map/ppermute | solution.py:492
  31.6 0.9 %shard_map.91 = f32[8,3,2,16,16]{4,3,2,1,0:T(8,128)} custom-call(f32[3,2,16,128]{3,2,1,0:T(8,128)S(1)} %get-tuple-element.20.kept, f32[3,2,16,128]{3,2,1,0:T(8,128)S(1)} %slice_bitcast_fusion.1.arrived, f32[3,2,16,128]{3,2,1,0:T(8,128)S(1)} %collective-permute-done.5.other), custom_call_target="tpu_custom_call" | custom-call | flops 100000 | bytes 600000 | tf_op jit(solution)/shard_map/pallas_call | solution.py:493
  (3 shorter events, 0.0 us)
Async XLA Ops:
  0.6 1.0 %copy-start.4 = (bf16[20,3,2,3,3,128]{5,2,4,3,1,0:T(2,128)(2,1)S(1)}, bf16[20,3,2,3,3,128]{5,2,4,3,1,0:T(2,128)(2,1)}, u32[]{:S(2)}) copy-start(bf16[20,3,2,3,3,128]{5,2,4,3,1,0:T(2,128)(2,1)} %param.7) | copy-start | bytes 829444
  1.6 0.7 %copy-start.6 = (s32[16]{0:T(128)S(1)}, s32[16]{0:T(128)}, u32[]{:S(2)}) copy-start(s32[16]{0:T(128)} %chosen.1) | copy-start | bytes 196
  2.2 18.3 %copy-start.1 = (bf16[2,4,3,3,2,3,3,128]{7,4,6,5,3,2,1,0:T(2,128)(2,1)S(1)}, bf16[2,4,3,3,2,3,3,128]{7,4,6,5,3,2,1,0:T(2,128)(2,1)}, u32[]{:S(2)}) copy-start(bf16[2,4,3,3,2,3,3,128]{7,4,6,5,3,2,1,0:T(2,128)(2,1)} %param.8) | copy-start | bytes 995332
  3.1 10.6 %collective-permute-start = (bf16[864,128]{1,0:T(8,128)(2,1)S(1)}, bf16[864,128]{1,0:T(8,128)(2,1)S(1)}, u32[]{:S(2)}, u32[]{:S(2)}) collective-permute-start(bf16[864,128]{1,0:T(8,128)(2,1)S(1)} %shard_map.86), channel_id=1, source_target_pairs={{0,1},{1,0},{2,3},{3,2},{4,5},{5,4},{6,7},{7,6},{8,9},{9,8},{10,11... | collective-permute-start | bytes 663560 | tf_op jit(solution)/shard_map/ppermute | solution.py:381
  3.6 10.1 %collective-permute-start.1 = (bf16[864,128]{1,0:T(8,128)(2,1)S(1)}, bf16[864,128]{1,0:T(8,128)(2,1)S(1)}, u32[]{:S(2)}, u32[]{:S(2)}) collective-permute-start(bf16[864,128]{1,0:T(8,128)(2,1)S(1)} %shard_map.86), channel_id=1, source_target_pairs={{0,2},{2,0},{1,3},{3,1},{4,6},{6,4},{5,7},{7,5},{8,10},{10,8},{9,1... | collective-permute-start | bytes 663560 | tf_op jit(solution)/shard_map/ppermute | solution.py:381
  6.1 12.6 %collective-permute-start.2 = (bf16[864,128]{1,0:T(8,128)(2,1)S(1)}, bf16[864,128]{1,0:T(8,128)(2,1)S(1)}, u32[]{:S(2)}, u32[]{:S(2)}) collective-permute-start(bf16[864,128]{1,0:T(8,128)(2,1)S(1)} %shard_map.86), channel_id=1, source_target_pairs={{0,4},{4,0},{8,12},{12,8},{1,5},{5,1},{9,13},{13,9},{2,6},{6,2},{1... | collective-permute-start | bytes 663560 | tf_op jit(solution)/shard_map/ppermute | solution.py:416
  7.7 12.8 %collective-permute-start.3 = (bf16[864,128]{1,0:T(8,128)(2,1)S(1)}, bf16[864,128]{1,0:T(8,128)(2,1)S(1)}, u32[]{:S(2)}, u32[]{:S(2)}) collective-permute-start(bf16[864,128]{1,0:T(8,128)(2,1)S(1)} %shard_map.86), channel_id=1, source_target_pairs={{4,8},{8,4},{12,0},{0,12},{5,9},{9,5},{13,1},{1,13},{6,10},{10,6},... | collective-permute-start | bytes 663560 | tf_op jit(solution)/shard_map/ppermute | solution.py:417
  10.2 1.0 %copy-start = (bf16[2,4,3,3,2,3,3,128]{7,4,6,5,3,2,1,0:T(2,128)(2,1)S(1)}, bf16[2,4,3,3,2,3,3,128]{7,4,6,5,3,2,1,0:T(2,128)(2,1)}, u32[]{:S(2)}) copy-start(bf16[2,4,3,3,2,3,3,128]{7,4,6,5,3,2,1,0:T(2,128)(2,1)} %param.8) | copy-start | bytes 995332
  11.2 1.0 %copy-start.2 = (bf16[2,4,3,3,2,3,3,128]{7,4,6,5,3,2,1,0:T(2,128)(2,1)S(1)}, bf16[2,4,3,3,2,3,3,128]{7,4,6,5,3,2,1,0:T(2,128)(2,1)}, u32[]{:S(2)}) copy-start(bf16[2,4,3,3,2,3,3,128]{7,4,6,5,3,2,1,0:T(2,128)(2,1)} %param.9) | copy-start | bytes 995332
  12.1 8.4 %copy-start.3 = (bf16[2,4,3,3,2,3,3,128]{7,4,6,5,3,2,1,0:T(2,128)(2,1)S(1)}, bf16[2,4,3,3,2,3,3,128]{7,4,6,5,3,2,1,0:T(2,128)(2,1)}, u32[]{:S(2)}) copy-start(bf16[2,4,3,3,2,3,3,128]{7,4,6,5,3,2,1,0:T(2,128)(2,1)} %param.9) | copy-start | bytes 995332
  13.7 0.7 %copy-start.5 = (s32[8,3]{0,1:T(4,128)S(1)}, s32[8,3]{0,1:T(4,128)}, u32[]{:S(2)}) copy-start(s32[8,3]{0,1:T(4,128)} %param.11) | copy-start | bytes 292
  14.4 0.7 %copy-start.7 = (s32[4]{0:T(128)S(1)}, s32[4]{0:T(128)}, u32[]{:S(2)}) copy-start(s32[4]{0:T(128)} %dirs.1) | copy-start | bytes 52
  15.0 0.7 %copy-start.8 = (s32[4]{0:T(128)S(1)}, s32[4]{0:T(128)}, u32[]{:S(2)}) copy-start(s32[4]{0:T(128)} %masks.1) | copy-start | bytes 52
  26.0 1.4 %collective-permute-start.4 = (f32[2,3,2,16,128]{4,3,2,1,0:T(8,128)S(1)}, f32[2,3,2,16,128]{4,3,2,1,0:T(8,128)S(1)}, u32[]{:S(2)}, u32[]{:S(2)}) collective-permute-start(f32[2,3,2,16,128]{4,3,2,1,0:T(8,128)S(1)} %pad_maximum_fusion), channel_id=1, source_target_pairs={{0,1},{1,0},{2,3},{3,2},{4,5},{5,4},{6,7},{7,6},{8,9},{9,8},{10,11... | collective-permute-start | bytes 294920 | tf_op jit(solution)/shard_map/ppermute | solution.py:491
  27.4 4.2 %collective-permute-start.5 = (f32[3,2,16,128]{3,2,1,0:T(8,128)S(1)}, f32[3,2,16,128]{3,2,1,0:T(8,128)S(1)}, u32[]{:S(2)}, u32[]{:S(2)}) collective-permute-start(f32[3,2,16,128]{3,2,1,0:T(8,128)S(1)} %fusion), channel_id=1, source_target_pairs={{0,2},{2,0},{1,3},{3,1},{4,6},{6,4},{5,7},{7,5},{8,10},{10,8},{9,1... | collective-permute-start | bytes 147464 | tf_op jit(solution)/shard_map/ppermute | solution.py:492
where the time goes:
time: 32.7 us; the launch traced here: 32.5 us
  Pallas kernels  12.4 us (38%)
  starting transfers between devices  7.81 us (24%)
  waiting for transfers between devices  5.91 us (18%)
  local copies, waits for them, and re-layouts  5.55 us (17%)
  between operations  0.73 us (2%)
    unnamed x18, local copies, waits for them, and re-layouts  5.54 us
    pallas_call x1, Pallas kernels, on_device(): call(functools.partial(last_kernel, times, depth), [jax.ShapeDtypeStruct(...  5.48 us
    ppermute x1, waiting for transfers between devices, on_device(): other = lax.ppermute(pieces[2] + got[1], 'gz', swap)  3.55 us
    ppermute x2, starting transfers between devices, exchange(): before = lax.ppermute(value, axis, up)  3.08 us
    pallas_call x1, Pallas kernels, on_device(): call(functools.partial(side_kernel, times, depth, (total_y, total_z, scal...  2.99 us
    ppermute x1, starting transfers between devices, on_device(): bfield = lax.ppermute(packed, 'ta', far)  2.47 us
    ppermute x1, waiting for transfers between devices, on_device(): bfield = lax.ppermute(packed, 'ta', far)  1.8 us
    ppermute x1, starting transfers between devices, on_device(): afield = lax.ppermute(packed, 'ta', near)  1.58 us
  transfers between devices with their start and end apart: 6, of which 3 were waited for; matrix products, arithmetic and copies ran while one was open for 0% of the time, Pallas kernels for 16%

commit v1 on v0

v1 whole, which is shorter than its diff:
```python
import functools
import math

import jax
import jax.numpy as jnp
from jax import lax
from jax.experimental import pallas as pl
from jax.experimental.pallas import tpu as pltpu
from jax.sharding import PartitionSpec as P

NX = 64
HALF = NX // 2
LANES = 128
F32 = jnp.float32
BF16 = jnp.bfloat16
VM = pl.BlockSpec(memory_space=pltpu.VMEM)
SM = pl.BlockSpec(memory_space=pltpu.SMEM)
HB = pl.BlockSpec(memory_space=pltpu.HBM)


def call(body, outs, ins, scratch, cost):
    return pl.pallas_call(
        body,
        out_shape=outs,
        in_specs=ins,
        out_specs=[VM] * len(outs),
        scratch_shapes=scratch,
        compiler_params=pltpu.CompilerParams(vmem_limit_bytes=40 * 1024 * 1024),
        cost_estimate=pl.CostEstimate(flops=cost, bytes_accessed=cost, transcendentals=0),
    )


def gather_kernel(
    vectors, chosen_hbm, store_hbm, fat_hbm, long_hbm,
    far, side, out, fat, long,
    chosen, store, wide, turned, sems,
):
    first = [
        pltpu.make_async_copy(chosen_hbm, chosen, sems.at[0]),
        pltpu.make_async_copy(store_hbm, store, sems.at[1]),
    ]
    later = [
        pltpu.make_async_copy(fat_hbm, fat, sems.at[2]),
        pltpu.make_async_copy(long_hbm, long, sems.at[3]),
    ]
    for copy in first + later:
        copy.start()
    for copy in first:
        copy.wait()
    size = out.shape[0]
    rows = size // vectors
    wide[...] = store[...].astype(F32)
    full = rows // 8
    rest = rows - 8 * full
    for n in range(vectors):
        start = chosen[n] * rows
        for q in range(full):
            turned[pl.ds(q * 8 * vectors + n, 8, stride=vectors), :] = wide[
                pl.ds(start + 8 * q, 8), :
            ]
        if rest:
            turned[pl.ds(full * 8 * vectors + n, rest, stride=vectors), :] = wide[
                pl.ds(start + 8 * full, rest), :
            ]
    for r in range(0, size, 16):
        block = turned[r : r + 16, :].astype(BF16)
        out[r : r + 16, :] = block
        far[r : r + 16, :] = block
        side[r : r + 16, :] = block
    for ref in (far, side):
        ref[size:, :] = jnp.zeros((ref.shape[0] - size, LANES), BF16)
    for copy in later:
        copy.wait()


class Links:
    def __init__(self, ref, times, depth):
        self.ref, self.times, self.depth = ref, times, depth

    def row(self, w, mu, a, b, t, z, ri):
        at = (((((w * 4 + mu) * 3 + a) * 3 + b) * self.times + t) * self.depth + z) * 2 + ri
        return self.ref[at : at + 1, :]


def add_hop(acc, links, w, mu, t, z, vec, minus):
    for a in range(3):
        for b in range(3):
            lr = links.row(w, mu, a, b, t, z, 0)
            li = links.row(w, mu, a, b, t, z, 1)
            vr, vi = vec[b]
            if minus:
                acc[a][0] = (acc[a][0] - lr * vr) + li * vi
                acc[a][1] = (acc[a][1] - lr * vi) - li * vr
            else:
                acc[a][0] = (acc[a][0] + lr * vr) - li * vi
                acc[a][1] = (acc[a][1] + lr * vi) + li * vr


class Field:
    def __init__(self, ref, times, depth, vectors):
        self.ref, self.times, self.depth, self.vectors = ref, times, depth, vectors

    def raw(self, t, z):
        out = []
        for a in range(3):
            pair = []
            for ri in range(2):
                at = (((a * self.times + t) * self.depth + z) * 2 + ri) * self.vectors
                pair.append(self.ref[at : at + self.vectors, :])
            out.append(pair)
        return out

    def read(self, t, z):
        return widen(self.raw(t, z))

    def stacked(self, t, z):
        return jnp.concatenate([v for pair in self.raw(t, z) for v in pair], axis=0)


def widen(parts):
    return [[v.astype(F32) for v in pair] for pair in parts]


def zeros(vectors):
    return [[jnp.zeros((vectors, LANES), F32) for _ in range(2)] for _ in range(3)]


def read(ref, t, z):
    return [[ref[a, t, z, ri] for ri in range(2)] for a in range(3)]


def write(ref, t, z, acc):
    for a in range(3):
        for ri in range(2):
            ref[a, t, z, ri] = acc[a][ri].astype(ref.dtype)


def subtract(acc, other):
    for a in range(3):
        for ri in range(2):
            acc[a][ri] = acc[a][ri] - other[a][ri]


def split_hops(product, vectors, count):
    out = []
    for h in range(count):
        cols = product[:, h * LANES : (h + 1) * LANES]
        out.append(
            [
                [cols[(a * 2 + ri) * vectors : (a * 2 + ri + 1) * vectors] for ri in range(2)]
                for a in range(3)
            ]
        )
    return out


def x_permutation(e):
    src = lax.broadcasted_iota(jnp.int32, (LANES, 4 * LANES), 0)
    col = lax.broadcasted_iota(jnp.int32, (LANES, 4 * LANES), 1)
    h = col // LANES
    dst = col % LANES
    y = dst // HALF
    k = dst % HALF
    s = (e + y) % 2
    lead = jnp.where(h == 0, 1, jnp.where(h == 1, 0, jnp.where(h == 2, 2, -1)))
    want = y * HALF + (k + lead - s + HALF) % HALF
    return jnp.where(src == want, 1.0, 0.0).astype(BF16)


def y_permutation():
    rows = LANES // HALF
    src = lax.broadcasted_iota(jnp.int32, (2 * LANES, 4 * LANES), 0)
    col = lax.broadcasted_iota(jnp.int32, (2 * LANES, 4 * LANES), 1)
    h = col // LANES
    dst = col % LANES
    y = dst // HALF
    k = dst % HALF
    d = jnp.where(h == 0, 1, jnp.where(h == 1, -1, jnp.where(h == 2, 3, -3)))
    want = ((y + d + 2 * rows) % (2 * rows)) * HALF + k
    return jnp.where(src == want, 1.0, 0.0).astype(BF16)


def local_kernel(
    times, depth, vectors, sizes,
    momenta_hbm, field_ref, y_ref, fat, long,
    dacc, back_xy, weights, fatf, longf,
    momenta, x_perm, y_perm, sem,
):
    total_y, total_z, scale = sizes
    copy = pltpu.make_async_copy(momenta_hbm, momenta, sem)
    copy.start()
    fatf[...] = fat[...].astype(F32)
    longf[...] = long[...].astype(F32)
    fat_l, long_l = Links(fatf, times, depth), Links(longf, times, depth)
    field = Field(field_ref, times, depth, vectors)
    y_field = Field(y_ref, times, depth, vectors)
    origin = lax.axis_index("ta") * times + lax.axis_index("gz") * depth
    for e in range(2):
        x_perm[e] = x_permutation(origin + e)
    y_perm[...] = y_permutation()
    for t in range(times):
        for z in range(depth):
            here = field.stacked(t, z)
            moved = jnp.dot(here, x_perm[(t + z) % 2], preferred_element_type=F32)
            plus1, minus1, plus3, minus3 = split_hops(moved, vectors, 4)
            back = zeros(vectors)
            add_hop(back, fat_l, 1, 3, t, z, minus1, False)
            write(back_xy.at[1], t, z, back)
            acc = [[-v for v in pair] for pair in back]
            add_hop(acc, fat_l, 0, 3, t, z, plus1, False)
            add_hop(acc, long_l, 0, 3, t, z, plus3, False)
            add_hop(acc, long_l, 1, 3, t, z, minus3, True)
            both = jnp.concatenate([here, y_field.stacked(t, z)], axis=1)
            moved = jnp.dot(both, y_perm[...], preferred_element_type=F32)
            plus1, minus1, plus3, minus3 = split_hops(moved, vectors, 4)
            back = zeros(vectors)
            add_hop(back, fat_l, 1, 2, t, z, minus1, False)
            write(back_xy.at[0], t, z, back)
            subtract(acc, back)
            add_hop(acc, fat_l, 0, 2, t, z, plus1, False)
            add_hop(acc, long_l, 0, 2, t, z, plus3, False)
            add_hop(acc, long_l, 1, 2, t, z, minus3, True)
            if t + 1 < times:
                add_hop(acc, fat_l, 0, 0, t, z, field.read(t + 1, z), False)
            if t >= 1:
                add_hop(acc, fat_l, 1, 0, t, z, field.read(t - 1, z), True)
            if z + 1 < depth:
                add_hop(acc, fat_l, 0, 1, t, z, field.read(t, z + 1), False)
            write(dacc, t, z, acc)
    copy.wait()
    count = momenta.shape[1]
    lane = lax.broadcasted_iota(jnp.int32, (count, LANES), 1)
    sub = lax.broadcasted_iota(jnp.int32, (count, LANES), 0)
    y_glob = lax.axis_index("gy") * (LANES // HALF) + lane // HALF
    q = [jnp.zeros((count, LANES), F32) for _ in range(3)]
    for p in range(count):
        for axis in range(3):
            q[axis] = jnp.where(sub == p, momenta[axis, p].astype(F32), q[axis])
    for t in range(times):
        for z in range(depth):
            z_glob = lax.axis_index("gz") * depth + z
            x_glob = 2 * (lane % HALF) + 1 - (origin + t + z + y_glob) % 2
            turns = (
                q[0] * (x_glob.astype(F32) * (1.0 / NX))
                + q[1] * (y_glob.astype(F32) * (1.0 / total_y))
                + q[2] * (z_glob.astype(F32) * (1.0 / total_z))
            )
            cosine, sine = sincos_turns(turns)
            weights[t * depth + z, 0:count] = cosine * scale
            weights[t * depth + z, count : 2 * count] = sine * scale


def turn_split(value):
    high = value.astype(BF16)
    low = (value - high.astype(F32)).astype(BF16)
    return high, low


def sincos_turns(turns):
    quarters = 4.0 * (turns - jnp.floor(turns + 0.5))
    near = jnp.floor(quarters + 0.5)
    x = (quarters - near) * (0.5 * math.pi)
    x2 = x * x
    s = x * (1.0 + x2 * (-1.0 / 6 + x2 * (1.0 / 120 + x2 * (-1.0 / 5040 + x2 / 362880))))
    c = 1.0 + x2 * (-0.5 + x2 * (1.0 / 24 + x2 * (-1.0 / 720 + x2 * (1.0 / 40320))))
    which = near.astype(jnp.int32) & 3
    odd = (which & 1) == 1
    cosine = jnp.where(odd, s, c)
    sine = jnp.where(odd, c, s)
    cosine = jnp.where((which == 1) | (which == 2), -cosine, cosine)
    sine = jnp.where(which >= 2, -sine, sine)
    return cosine, sine


def side_kernel(
    times, depth, vectors, rotate,
    dirs_hbm, masks_hbm, field_ref, before_ref, after_ref, fatf, longf, dacc_in, back_xy,
    dacc, left,
    dirs, masks, back, sems,
):
    copies = [
        pltpu.make_async_copy(dirs_hbm, dirs, sems.at[0]),
        pltpu.make_async_copy(masks_hbm, masks, sems.at[1]),
    ]
    for copy in copies:
        copy.start()
    fat_l, long_l = Links(fatf, times, depth), Links(longf, times, depth)
    field = Field(field_ref, times, depth, vectors)
    before = Field(before_ref, times, depth, vectors)
    after = Field(after_ref, times, depth, vectors)
    for t in range(times):
        for z in range(depth):
            acc = read(dacc_in, t, z)
            back_z = zeros(vectors)
            source = field.read(t, z - 1) if z >= 1 else before.read(t, depth - 1)
            add_hop(back_z, fat_l, 1, 1, t, z, source, False)
            write(back.at[0], t, z, back_z)
            for d in range(2):
                write(back.at[1 + d], t, z, read(back_xy.at[d], t, z))
            subtract(acc, back_z)
            if z + 1 == depth:
                add_hop(acc, fat_l, 0, 1, t, z, after.read(t, 0), False)
            add_hop(acc, long_l, 0, 1, t, z, after.read(t, z), False)
            add_hop(acc, long_l, 1, 1, t, z, before.read(t, z), True)
            write(dacc, t, z, acc)
    for copy in copies:
        copy.wait()
    slots = dirs.shape[0]
    if rotate:
        gz, gy = lax.axis_index("gz"), lax.axis_index("gy")
        current_of = [((gz + d // 2) % 2) * 2 + (gy + d % 2) % 2 for d in range(slots)]
    else:
        current_of = list(range(slots))
    lane = lax.broadcasted_iota(jnp.int32, (1, LANES), 1)
    y_glob = lax.axis_index("gy") * (LANES // HALF) + lane // HALF
    origin = lax.axis_index("ta") * times + lax.axis_index("gz") * depth
    low_part = slots * 2 * vectors
    for slot in range(slots):
        direction = dirs[current_of[slot]] - 1
        mask = masks[current_of[slot]]
        for t in range(times):
            for z in range(depth):
                z_glob = lax.axis_index("gz") * depth + z
                x_glob = 2 * (lane % HALF) + 1 - (origin + t + z + y_glob) % 2
                exponent = (
                    (mask & 1) * x_glob + ((mask >> 1) & 1) * y_glob + ((mask >> 2) & 1) * z_glob
                )
                sign = (1 - 2 * (exponent & 1)).astype(F32)
                for a in range(3):
                    col = (z * 3 + a) * 2 * LANES
                    first = slice(col, col + LANES)
                    other = slice(col + LANES, col + 2 * LANES)
                    real = turn_split(back[direction, a, t, z, 0] * sign)
                    imag = turn_split(back[direction, a, t, z, 1] * sign)
                    for part in range(2):
                        top = part * low_part + slot * 2 * vectors
                        turned = top + vectors
                        left[t, top : top + vectors, first] = real[part]
                        left[t, top : top + vectors, other] = imag[part]
                        left[t, turned : turned + vectors, first] = -imag[part]
                        left[t, turned : turned + vectors, other] = real[part]


NT_DIMS = (((1,), (1,)), ((), ()))


def last_kernel(
    times, depth, vectors,
    far_ref, dacc, near_ref, fatf, longf, weights, left,
    dirac16, *pieces,
):
    fat_l, long_l = Links(fatf, times, depth), Links(longf, times, depth)
    near = Field(near_ref, times, depth, vectors)
    far = Field(far_ref, times, depth, vectors)
    even = lax.axis_index("ta") % 2 == 0

    def pick(first, second, t, z):
        return [
            [jnp.where(even, f, s) for f, s in zip(x, y)]
            for x, y in zip(first.raw(t, z), second.raw(t, z))
        ]

    rows = 2 * vectors
    left_rows = left.shape[1] // 2
    count = weights.shape[1]
    half = count * vectors // 2
    for t in range(times):
        main = jnp.zeros((2 * left_rows, count * vectors), F32)
        rest = jnp.zeros((left_rows, count * vectors), F32)
        for z in range(depth):
            acc = read(dacc, t, z)
            add_hop(acc, long_l, 0, 0, t, z, widen(pick(near, far, t, z)), False)
            add_hop(acc, long_l, 1, 0, t, z, widen(pick(far, near, t, z)), True)
            if t + 1 == times:
                add_hop(acc, fat_l, 0, 0, t, z, widen(pick(near, far, 0, z)), False)
            if t == 0:
                add_hop(acc, fat_l, 1, 0, t, z, widen(pick(far, near, times - 1, z)), True)
            write(dirac16, t, z, acc)
            for a in range(3):
                high, low = [], []
                for ri in range(2):
                    parts = [
                        turn_split(acc[a][ri] * weights[t * depth + z, w : w + 1, :])
                        for w in range(count)
                    ]
                    high.append(jnp.concatenate([h for h, _ in parts], axis=0))
                    low.append(jnp.concatenate([l for _, l in parts], axis=0))
                high = jnp.concatenate(high, axis=1)
                low = jnp.concatenate(low, axis=1)
                col = (z * 3 + a) * 2 * LANES
                lefts = left[t, :, col : col + 2 * LANES]
                main = main + lax.dot_general(lefts, high, NT_DIMS, preferred_element_type=F32)
                rest = rest + lax.dot_general(
                    lefts[:left_rows], low, NT_DIMS, preferred_element_type=F32
                )
        total = main[:left_rows] + main[left_rows:] + rest
        for slot, piece in enumerate(pieces):
            plain = total[slot * rows : slot * rows + vectors]
            turned = total[slot * rows + vectors : (slot + 1) * rows]
            piece[t, 0] = plain[:, :half] + turned[:, half:]
            piece[t, 1] = turned[:, :half] - plain[:, half:]


def spread_kernel(dirac16, out, wide):
    rows, vectors = dirac16.shape[0], dirac16.shape[1]
    for r in range(rows):
        wide[pl.ds(r, vectors, stride=rows), :] = dirac16[r].astype(F32)
    out[...] = wide[...].astype(BF16)


def final_kernel(kept, arrived, other, out):
    times = kept.shape[0]
    for t in range(times):
        for ri in range(2):
            total = kept[t, ri] + arrived[t, ri] + other[t, ri]
            for p in range(out.shape[0]):
                width = out.shape[4]
                out[p, t, ri] = total[:, p * width : (p + 1) * width]


def exchange(value, axis):
    size = lax.axis_size(axis)
    up = [(i, (i + 1) % size) for i in range(size)]
    down = [(j, i) for i, j in up]
    before = lax.ppermute(value, axis, up)
    if size == 2:
        return before, before
    return before, lax.ppermute(value, axis, down)


def on_device(eigen_store, fat_links, long_links, chosen, momenta, current_dirs, taste_masks):
    stored, _, _, times, depth, _ = eigen_store.shape
    vectors = chosen.shape[0]
    per_vector = 6 * times * depth
    n_ta, n_gz, n_gy = (lax.axis_size(a) for a in ("ta", "gz", "gy"))
    total_y = (LANES // HALF) * n_gy
    total_z = depth * n_gz

    store = eigen_store.transpose(0, 1, 3, 4, 2, 5).reshape(stored * per_vector, LANES)
    fat = fat_links.transpose(0, 1, 2, 3, 5, 6, 4, 7).reshape(-1, LANES)
    long = long_links.transpose(0, 1, 2, 3, 5, 6, 4, 7).reshape(-1, LANES)
    link_rows = fat.shape[0]
    shape6 = (3, times, depth, 2, vectors, LANES)
    size = per_vector * vectors

    def rows_of(n, dtype=BF16):
        return jax.ShapeDtypeStruct((n, LANES), dtype)

    far_out, side_out, packed, fat_v, long_v = call(
        functools.partial(gather_kernel, vectors),
        [rows_of(size + 32), rows_of(size + 16), rows_of(size), rows_of(link_rows), rows_of(link_rows)],
        [HB] * 4,
        [
            pltpu.SMEM(chosen.shape, jnp.int32),
            pltpu.VMEM(store.shape, BF16),
            pltpu.VMEM(store.shape, F32),
            pltpu.VMEM((size, LANES), F32),
            pltpu.SemaphoreType.DMA((4,)),
        ],
        1000,
    )(chosen, store, fat, long)
    near = [(i, i ^ 1) for i in range(n_ta)]
    far = [((i + 1) % n_ta, ((i ^ 1) + 1) % n_ta) for i in range(n_ta)]
    far_field = lax.ppermute(far_out, "ta", far)
    before_z, after_z = exchange(side_out, "gz")
    near_field = lax.ppermute(packed, "ta", near)
    y_field, _ = exchange(packed, "gy")

    slots = current_dirs.shape[0]
    count = momenta.shape[0]
    width = depth * 6 * LANES
    left_rows = slots * 2 * vectors
    rotate = n_gz == 2 and n_gy == 2
    scale = 1.0 / math.sqrt(NX * total_y * total_z / 2)
    dacc, back_xy, weights, fatf, longf = call(
        functools.partial(local_kernel, times, depth, vectors, (total_y, total_z, scale)),
        [
            jax.ShapeDtypeStruct(shape6, F32),
            jax.ShapeDtypeStruct((2,) + shape6, F32),
            jax.ShapeDtypeStruct((times * depth, 2 * count, LANES), F32),
            rows_of(link_rows, F32),
            rows_of(link_rows, F32),
        ],
        [HB] + [VM] * 4,
        [
            pltpu.SMEM((3, count), jnp.int32),
            pltpu.VMEM((2, LANES, 4 * LANES), BF16),
            pltpu.VMEM((2 * LANES, 4 * LANES), BF16),
            pltpu.SemaphoreType.DMA,
        ],
        1000,
    )(momenta.T, packed, y_field, fat_v, long_v)
    dacc, left = call(
        functools.partial(side_kernel, times, depth, vectors, rotate),
        [
            jax.ShapeDtypeStruct(shape6, F32),
            jax.ShapeDtypeStruct((times, 2 * left_rows, width), BF16),
        ],
        [HB] * 2 + [VM] * 7,
        [
            pltpu.SMEM((slots,), jnp.int32),
            pltpu.SMEM((slots,), jnp.int32),
            pltpu.VMEM((3,) + shape6, F32),
            pltpu.SemaphoreType.DMA((2,)),
        ],
        1000,
    )(current_dirs, taste_masks, packed, before_z, after_z, fatf, longf, dacc, back_xy)
    piece = jax.ShapeDtypeStruct((times, 2, vectors, count * vectors), F32)
    dirac16, *pieces = call(
        functools.partial(last_kernel, times, depth, vectors),
        [jax.ShapeDtypeStruct(shape6, BF16)] + [piece] * slots,
        [VM] * 7,
        [],
        1000,
    )(far_field, dacc, near_field, fatf, longf, weights, left)

    (odd_rows,) = call(
        spread_kernel,
        [jax.ShapeDtypeStruct((vectors * per_vector, LANES), BF16)],
        [VM],
        [pltpu.VMEM((vectors * per_vector, LANES), F32)],
        1000,
    )(dirac16.reshape(per_vector, vectors, LANES))
    odd_vectors = odd_rows.reshape(vectors, 3, times, depth, 2, LANES).transpose(0, 1, 4, 2, 3, 5)

    if rotate:
        swap = [(0, 1), (1, 0)]
        got = lax.ppermute(jnp.stack([pieces[1], pieces[3]]), "gy", swap)
        other = lax.ppermute(pieces[2] + got[1], "gz", swap)
        (meson_fields,) = call(
            final_kernel,
            [jax.ShapeDtypeStruct((count, times, 2, vectors, vectors), F32)],
            [VM] * 3,
            [],
            1000,
        )(pieces[0], got[0], other)
    else:
        whole = jnp.stack(pieces).reshape(slots, times, 2, vectors, count, vectors)
        whole = whole.transpose(0, 4, 1, 2, 3, 5).reshape(
            slots * count, times, 2, vectors, vectors
        )
        meson_fields = lax.psum_scatter(whole, ("gz", "gy"), scatter_dimension=0, tiled=True)
    return odd_vectors, meson_fields


def solution(mesh):
    in_specs = (
        P(None, None, None, ("cfg", "ta"), "gz", "gy"),
        P(None, None, None, None, None, ("cfg", "ta"), "gz", "gy"),
        P(None, None, None, None, None, ("cfg", "ta"), "gz", "gy"),
        P("cfg"),
        P(),
        P(),
        P(),
    )
    out_specs = (
        P(None, None, None, ("cfg", "ta"), "gz", "gy"),
        P(("gz", "gy"), ("cfg", "ta"), None, None, None),
    )
    return jax.shard_map(
        on_device, mesh=mesh, in_specs=in_specs, out_specs=out_specs, check_vma=False
    )
```

time: 32.7 us -> 29.9 us (0.914)
  Pallas kernels: 12.4 us -> 9.04 us
  starting transfers between devices: 7.81 us -> 8.28 us
    pallas_call x5, Pallas kernels: 11.7 us -> 8.3 us  [the longest x1 2.73 us: on_device(): call(functools.partial(local_kernel, times, depth, vectors, (total_y, tot...]
    ppermute x2, waiting for transfers between devices: 0.01 us -> 2.06 us  [exchange(): before = lax.ppermute(value, axis, up)]
    ppermute x2, starting transfers between devices: 3.08 us -> 1.49 us  [exchange(): before = lax.ppermute(value, axis, up)]
    ppermute x2, starting transfers between devices: 4.05 us -> 5.12 us  [the longest x1 5.11 us: on_device(): far_field = lax.ppermute(far_out, 'ta', far)]
    ppermute x1, waiting for transfers between devices: 3.55 us -> 2.59 us  [on_device(): other = lax.ppermute(pieces[2] + got[1], 'gz', swap)]
    ppermute x1, starting transfers between devices: 0.6 us -> 1.56 us  [on_device(): other = lax.ppermute(pieces[2] + got[1], 'gz', swap)]
    ppermute x2, waiting for transfers between devices: 1.81 us -> 0.93 us  [the longest x1 0.92 us: on_device(): near_field = lax.ppermute(packed, 'ta', near)]
    unnamed x18 -> x14, local copies, waits for them, and re-layouts: 5.54 us -> 5.54 us
  transfers between devices with their start and end apart: 6 -> 6, of which waited for: 3 -> 5; matrix products, arithmetic and copies ran while one was open for 0% -> 0% of each run, Pallas kernels for 16% -> 16%
where the time goes in v1:
time: 29.9 us; the launch traced here: 29.7 us
  Pallas kernels  9.04 us (30%)
  starting transfers between devices  8.28 us (28%)
  waiting for transfers between devices  6.09 us (20%)
  local copies, waits for them, and re-layouts  5.55 us (19%)
  between operations  0.69 us (2%)
    unnamed x14, local copies, waits for them, and re-layouts  5.54 us
    ppermute x1, starting transfers between devices, on_device(): far_field = lax.ppermute(far_out, 'ta', far)  5.11 us
    pallas_call x1, Pallas kernels, on_device(): call(functools.partial(local_kernel, times, depth, vectors, (total_y, tot...  2.73 us
    ppermute x1, waiting for transfers between devices, on_device(): other = lax.ppermute(pieces[2] + got[1], 'gz', swap)  2.59 us
    pallas_call x1, Pallas kernels, on_device(): call(functools.partial(last_kernel, times, depth, vectors), [jax.ShapeDty...  2.57 us
    ppermute x2, waiting for transfers between devices, exchange(): before = lax.ppermute(value, axis, up)  2.06 us
    ppermute x1, starting transfers between devices, on_device(): other = lax.ppermute(pieces[2] + got[1], 'gz', swap)  1.56 us
    ppermute x2, starting transfers between devices, exchange(): before = lax.ppermute(value, axis, up)  1.49 us
  transfers between devices with their start and end apart: 6, of which 5 were waited for; matrix products, arithmetic and copies ran while one was open for 0% of the time, Pallas kernels for 16%

profile of v1, /device:TPU:0, one launch (start us, length us, event | category | flops | bytes accessed | tf_op | source)
XLA Modules:
  0.0 29.7 jit_solution(7640357749718676816)
XLA Ops:
  0.6 0.0 copy-start
  0.6 1.0 %copy-done = bf16[2,4,3,3,2,3,3,128]{7,4,6,5,3,2,1,0:T(2,128)(2,1)S(1)} copy-done((bf16[2,4,3,3,2,3,3,128]{7,4,6,5,3,2,1,0:T(2,128)(2,1)S(1)}, bf16[2,4,3,3,2,3,3,128]{7,4,6,5,3,2,1,0:T(2,128)(2,1)}, u32[]{:S(2)}) %copy-start) | copy-done | bytes 331800
  1.6 0.0 copy-start.1
  1.6 1.0 %copy-done.1 = bf16[2,4,3,3,2,3,3,128]{7,4,6,5,3,2,1,0:T(2,128)(2,1)S(1)} copy-done((bf16[2,4,3,3,2,3,3,128]{7,4,6,5,3,2,1,0:T(2,128)(2,1)S(1)}, bf16[2,4,3,3,2,3,3,128]{7,4,6,5,3,2,1,0:T(2,128)(2,1)}, u32[]{:S(2)}) %copy-start.1) | copy-done | bytes 331800
  2.6 0.0 copy-start.2
  2.6 1.0 %copy-done.2 = bf16[20,3,2,3,3,128]{5,2,4,3,1,0:T(2,128)(2,1)S(1)} copy-done((bf16[20,3,2,3,3,128]{5,2,4,3,1,0:T(2,128)(2,1)S(1)}, bf16[20,3,2,3,3,128]{5,2,4,3,1,0:T(2,128)(2,1)}, u32[]{:S(2)}) %copy-start.2) | copy-done | bytes 276504
  3.5 0.0 copy-start.4
  3.5 0.7 %copy-done.4 = s32[16]{0:T(128)S(1)} copy-done((s32[16]{0:T(128)S(1)}, s32[16]{0:T(128)}, u32[]{:S(2)}) %copy-start.4) | copy-done | bytes 88
  4.2 0.9 %shard_map.86 = (bf16[896,128]{1,0:T(8,128)(2,1)S(1)}, bf16[880,128]{1,0:T(8,128)(2,1)S(1)}, bf16[864,128]{1,0:T(8,128)(2,1)S(1)}, bf16[1296,128]{1,0:T(8,128)(2,1)S(1)}, bf16[1296,128]{1,0:T(8,128)(2,1)S(1)}) custom-call(s32[16]{0:T(128)S(1)} %copy-done.4, bf16[1080,128]{1,0:T(8,128)(2,1)S(1)} %bitcast.24, bf16[1296,128]{1,0:T(8,128)(2,1)S(1)} %bitcast.22, ...), custom_call_target="tpu_custom_call" | custom-call | flops 1000 | bytes 1000 | tf_op jit(solution)/shard_map/pallas_call | solution.py:449
  5.1 5.1 %collective-permute-start = (bf16[896,128]{1,0:T(8,128)(2,1)S(1)}, bf16[896,128]{1,0:T(8,128)(2,1)S(1)}, u32[]{:S(2)}, u32[]{:S(2)}) collective-permute-start(bf16[896,128]{1,0:T(8,128)(2,1)S(1)} %get-tuple-element.19), channel_id=1, source_target_pairs={{4,8},{8,4},{12,0},{0,12},{5,9},{9,5},{13,1},{1,13},{6,10},{10,6},... | collective-permute-start | bytes 688136 | tf_op jit(solution)/shard_map/ppermute | solution.py:464
  10.2 1.5 %collective-permute-start.1 = (bf16[880,128]{1,0:T(8,128)(2,1)S(1)}, bf16[880,128]{1,0:T(8,128)(2,1)S(1)}, u32[]{:S(2)}, u32[]{:S(2)}) collective-permute-start(bf16[880,128]{1,0:T(8,128)(2,1)S(1)} %get-tuple-element.21), channel_id=1, source_target_pairs={{0,2},{2,0},{1,3},{3,1},{4,6},{6,4},{5,7},{7,5},{8,10},{10,8},{9,1... | collective-permute-start | bytes 675848 | tf_op jit(solution)/shard_map/ppermute | solution.py:425
  11.7 0.0 collective-permute-start.2
  11.7 0.0 collective-permute-start.3
  11.7 1.5 %collective-permute-done.2.y_ref = bf16[864,128]{1,0:T(8,128)(2,1)S(1)} collective-permute-done((bf16[864,128]{1,0:T(8,128)(2,1)S(1)}, bf16[864,128]{1,0:T(8,128)(2,1)S(1)}, u32[]{:S(2)}, u32[]{:S(2)}) %collective-permute-start.2) | collective-permute-done | bytes 221216 | tf_op jit(solution)/shard_map/ppermute | solution.py:425
  13.2 0.0 copy-start.3
  13.2 0.7 %copy-done.3 = s32[8,3]{0,1:T(4,128)S(1)} copy-done((s32[8,3]{0,1:T(4,128)S(1)}, s32[8,3]{0,1:T(4,128)}, u32[]{:S(2)}) %copy-start.3) | copy-done | bytes 120
  13.8 2.7 %shard_map.87 = (f32[3,3,3,2,16,128]{5,4,3,2,1,0:T(8,128)S(1)}, f32[2,3,3,3,2,16,128]{6,5,4,3,2,1,0:T(8,128)S(1)}, f32[9,16,128]{2,1,0:T(8,128)S(1)}, f32[1296,128]{1,0:T(8,128)S(1)}, f32[1296,128]{1,0:T(8,128)S(1)}) custom-call(s32[3,8]{1,0:T(4,128)S(1)} %bitcast.28, bf16[864,128]{1,0:T(8,128)(2,1)S(1)} %get-tuple-element.20.field_ref, ...), custom_call_target="tpu_custom_call" | custom-call | flops 1000 | bytes 1000 | tf_op jit(solution)/shard_map/pallas_call | solution.py:475
  16.6 0.6 %collective-permute-done.1.before_ref.after_ref = bf16[880,128]{1,0:T(8,128)(2,1)S(1)} collective-permute-done((bf16[880,128]{1,0:T(8,128)(2,1)S(1)}, bf16[880,128]{1,0:T(8,128)(2,1)S(1)}, u32[]{:S(2)}, u32[]{:S(2)}) %collective-permute-start.1) | collective-permute-done | bytes 225312 | tf_op jit(solution)/shard_map/ppermute | solution.py:425
  17.2 0.0 copy-start.5
  17.2 0.7 %copy-done.5 = s32[4]{0:T(128)S(1)} copy-done((s32[4]{0:T(128)S(1)}, s32[4]{0:T(128)}, u32[]{:S(2)}) %copy-start.5) | copy-done | bytes 40
  17.8 0.0 copy-start.6
  17.8 0.7 %copy-done.6 = s32[4]{0:T(128)S(1)} copy-done((s32[4]{0:T(128)S(1)}, s32[4]{0:T(128)}, u32[]{:S(2)}) %copy-start.6) | copy-done | bytes 40
  18.5 1.2 %shard_map.88 = (f32[3,3,3,2,16,128]{5,4,3,2,1,0:T(8,128)S(1)}, bf16[3,256,2304]{2,1,0:T(8,128)(2,1)S(1)}) custom-call(s32[4]{0:T(128)S(1)} %copy-done.5, s32[4]{0:T(128)S(1)} %copy-done.6, bf16[864,128]{1,0:T(8,128)(2,1)S(1)} %get-tuple-element.20.field_ref, bf16[880,128]{1,0:T(8,128)(2,1)S(1)} %collective-permute-done.1.before_ref.after_ref, ...), custom_call_target="tpu_custom_call" | custom-call | flops 1000 | bytes 1000 | tf_op jit(solution)/shard_map/pallas_call | solution.py:493
  19.7 0.9 %collective-permute-done.3.near_ref = bf16[864,128]{1,0:T(8,128)(2,1)S(1)} collective-permute-done((bf16[864,128]{1,0:T(8,128)(2,1)S(1)}, bf16[864,128]{1,0:T(8,128)(2,1)S(1)}, u32[]{:S(2)}, u32[]{:S(2)}) %collective-permute-start.3) | collective-permute-done | bytes 221216 | tf_op jit(solution)/shard_map/ppermute | solution.py:466
  20.6 0.0 collective-permute-done.far_ref
  20.6 2.6 %shard_map.89 = (bf16[3,3,3,2,16,128]{5,4,3,2,1,0:T(8,128)(2,1)S(1)}, f32[3,2,16,128]{3,2,1,0:T(8,128)S(1)}, f32[3,2,16,128]{3,2,1,0:T(8,128)S(1)}, f32[3,2,16,128]{3,2,1,0:T(8,128)S(1)}, f32[3,2,16,128]{3,2,1,0:T(8,128)S(1)}) custom-call(bf16[896,128]{1,0:T(8,128)(2,1)S(1)} %collective-permute-done.far_ref, ...), custom_call_target="tpu_custom_call" | custom-call | flops 1000 | bytes 1000 | tf_op jit(solution)/shard_map/pallas_call | solution.py:509
  23.2 0.1 collective-permute-start.4
  23.3 0.7 %shard_map.90 = bf16[864,128]{1,0:T(8,128)(2,1)} custom-call(bf16[54,16,128]{2,1,0:T(8,128)(2,1)S(1)} %bitcast.25), custom_call_target="tpu_custom_call" | custom-call | flops 1000 | bytes 1000 | tf_op jit(solution)/shard_map/pallas_call | solution.py:517
  24.1 0.5 %collective-permute-done.4 = f32[2,3,2,16,128]{4,3,2,1,0:T(8,128)S(1)} collective-permute-done((f32[2,3,2,16,128]{4,3,2,1,0:T(8,128)S(1)}, f32[2,3,2,16,128]{4,3,2,1,0:T(8,128)S(1)}, u32[]{:S(2)}, u32[]{:S(2)}) %collective-permute-start.4) | collective-permute-done | bytes 98336 | tf_op jit(solution)/shard_map/ppermute | solution.py:528
  24.6 1.6 %collective-permute-start.5 = (f32[3,2,16,128]{3,2,1,0:T(8,128)S(1)}, f32[3,2,16,128]{3,2,1,0:T(8,128)S(1)}, u32[]{:S(2)}, u32[]{:S(2)}) collective-permute-start(f32[3,2,16,128]{3,2,1,0:T(8,128)S(1)} %fusion), channel_id=1, source_target_pairs={{0,2},{2,0},{1,3},{3,1},{4,6},{6,4},{5,7},{7,5},{8,10},{10,8},{9,1... | collective-permute-start | bytes 147464 | tf_op jit(solution)/shard_map/ppermute | solution.py:529
  26.2 2.6 %collective-permute-done.5.other = f32[3,2,16,128]{3,2,1,0:T(8,128)S(1)} collective-permute-done((f32[3,2,16,128]{3,2,1,0:T(8,128)S(1)}, f32[3,2,16,128]{3,2,1,0:T(8,128)S(1)}, u32[]{:S(2)}, u32[]{:S(2)}) %collective-permute-start.5) | collective-permute-done | bytes 49184 | tf_op jit(solution)/shard_map/ppermute | solution.py:529
  28.8 0.9 %shard_map.91 = f32[8,3,2,16,16]{4,3,2,1,0:T(8,128)} custom-call(f32[3,2,16,128]{3,2,1,0:T(8,128)S(1)} %get-tuple-element.32.kept, f32[3,2,16,128]{3,2,1,0:T(8,128)S(1)} %slice_bitcast_fusion.1.arrived, f32[3,2,16,128]{3,2,1,0:T(8,128)S(1)} %collective-permute-done.5.other), custom_call_target="tpu_custom_call" | custom-call | flops 1000 | bytes 1000 | tf_op jit(solution)/shard_map/pallas_call | solution.py:530
  (3 shorter events, 0.0 us)
Async XLA Ops:
  0.6 1.0 %copy-start = (bf16[2,4,3,3,2,3,3,128]{7,4,6,5,3,2,1,0:T(2,128)(2,1)S(1)}, bf16[2,4,3,3,2,3,3,128]{7,4,6,5,3,2,1,0:T(2,128)(2,1)}, u32[]{:S(2)}) copy-start(bf16[2,4,3,3,2,3,3,128]{7,4,6,5,3,2,1,0:T(2,128)(2,1)} %param.8) | copy-start | bytes 995332
  1.6 1.0 %copy-start.1 = (bf16[2,4,3,3,2,3,3,128]{7,4,6,5,3,2,1,0:T(2,128)(2,1)S(1)}, bf16[2,4,3,3,2,3,3,128]{7,4,6,5,3,2,1,0:T(2,128)(2,1)}, u32[]{:S(2)}) copy-start(bf16[2,4,3,3,2,3,3,128]{7,4,6,5,3,2,1,0:T(2,128)(2,1)} %param.9) | copy-start | bytes 995332
  2.6 1.0 %copy-start.2 = (bf16[20,3,2,3,3,128]{5,2,4,3,1,0:T(2,128)(2,1)S(1)}, bf16[20,3,2,3,3,128]{5,2,4,3,1,0:T(2,128)(2,1)}, u32[]{:S(2)}) copy-start(bf16[20,3,2,3,3,128]{5,2,4,3,1,0:T(2,128)(2,1)} %param.7) | copy-start | bytes 829444
  3.5 0.7 %copy-start.4 = (s32[16]{0:T(128)S(1)}, s32[16]{0:T(128)}, u32[]{:S(2)}) copy-start(s32[16]{0:T(128)} %chosen_hbm.1) | copy-start | bytes 196
  5.1 15.6 %collective-permute-start = (bf16[896,128]{1,0:T(8,128)(2,1)S(1)}, bf16[896,128]{1,0:T(8,128)(2,1)S(1)}, u32[]{:S(2)}, u32[]{:S(2)}) collective-permute-start(bf16[896,128]{1,0:T(8,128)(2,1)S(1)} %get-tuple-element.19), channel_id=1, source_target_pairs={{4,8},{8,4},{12,0},{0,12},{5,9},{9,5},{13,1},{1,13},{6,10},{10,6},... | collective-permute-start | bytes 688136 | tf_op jit(solution)/shard_map/ppermute | solution.py:464
  10.2 7.0 %collective-permute-start.1 = (bf16[880,128]{1,0:T(8,128)(2,1)S(1)}, bf16[880,128]{1,0:T(8,128)(2,1)S(1)}, u32[]{:S(2)}, u32[]{:S(2)}) collective-permute-start(bf16[880,128]{1,0:T(8,128)(2,1)S(1)} %get-tuple-element.21), channel_id=1, source_target_pairs={{0,2},{2,0},{1,3},{3,1},{4,6},{6,4},{5,7},{7,5},{8,10},{10,8},{9,1... | collective-permute-start | bytes 675848 | tf_op jit(solution)/shard_map/ppermute | solution.py:425
  11.7 1.5 %collective-permute-start.2 = (bf16[864,128]{1,0:T(8,128)(2,1)S(1)}, bf16[864,128]{1,0:T(8,128)(2,1)S(1)}, u32[]{:S(2)}, u32[]{:S(2)}) collective-permute-start(bf16[864,128]{1,0:T(8,128)(2,1)S(1)} %get-tuple-element.20.field_ref), channel_id=1, source_target_pairs={{0,1},{1,0},{2,3},{3,2},{4,5},{5,4},{6,7},{7,6},{8,9},{9,8},{10,11... | collective-permute-start | bytes 663560 | tf_op jit(solution)/shard_map/ppermute | solution.py:425
  11.7 8.9 %collective-permute-start.3 = (bf16[864,128]{1,0:T(8,128)(2,1)S(1)}, bf16[864,128]{1,0:T(8,128)(2,1)S(1)}, u32[]{:S(2)}, u32[]{:S(2)}) collective-permute-start(bf16[864,128]{1,0:T(8,128)(2,1)S(1)} %get-tuple-element.20.field_ref), channel_id=1, source_target_pairs={{0,4},{4,0},{8,12},{12,8},{1,5},{5,1},{9,13},{13,9},{2,6},{6,2},{1... | collective-permute-start | bytes 663560 | tf_op jit(solution)/shard_map/ppermute | solution.py:466
  13.2 0.7 %copy-start.3 = (s32[8,3]{0,1:T(4,128)S(1)}, s32[8,3]{0,1:T(4,128)}, u32[]{:S(2)}) copy-start(s32[8,3]{0,1:T(4,128)} %param.11) | copy-start | bytes 292
  17.2 0.7 %copy-start.5 = (s32[4]{0:T(128)S(1)}, s32[4]{0:T(128)}, u32[]{:S(2)}) copy-start(s32[4]{0:T(128)} %dirs_hbm.1) | copy-start | bytes 52
  17.8 0.7 %copy-start.6 = (s32[4]{0:T(128)S(1)}, s32[4]{0:T(128)}, u32[]{:S(2)}) copy-start(s32[4]{0:T(128)} %masks_hbm.1) | copy-start | bytes 52
  23.2 1.4 %collective-permute-start.4 = (f32[2,3,2,16,128]{4,3,2,1,0:T(8,128)S(1)}, f32[2,3,2,16,128]{4,3,2,1,0:T(8,128)S(1)}, u32[]{:S(2)}, u32[]{:S(2)}) collective-permute-start(f32[2,3,2,16,128]{4,3,2,1,0:T(8,128)S(1)} %pad_maximum_fusion), channel_id=1, source_target_pairs={{0,1},{1,0},{2,3},{3,2},{4,5},{5,4},{6,7},{7,6},{8,9},{9,8},{10,11... | collective-permute-start | bytes 294920 | tf_op jit(solution)/shard_map/ppermute | solution.py:528
  24.6 4.2 %collective-permute-start.5 = (f32[3,2,16,128]{3,2,1,0:T(8,128)S(1)}, f32[3,2,16,128]{3,2,1,0:T(8,128)S(1)}, u32[]{:S(2)}, u32[]{:S(2)}) collective-permute-start(f32[3,2,16,128]{3,2,1,0:T(8,128)S(1)} %fusion), channel_id=1, source_target_pairs={{0,2},{2,0},{1,3},{3,1},{4,6},{6,4},{5,7},{7,5},{8,10},{10,8},{9,1... | collective-permute-start | bytes 147464 | tf_op jit(solution)/shard_map/ppermute | solution.py:529

commit v2 on v1

--- a/solution.py
+++ b/solution.py
@@ -16,6 +16,10 @@
 VM = pl.BlockSpec(memory_space=pltpu.VMEM)
 SM = pl.BlockSpec(memory_space=pltpu.SMEM)
 HB = pl.BlockSpec(memory_space=pltpu.HBM)
+
+
+def pinned(value):
+    return pltpu.with_memory_space_constraint(value, pltpu.HBM)
 
 
 def call(body, outs, ins, scratch, cost):
@@ -401,20 +405,26 @@
             piece[t, 1] = turned[:, :half] - plain[:, half:]
 
 
-def spread_kernel(dirac16, out, wide):
+def spread_kernel(dirac16, kept, arrived, out, partial, wide):
     rows, vectors = dirac16.shape[0], dirac16.shape[1]
+    if partial is not None:
+        partial[...] = kept[...] + arrived[...]
     for r in range(rows):
         wide[pl.ds(r, vectors, stride=rows), :] = dirac16[r].astype(F32)
     out[...] = wide[...].astype(BF16)
 
 
-def final_kernel(kept, arrived, other, out):
-    times = kept.shape[0]
+def turn_kernel(dirac16, out, wide):
+    spread_kernel(dirac16, None, None, out, None, wide)
+
+
+def final_kernel(partial, other, out):
+    times = partial.shape[0]
+    width = out.shape[4]
     for t in range(times):
         for ri in range(2):
-            total = kept[t, ri] + arrived[t, ri] + other[t, ri]
+            total = partial[t, ri] + other[t, ri]
             for p in range(out.shape[0]):
-                width = out.shape[4]
                 out[p, t, ri] = total[:, p * width : (p + 1) * width]
 
 
@@ -458,7 +468,7 @@
             pltpu.SemaphoreType.DMA((4,)),
         ],
         1000,
-    )(chosen, store, fat, long)
+    )(*map(pinned, (chosen, store, fat, long)))
     near = [(i, i ^ 1) for i in range(n_ta)]
     far = [((i + 1) % n_ta, ((i ^ 1) + 1) % n_ta) for i in range(n_ta)]
     far_field = lax.ppermute(far_out, "ta", far)
@@ -489,7 +499,7 @@
             pltpu.SemaphoreType.DMA,
         ],
         1000,
-    )(momenta.T, packed, y_field, fat_v, long_v)
+    )(pinned(momenta.T), packed, y_field, fat_v, long_v)
     dacc, left = call(
         functools.partial(side_kernel, times, depth, vectors, rotate),
         [
@@ -504,7 +514,9 @@
             pltpu.SemaphoreType.DMA((2,)),
         ],
         1000,
-    )(current_dirs, taste_masks, packed, before_z, after_z, fatf, longf, dacc, back_xy)
+    )(
+        pinned(current_dirs), pinned(taste_masks), packed, before_z, after_z, fatf, longf, dacc, back_xy
+    )
     piece = jax.ShapeDtypeStruct((times, 2, vectors, count * vectors), F32)
     dirac16, *pieces = call(
         functools.partial(last_kernel, times, depth, vectors),
@@ -514,32 +526,26 @@
         1000,
     )(far_field, dacc, near_field, fatf, longf, weights, left)
 
-    (odd_rows,) = call(
-        spread_kernel,
-        [jax.ShapeDtypeStruct((vectors * per_vector, LANES), BF16)],
-        [VM],
-        [pltpu.VMEM((vectors * per_vector, LANES), F32)],
-        1000,
-    )(dirac16.reshape(per_vector, vectors, LANES))
-    odd_vectors = odd_rows.reshape(vectors, 3, times, depth, 2, LANES).transpose(0, 1, 4, 2, 3, 5)
-
+    odd_shape = rows_of(size)
+    turned = dirac16.reshape(per_vector, vectors, LANES)
+    scratch = [pltpu.VMEM((size, LANES), F32)]
     if rotate:
         swap = [(0, 1), (1, 0)]
         got = lax.ppermute(jnp.stack([pieces[1], pieces[3]]), "gy", swap)
         other = lax.ppermute(pieces[2] + got[1], "gz", swap)
-        (meson_fields,) = call(
-            final_kernel,
-            [jax.ShapeDtypeStruct((count, times, 2, vectors, vectors), F32)],
-            [VM] * 3,
-            [],
-            1000,
-        )(pieces[0], got[0], other)
+        odd_rows, partial = call(
+            spread_kernel, [odd_shape, piece], [VM] * 3, scratch, 1000
+        )(turned, pieces[0], got[0])
+        meson_shape = jax.ShapeDtypeStruct((count, times, 2, vectors, vectors), F32)
+        (meson_fields,) = call(final_kernel, [meson_shape], [VM] * 2, [], 1000)(partial, other)
     else:
+        (odd_rows,) = call(turn_kernel, [odd_shape], [VM], scratch, 1000)(turned)
         whole = jnp.stack(pieces).reshape(slots, times, 2, vectors, count, vectors)
         whole = whole.transpose(0, 4, 1, 2, 3, 5).reshape(
             slots * count, times, 2, vectors, vectors
         )
         meson_fields = lax.psum_scatter(whole, ("gz", "gy"), scatter_dimension=0, tiled=True)
+    odd_vectors = odd_rows.reshape(vectors, 3, times, depth, 2, LANES).transpose(0, 1, 4, 2, 3, 5)
     return odd_vectors, meson_fields
 
 

time: 29.9 us -> 26.6 us (0.89)
  local copies, waits for them, and re-layouts: 5.55 us -> 0.01 us
  waiting for transfers between devices: 6.09 us -> 8.14 us
  Pallas kernels: 9.04 us -> 9.37 us
    unnamed x14 -> x0, local copies, waits for them, and re-layouts: 5.54 us -> none
    ppermute x1, waiting for transfers between devices: 0.92 us -> 2.25 us  [on_device(): near_field = lax.ppermute(packed, 'ta', near)]
    ppermute x1, waiting for transfers between devices: 2.59 us -> 1.85 us  [on_device(): other = lax.ppermute(pieces[2] + got[1], 'gz', swap)]
    ppermute x1, waiting for transfers between devices: 0.51 us -> 1.25 us  [on_device(): got = lax.ppermute(jnp.stack([pieces[1], pieces[3]]), 'gy', swap)]
    ppermute x2, waiting for transfers between devices: 2.06 us -> 2.79 us  [exchange(): before = lax.ppermute(value, axis, up)]
    pallas_call x1, Pallas kernels: 0.87 us -> 1.29 us  [on_device(): call(functools.partial(gather_kernel, vectors), [rows_of(size + 32), rows...]
  transfers between devices with their start and end apart: 6 -> 6, of which waited for: 5 -> 5; matrix products, arithmetic and copies ran while one was open for 0% -> 0% of each run, Pallas kernels for 16% -> 17%
where the time goes in v2:
time: 26.6 us; the launch traced here: 26.5 us
  Pallas kernels  9.37 us (35%)
  starting transfers between devices  8.29 us (31%)
  waiting for transfers between devices  8.14 us (31%)
  between operations  0.68 us (3%)
    ppermute x1, starting transfers between devices, on_device(): far_field = lax.ppermute(far_out, 'ta', far)  5.11 us
    ppermute x2, waiting for transfers between devices, exchange(): before = lax.ppermute(value, axis, up)  2.79 us
    pallas_call x1, Pallas kernels, on_device(): call(functools.partial(local_kernel, times, depth, vectors, (total_y, tot...  2.68 us
    pallas_call x1, Pallas kernels, on_device(): call(functools.partial(last_kernel, times, depth, vectors), [jax.ShapeDty...  2.54 us
    ppermute x1, waiting for transfers between devices, on_device(): near_field = lax.ppermute(packed, 'ta', near)  2.25 us
    ppermute x1, waiting for transfers between devices, on_device(): other = lax.ppermute(pieces[2] + got[1], 'gz', swap)  1.85 us
    ppermute x1, starting transfers between devices, on_device(): other = lax.ppermute(pieces[2] + got[1], 'gz', swap)  1.56 us
    ppermute x2, starting transfers between devices, exchange(): before = lax.ppermute(value, axis, up)  1.49 us
  transfers between devices with their start and end apart: 6, of which 5 were waited for; matrix products, arithmetic and copies ran while one was open for 0% of the time, Pallas kernels for 17%

profile of v2, /device:TPU:0, one launch (start us, length us, event | category | flops | bytes accessed | tf_op | source)
XLA Modules:
  0.0 26.5 jit_solution(16799569336913865860)
XLA Ops:
  0.6 1.3 %shard_map.86 = (bf16[896,128]{1,0:T(8,128)(2,1)S(1)}, bf16[880,128]{1,0:T(8,128)(2,1)S(1)}, bf16[864,128]{1,0:T(8,128)(2,1)S(1)}, bf16[1296,128]{1,0:T(8,128)(2,1)S(1)}, bf16[1296,128]{1,0:T(8,128)(2,1)S(1)}) custom-call(s32[16]{0:T(128)} %chosen_hbm.1, bf16[1080,128]{1,0:T(8,128)(2,1)} %bitcast.27, bf16[1296,128]{1,0:T(8,128)(2,1)} %bitcast.25, ...), custom_call_target="tpu_custom_call" | custom-call | flops 1000 | bytes 1000 | tf_op jit(solution)/shard_map/pallas_call | solution.py:459
  1.9 5.1 %collective-permute-start = (bf16[896,128]{1,0:T(8,128)(2,1)S(1)}, bf16[896,128]{1,0:T(8,128)(2,1)S(1)}, u32[]{:S(2)}, u32[]{:S(2)}) collective-permute-start(bf16[896,128]{1,0:T(8,128)(2,1)S(1)} %get-tuple-element.21), channel_id=1, source_target_pairs={{4,8},{8,4},{12,0},{0,12},{5,9},{9,5},{13,1},{1,13},{6,10},{10,6},... | collective-permute-start | bytes 688136 | tf_op jit(solution)/shard_map/ppermute | solution.py:474
  7.0 1.5 %collective-permute-start.1 = (bf16[880,128]{1,0:T(8,128)(2,1)S(1)}, bf16[880,128]{1,0:T(8,128)(2,1)S(1)}, u32[]{:S(2)}, u32[]{:S(2)}) collective-permute-start(bf16[880,128]{1,0:T(8,128)(2,1)S(1)} %get-tuple-element.23), channel_id=1, source_target_pairs={{0,2},{2,0},{1,3},{3,1},{4,6},{6,4},{5,7},{7,5},{8,10},{10,8},{9,1... | collective-permute-start | bytes 675848 | tf_op jit(solution)/shard_map/ppermute | solution.py:435
  8.5 0.0 collective-permute-start.2
  8.5 0.0 collective-permute-start.3
  8.5 1.5 %collective-permute-done.2.y_ref = bf16[864,128]{1,0:T(8,128)(2,1)S(1)} collective-permute-done((bf16[864,128]{1,0:T(8,128)(2,1)S(1)}, bf16[864,128]{1,0:T(8,128)(2,1)S(1)}, u32[]{:S(2)}, u32[]{:S(2)}) %collective-permute-start.2) | collective-permute-done | bytes 221216 | tf_op jit(solution)/shard_map/ppermute | solution.py:435
  10.0 2.7 %shard_map.87 = (f32[3,3,3,2,16,128]{5,4,3,2,1,0:T(8,128)S(1)}, f32[2,3,3,3,2,16,128]{6,5,4,3,2,1,0:T(8,128)S(1)}, f32[9,16,128]{2,1,0:T(8,128)S(1)}, f32[1296,128]{1,0:T(8,128)S(1)}, f32[1296,128]{1,0:T(8,128)S(1)}) custom-call(s32[3,8]{1,0:T(4,128)} %bitcast.28, bf16[864,128]{1,0:T(8,128)(2,1)S(1)} %get-tuple-element.22.field_ref, ...), custom_call_target="tpu_custom_call" | custom-call | flops 1000 | bytes 1000 | tf_op jit(solution)/shard_map/pallas_call | solution.py:485
  12.7 1.3 %collective-permute-done.1.before_ref.after_ref = bf16[880,128]{1,0:T(8,128)(2,1)S(1)} collective-permute-done((bf16[880,128]{1,0:T(8,128)(2,1)S(1)}, bf16[880,128]{1,0:T(8,128)(2,1)S(1)}, u32[]{:S(2)}, u32[]{:S(2)}) %collective-permute-start.1) | collective-permute-done | bytes 225312 | tf_op jit(solution)/shard_map/ppermute | solution.py:435
  14.0 1.2 %shard_map.88 = (f32[3,3,3,2,16,128]{5,4,3,2,1,0:T(8,128)S(1)}, bf16[3,256,2304]{2,1,0:T(8,128)(2,1)S(1)}) custom-call(s32[4]{0:T(128)} %dirs_hbm.1, s32[4]{0:T(128)} %masks_hbm.1, bf16[864,128]{1,0:T(8,128)(2,1)S(1)} %get-tuple-element.22.field_ref, bf16[880,128]{1,0:T(8,128)(2,1)S(1)} %collective-permute-done.1.before_ref.after_ref, ...), custom_call_target="tpu_custom_call" | custom-call | flops 1000 | bytes 1000 | tf_op jit(solution)/shard_map/pallas_call | solution.py:503
  15.2 2.2 %collective-permute-done.3.near_ref = bf16[864,128]{1,0:T(8,128)(2,1)S(1)} collective-permute-done((bf16[864,128]{1,0:T(8,128)(2,1)S(1)}, bf16[864,128]{1,0:T(8,128)(2,1)S(1)}, u32[]{:S(2)}, u32[]{:S(2)}) %collective-permute-start.3) | collective-permute-done | bytes 221216 | tf_op jit(solution)/shard_map/ppermute | solution.py:476
  17.5 0.0 collective-permute-done.far_ref
  17.5 2.5 %shard_map.89 = (bf16[3,3,3,2,16,128]{5,4,3,2,1,0:T(8,128)(2,1)S(1)}, f32[3,2,16,128]{3,2,1,0:T(8,128)S(1)}, f32[3,2,16,128]{3,2,1,0:T(8,128)S(1)}, f32[3,2,16,128]{3,2,1,0:T(8,128)S(1)}, f32[3,2,16,128]{3,2,1,0:T(8,128)S(1)}) custom-call(bf16[896,128]{1,0:T(8,128)(2,1)S(1)} %collective-permute-done.far_ref, ...), custom_call_target="tpu_custom_call" | custom-call | flops 1000 | bytes 1000 | tf_op jit(solution)/shard_map/pallas_call | solution.py:521
  20.1 0.1 collective-permute-start.4
  20.2 1.2 %collective-permute-done.4 = f32[2,3,2,16,128]{4,3,2,1,0:T(8,128)S(1)} collective-permute-done((f32[2,3,2,16,128]{4,3,2,1,0:T(8,128)S(1)}, f32[2,3,2,16,128]{4,3,2,1,0:T(8,128)S(1)}, u32[]{:S(2)}, u32[]{:S(2)}) %collective-permute-start.4) | collective-permute-done | bytes 98336 | tf_op jit(solution)/shard_map/ppermute | solution.py:534
  21.4 1.6 %collective-permute-start.5 = (f32[3,2,16,128]{3,2,1,0:T(8,128)S(1)}, f32[3,2,16,128]{3,2,1,0:T(8,128)S(1)}, u32[]{:S(2)}, u32[]{:S(2)}) collective-permute-start(f32[3,2,16,128]{3,2,1,0:T(8,128)S(1)} %fusion), channel_id=1, source_target_pairs={{0,2},{2,0},{1,3},{3,1},{4,6},{6,4},{5,7},{7,5},{8,10},{10,8},{9,1... | collective-permute-start | bytes 147464 | tf_op jit(solution)/shard_map/ppermute | solution.py:535
  23.0 0.7 %shard_map.90 = (bf16[864,128]{1,0:T(8,128)(2,1)}, f32[3,2,16,128]{3,2,1,0:T(8,128)S(1)}) custom-call(bf16[54,16,128]{2,1,0:T(8,128)(2,1)S(1)} %bitcast.22, f32[3,2,16,128]{3,2,1,0:T(8,128)S(1)} %get-tuple-element.34.kept, f32[3,2,16,128]{3,2,1,0:T(8,128)S(1)} %slice_bitcast_fusion.1.arrived), custom_call_target="tpu_custom_call" | custom-call | flops 1000 | bytes 1000 | tf_op jit(solution)/shard_map/pallas_call | solution.py:536
  23.7 1.8 %collective-permute-done.5.other = f32[3,2,16,128]{3,2,1,0:T(8,128)S(1)} collective-permute-done((f32[3,2,16,128]{3,2,1,0:T(8,128)S(1)}, f32[3,2,16,128]{3,2,1,0:T(8,128)S(1)}, u32[]{:S(2)}, u32[]{:S(2)}) %collective-permute-start.5) | collective-permute-done | bytes 49184 | tf_op jit(solution)/shard_map/ppermute | solution.py:535
  25.6 0.9 %shard_map.91 = f32[8,3,2,16,16]{4,3,2,1,0:T(8,128)} custom-call(f32[3,2,16,128]{3,2,1,0:T(8,128)S(1)} %get-tuple-element.38.partial, f32[3,2,16,128]{3,2,1,0:T(8,128)S(1)} %collective-permute-done.5.other), custom_call_target="tpu_custom_call" | custom-call | flops 1000 | bytes 1000 | tf_op jit(solution)/shard_map/pallas_call | solution.py:540
  (3 shorter events, 0.0 us)
Async XLA Ops:
  1.9 15.6 %collective-permute-start = (bf16[896,128]{1,0:T(8,128)(2,1)S(1)}, bf16[896,128]{1,0:T(8,128)(2,1)S(1)}, u32[]{:S(2)}, u32[]{:S(2)}) collective-permute-start(bf16[896,128]{1,0:T(8,128)(2,1)S(1)} %get-tuple-element.21), channel_id=1, source_target_pairs={{4,8},{8,4},{12,0},{0,12},{5,9},{9,5},{13,1},{1,13},{6,10},{10,6},... | collective-permute-start | bytes 688136 | tf_op jit(solution)/shard_map/ppermute | solution.py:474
  7.0 7.0 %collective-permute-start.1 = (bf16[880,128]{1,0:T(8,128)(2,1)S(1)}, bf16[880,128]{1,0:T(8,128)(2,1)S(1)}, u32[]{:S(2)}, u32[]{:S(2)}) collective-permute-start(bf16[880,128]{1,0:T(8,128)(2,1)S(1)} %get-tuple-element.23), channel_id=1, source_target_pairs={{0,2},{2,0},{1,3},{3,1},{4,6},{6,4},{5,7},{7,5},{8,10},{10,8},{9,1... | collective-permute-start | bytes 675848 | tf_op jit(solution)/shard_map/ppermute | solution.py:435
  8.5 1.5 %collective-permute-start.2 = (bf16[864,128]{1,0:T(8,128)(2,1)S(1)}, bf16[864,128]{1,0:T(8,128)(2,1)S(1)}, u32[]{:S(2)}, u32[]{:S(2)}) collective-permute-start(bf16[864,128]{1,0:T(8,128)(2,1)S(1)} %get-tuple-element.22.field_ref), channel_id=1, source_target_pairs={{0,1},{1,0},{2,3},{3,2},{4,5},{5,4},{6,7},{7,6},{8,9},{9,8},{10,11... | collective-permute-start | bytes 663560 | tf_op jit(solution)/shard_map/ppermute | solution.py:435
  8.5 8.9 %collective-permute-start.3 = (bf16[864,128]{1,0:T(8,128)(2,1)S(1)}, bf16[864,128]{1,0:T(8,128)(2,1)S(1)}, u32[]{:S(2)}, u32[]{:S(2)}) collective-permute-start(bf16[864,128]{1,0:T(8,128)(2,1)S(1)} %get-tuple-element.22.field_ref), channel_id=1, source_target_pairs={{0,4},{4,0},{8,12},{12,8},{1,5},{5,1},{9,13},{13,9},{2,6},{6,2},{1... | collective-permute-start | bytes 663560 | tf_op jit(solution)/shard_map/ppermute | solution.py:476
  20.1 1.4 %collective-permute-start.4 = (f32[2,3,2,16,128]{4,3,2,1,0:T(8,128)S(1)}, f32[2,3,2,16,128]{4,3,2,1,0:T(8,128)S(1)}, u32[]{:S(2)}, u32[]{:S(2)}) collective-permute-start(f32[2,3,2,16,128]{4,3,2,1,0:T(8,128)S(1)} %pad_maximum_fusion), channel_id=1, source_target_pairs={{0,1},{1,0},{2,3},{3,2},{4,5},{5,4},{6,7},{7,6},{8,9},{9,8},{10,11... | collective-permute-start | bytes 294920 | tf_op jit(solution)/shard_map/ppermute | solution.py:534
  21.4 4.2 %collective-permute-start.5 = (f32[3,2,16,128]{3,2,1,0:T(8,128)S(1)}, f32[3,2,16,128]{3,2,1,0:T(8,128)S(1)}, u32[]{:S(2)}, u32[]{:S(2)}) collective-permute-start(f32[3,2,16,128]{3,2,1,0:T(8,128)S(1)} %fusion), channel_id=1, source_target_pairs={{0,2},{2,0},{1,3},{3,1},{4,6},{6,4},{5,7},{7,5},{8,10},{10,8},{9,1... | collective-permute-start | bytes 147464 | tf_op jit(solution)/shard_map/ppermute | solution.py:535

commit v3 on v2

--- a/solution.py
+++ b/solution.py
@@ -34,22 +34,14 @@
     )
 
 
-def gather_kernel(
-    vectors, chosen_hbm, store_hbm, fat_hbm, long_hbm,
-    far, side, out, fat, long,
-    chosen, store, wide, turned, sems,
-):
-    first = [
+def gather_kernel(vectors, chosen_hbm, store_hbm, far, out, chosen, store, wide, turned, sems):
+    copies = [
         pltpu.make_async_copy(chosen_hbm, chosen, sems.at[0]),
         pltpu.make_async_copy(store_hbm, store, sems.at[1]),
     ]
-    later = [
-        pltpu.make_async_copy(fat_hbm, fat, sems.at[2]),
-        pltpu.make_async_copy(long_hbm, long, sems.at[3]),
-    ]
-    for copy in first + later:
+    for copy in copies:
         copy.start()
-    for copy in first:
+    for copy in copies:
         copy.wait()
     size = out.shape[0]
     rows = size // vectors
@@ -70,11 +62,7 @@
         block = turned[r : r + 16, :].astype(BF16)
         out[r : r + 16, :] = block
         far[r : r + 16, :] = block
-        side[r : r + 16, :] = block
-    for ref in (far, side):
-        ref[size:, :] = jnp.zeros((ref.shape[0] - size, LANES), BF16)
-    for copy in later:
-        copy.wait()
+    far[size:, :] = jnp.zeros((far.shape[0] - size, LANES), BF16)
 
 
 class Links:
@@ -186,15 +174,18 @@
 
 def local_kernel(
     times, depth, vectors, sizes,
-    momenta_hbm, field_ref, y_ref, fat, long,
+    momenta_hbm, fat_hbm, long_hbm, field_ref, y_ref,
     dacc, back_xy, weights, fatf, longf,
-    momenta, x_perm, y_perm, sem,
+    momenta, fat, long, x_perm, y_perm, sems,
 ):
     total_y, total_z, scale = sizes
-    copy = pltpu.make_async_copy(momenta_hbm, momenta, sem)
-    copy.start()
-    fatf[...] = fat[...].astype(F32)
-    longf[...] = long[...].astype(F32)
+    copies = [
+        pltpu.make_async_copy(fat_hbm, fat, sems.at[0]),
+        pltpu.make_async_copy(long_hbm, long, sems.at[1]),
+        pltpu.make_async_copy(momenta_hbm, momenta, sems.at[2]),
+    ]
+    for copy in copies:
+        copy.start()
     fat_l, long_l = Links(fatf, times, depth), Links(longf, times, depth)
     field = Field(field_ref, times, depth, vectors)
     y_field = Field(y_ref, times, depth, vectors)
@@ -202,6 +193,10 @@
     for e in range(2):
         x_perm[e] = x_permutation(origin + e)
     y_perm[...] = y_permutation()
+    for copy in copies:
+        copy.wait()
+    fatf[...] = fat[...].astype(F32)
+    longf[...] = long[...].astype(F32)
     for t in range(times):
         for z in range(depth):
             here = field.stacked(t, z)
@@ -231,7 +226,6 @@
             if z + 1 < depth:
                 add_hop(acc, fat_l, 0, 1, t, z, field.read(t, z + 1), False)
             write(dacc, t, z, acc)
-    copy.wait()
     count = momenta.shape[1]
     lane = lax.broadcasted_iota(jnp.int32, (count, LANES), 1)
     sub = lax.broadcasted_iota(jnp.int32, (count, LANES), 0)
@@ -254,7 +248,7 @@
             weights[t * depth + z, count : 2 * count] = sine * scale
 
 
-def turn_split(value):
+def halves(value):
     high = value.astype(BF16)
     low = (value - high.astype(F32)).astype(BF16)
     return high, low
@@ -334,8 +328,8 @@
                     col = (z * 3 + a) * 2 * LANES
                     first = slice(col, col + LANES)
                     other = slice(col + LANES, col + 2 * LANES)
-                    real = turn_split(back[direction, a, t, z, 0] * sign)
-                    imag = turn_split(back[direction, a, t, z, 1] * sign)
+                    real = halves(back[direction, a, t, z, 0] * sign)
+                    imag = halves(back[direction, a, t, z, 1] * sign)
                     for part in range(2):
                         top = part * low_part + slot * 2 * vectors
                         turned = top + vectors
@@ -366,11 +360,10 @@
 
     rows = 2 * vectors
     left_rows = left.shape[1] // 2
-    count = weights.shape[1]
-    half = count * vectors // 2
+    count = weights.shape[1] // 2
+    columns = count * vectors
     for t in range(times):
-        main = jnp.zeros((2 * left_rows, count * vectors), F32)
-        rest = jnp.zeros((left_rows, count * vectors), F32)
+        parts = jnp.zeros((2 * left_rows, 2 * columns), F32)
         for z in range(depth):
             acc = read(dacc, t, z)
             add_hop(acc, long_l, 0, 0, t, z, widen(pick(near, far, t, z)), False)
@@ -380,29 +373,36 @@
             if t == 0:
                 add_hop(acc, fat_l, 1, 0, t, z, widen(pick(far, near, times - 1, z)), True)
             write(dirac16, t, z, acc)
+            at = t * depth + z
             for a in range(3):
-                high, low = [], []
-                for ri in range(2):
-                    parts = [
-                        turn_split(acc[a][ri] * weights[t * depth + z, w : w + 1, :])
-                        for w in range(count)
-                    ]
-                    high.append(jnp.concatenate([h for h, _ in parts], axis=0))
-                    low.append(jnp.concatenate([l for _, l in parts], axis=0))
-                high = jnp.concatenate(high, axis=1)
-                low = jnp.concatenate(low, axis=1)
+                real, imag = acc[a]
+                right = [[], []]
+                for p in range(count):
+                    cosine = weights[at, p : p + 1, :]
+                    sine = weights[at, count + p : count + p + 1, :]
+                    right[0].append(halves(cosine * real + sine * imag))
+                    right[1].append(halves(cosine * imag - sine * real))
+                right = jnp.concatenate(
+                    [
+                        jnp.concatenate([h for h, _ in r] + [l for _, l in r], axis=0)
+                        for r in right
+                    ],
+                    axis=1,
+                )
                 col = (z * 3 + a) * 2 * LANES
-                lefts = left[t, :, col : col + 2 * LANES]
-                main = main + lax.dot_general(lefts, high, NT_DIMS, preferred_element_type=F32)
-                rest = rest + lax.dot_general(
-                    lefts[:left_rows], low, NT_DIMS, preferred_element_type=F32
+                parts = parts + lax.dot_general(
+                    left[t, :, col : col + 2 * LANES],
+                    right,
+                    NT_DIMS,
+                    preferred_element_type=F32,
                 )
-        total = main[:left_rows] + main[left_rows:] + rest
+        total = (parts[:left_rows, :columns] + parts[left_rows:, columns:]) + (
+            parts[left_rows:, :columns] + parts[:left_rows, columns:]
+        )
         for slot, piece in enumerate(pieces):
-            plain = total[slot * rows : slot * rows + vectors]
-            turned = total[slot * rows + vectors : (slot + 1) * rows]
-            piece[t, 0] = plain[:, :half] + turned[:, half:]
-            piece[t, 1] = turned[:, :half] - plain[:, half:]
+            for ri in range(2):
+                top = slot * rows + ri * vectors
+                piece[t, ri] = total[top : top + vectors]
 
 
 def spread_kernel(dirac16, kept, arrived, out, partial, wide):
@@ -456,23 +456,23 @@
     def rows_of(n, dtype=BF16):
         return jax.ShapeDtypeStruct((n, LANES), dtype)
 
-    far_out, side_out, packed, fat_v, long_v = call(
+    far_out, packed = call(
         functools.partial(gather_kernel, vectors),
-        [rows_of(size + 32), rows_of(size + 16), rows_of(size), rows_of(link_rows), rows_of(link_rows)],
-        [HB] * 4,
+        [rows_of(size + 16), rows_of(size)],
+        [HB] * 2,
         [
             pltpu.SMEM(chosen.shape, jnp.int32),
             pltpu.VMEM(store.shape, BF16),
             pltpu.VMEM(store.shape, F32),
             pltpu.VMEM((size, LANES), F32),
-            pltpu.SemaphoreType.DMA((4,)),
+            pltpu.SemaphoreType.DMA((2,)),
         ],
         1000,
-    )(*map(pinned, (chosen, store, fat, long)))
+    )(pinned(chosen), pinned(store))
     near = [(i, i ^ 1) for i in range(n_ta)]
     far = [((i + 1) % n_ta, ((i ^ 1) + 1) % n_ta) for i in range(n_ta)]
     far_field = lax.ppermute(far_out, "ta", far)
-    before_z, after_z = exchange(side_out, "gz")
+    before_z, after_z = exchange(packed, "gz")
     near_field = lax.ppermute(packed, "ta", near)
     y_field, _ = exchange(packed, "gy")
 
@@ -491,15 +491,17 @@
             rows_of(link_rows, F32),
             rows_of(link_rows, F32),
         ],
-        [HB] + [VM] * 4,
+        [HB] * 3 + [VM] * 2,
         [
             pltpu.SMEM((3, count), jnp.int32),
+            pltpu.VMEM((link_rows, LANES), BF16),
+            pltpu.VMEM((link_rows, LANES), BF16),
             pltpu.VMEM((2, LANES, 4 * LANES), BF16),
             pltpu.VMEM((2 * LANES, 4 * LANES), BF16),
-            pltpu.SemaphoreType.DMA,
+            pltpu.SemaphoreType.DMA((3,)),
         ],
         1000,
-    )(pinned(momenta.T), packed, y_field, fat_v, long_v)
+    )(pinned(momenta.T), pinned(fat), pinned(long), packed, y_field)
     dacc, left = call(
         functools.partial(side_kernel, times, depth, vectors, rotate),
         [

time: 26.6 us -> 25.9 us (0.974)
  waiting for transfers between devices: 8.14 us -> 7.02 us
  Pallas kernels: 9.37 us -> 9.74 us
    pallas_call x1, Pallas kernels: 2.68 us -> 3.74 us  [on_device(): call(functools.partial(local_kernel, times, depth, vectors, (total_y, tot...]
    ppermute x1, waiting for transfers between devices: 2.25 us -> 1.3 us  [on_device(): near_field = lax.ppermute(packed, 'ta', near)]
    pallas_call x1, Pallas kernels: 2.54 us -> 1.89 us  [on_device(): call(functools.partial(last_kernel, times, depth, vectors), [jax.ShapeDty...]
  transfers between devices with their start and end apart: 6 -> 6, of which waited for: 5 -> 4; matrix products, arithmetic and copies ran while one was open for 0% -> 0% of each run, Pallas kernels for 17% -> 22%
where the time goes in v3:
time: 25.9 us; the launch traced here: 25.7 us
  Pallas kernels  9.74 us (38%)
  starting transfers between devices  8.24 us (32%)
  waiting for transfers between devices  7.02 us (27%)
  between operations  0.68 us (3%)
    ppermute x1, starting transfers between devices, on_device(): far_field = lax.ppermute(far_out, 'ta', far)  5.11 us
    pallas_call x1, Pallas kernels, on_device(): call(functools.partial(local_kernel, times, depth, vectors, (total_y, tot...  3.74 us
    ppermute x2, waiting for transfers between devices, exchange(): before = lax.ppermute(value, axis, up)  2.59 us
    pallas_call x1, Pallas kernels, on_device(): call(functools.partial(last_kernel, times, depth, vectors), [jax.ShapeDty...  1.89 us
    ppermute x1, waiting for transfers between devices, on_device(): other = lax.ppermute(pieces[2] + got[1], 'gz', swap)  1.84 us
    ppermute x1, starting transfers between devices, on_device(): other = lax.ppermute(pieces[2] + got[1], 'gz', swap)  1.56 us
    ppermute x2, starting transfers between devices, exchange(): before = lax.ppermute(value, axis, up)  1.49 us
    ppermute x1, waiting for transfers between devices, on_device(): near_field = lax.ppermute(packed, 'ta', near)  1.3 us
  transfers between devices with their start and end apart: 6, of which 4 were waited for; matrix products, arithmetic and copies ran while one was open for 0% of the time, Pallas kernels for 22%

profile of v3, /device:TPU:0, one launch (start us, length us, event | category | flops | bytes accessed | tf_op | source)
XLA Modules:
  0.0 25.7 jit_solution(17362698738461702780)
XLA Ops:
  0.6 1.3 %shard_map.86 = (bf16[880,128]{1,0:T(8,128)(2,1)S(1)}, bf16[864,128]{1,0:T(8,128)(2,1)S(1)}) custom-call(s32[16]{0:T(128)} %chosen_hbm.1, bf16[1080,128]{1,0:T(8,128)(2,1)} %bitcast.27), custom_call_target="tpu_custom_call" | custom-call | flops 1000 | bytes 1000 | tf_op jit(solution)/shard_map/pallas_call | solution.py:459
  1.9 5.1 %collective-permute-start = (bf16[880,128]{1,0:T(8,128)(2,1)S(1)}, bf16[880,128]{1,0:T(8,128)(2,1)S(1)}, u32[]{:S(2)}, u32[]{:S(2)}) collective-permute-start(bf16[880,128]{1,0:T(8,128)(2,1)S(1)} %get-tuple-element.18), channel_id=1, source_target_pairs={{4,8},{8,4},{12,0},{0,12},{5,9},{9,5},{13,1},{1,13},{6,10},{10,6},... | collective-permute-start | bytes 675848 | tf_op jit(solution)/shard_map/ppermute | solution.py:474
  7.0 0.0 collective-permute-start.2
  7.0 1.5 %collective-permute-start.1 = (bf16[864,128]{1,0:T(8,128)(2,1)S(1)}, bf16[864,128]{1,0:T(8,128)(2,1)S(1)}, u32[]{:S(2)}, u32[]{:S(2)}) collective-permute-start(bf16[864,128]{1,0:T(8,128)(2,1)S(1)} %get-tuple-element.19.field_ref), channel_id=1, source_target_pairs={{0,2},{2,0},{1,3},{3,1},{4,6},{6,4},{5,7},{7,5},{8,10},{10,8},{9,1... | collective-permute-start | bytes 663560 | tf_op jit(solution)/shard_map/ppermute | solution.py:435
  8.5 0.0 collective-permute-start.3
  8.5 0.0 collective-permute-done.2.y_ref
  8.5 3.7 %shard_map.87 = (f32[3,3,3,2,16,128]{5,4,3,2,1,0:T(8,128)S(1)}, f32[2,3,3,3,2,16,128]{6,5,4,3,2,1,0:T(8,128)S(1)}, f32[9,16,128]{2,1,0:T(8,128)S(1)}, f32[1296,128]{1,0:T(8,128)S(1)}, f32[1296,128]{1,0:T(8,128)S(1)}) custom-call(s32[3,8]{1,0:T(4,128)} %bitcast.28, bf16[1296,128]{1,0:T(8,128)(2,1)} %bitcast.25, bf16[1296,128]{1,0:T(8,128)(2,1)} %bitcast.26, ...), custom_call_target="tpu_custom_call" | custom-call | flops 1000 | bytes 1000 | tf_op jit(solution)/shard_map/pallas_call | solution.py:485
  12.3 2.6 %collective-permute-done.1.before_ref.after_ref = bf16[864,128]{1,0:T(8,128)(2,1)S(1)} collective-permute-done((bf16[864,128]{1,0:T(8,128)(2,1)S(1)}, bf16[864,128]{1,0:T(8,128)(2,1)S(1)}, u32[]{:S(2)}, u32[]{:S(2)}) %collective-permute-start.1) | collective-permute-done | bytes 221216 | tf_op jit(solution)/shard_map/ppermute | solution.py:435
  14.8 1.2 %shard_map.88 = (f32[3,3,3,2,16,128]{5,4,3,2,1,0:T(8,128)S(1)}, bf16[3,256,2304]{2,1,0:T(8,128)(2,1)S(1)}) custom-call(s32[4]{0:T(128)} %dirs_hbm.1, s32[4]{0:T(128)} %masks_hbm.1, bf16[864,128]{1,0:T(8,128)(2,1)S(1)} %get-tuple-element.19.field_ref, bf16[864,128]{1,0:T(8,128)(2,1)S(1)} %collective-permute-done.1.before_ref.after_ref, ...), custom_call_target="tpu_custom_call" | custom-call | flops 1000 | bytes 1000 | tf_op jit(solution)/shard_map/pallas_call | solution.py:505
  16.1 1.3 %collective-permute-done.3.near_ref = bf16[864,128]{1,0:T(8,128)(2,1)S(1)} collective-permute-done((bf16[864,128]{1,0:T(8,128)(2,1)S(1)}, bf16[864,128]{1,0:T(8,128)(2,1)S(1)}, u32[]{:S(2)}, u32[]{:S(2)}) %collective-permute-start.3) | collective-permute-done | bytes 221216 | tf_op jit(solution)/shard_map/ppermute | solution.py:476
  17.4 0.0 collective-permute-done.far_ref
  17.4 1.9 %shard_map.89 = (bf16[3,3,3,2,16,128]{5,4,3,2,1,0:T(8,128)(2,1)S(1)}, f32[3,2,16,128]{3,2,1,0:T(8,128)S(1)}, f32[3,2,16,128]{3,2,1,0:T(8,128)S(1)}, f32[3,2,16,128]{3,2,1,0:T(8,128)S(1)}, f32[3,2,16,128]{3,2,1,0:T(8,128)S(1)}) custom-call(bf16[880,128]{1,0:T(8,128)(2,1)S(1)} %collective-permute-done.far_ref, ...), custom_call_target="tpu_custom_call" | custom-call | flops 1000 | bytes 1000 | tf_op jit(solution)/shard_map/pallas_call | solution.py:523
  19.3 0.1 collective-permute-start.4
  19.4 1.3 %collective-permute-done.4 = f32[2,3,2,16,128]{4,3,2,1,0:T(8,128)S(1)} collective-permute-done((f32[2,3,2,16,128]{4,3,2,1,0:T(8,128)S(1)}, f32[2,3,2,16,128]{4,3,2,1,0:T(8,128)S(1)}, u32[]{:S(2)}, u32[]{:S(2)}) %collective-permute-start.4) | collective-permute-done | bytes 98336 | tf_op jit(solution)/shard_map/ppermute | solution.py:536
  20.7 1.6 %collective-permute-start.5 = (f32[3,2,16,128]{3,2,1,0:T(8,128)S(1)}, f32[3,2,16,128]{3,2,1,0:T(8,128)S(1)}, u32[]{:S(2)}, u32[]{:S(2)}) collective-permute-start(f32[3,2,16,128]{3,2,1,0:T(8,128)S(1)} %fusion), channel_id=1, source_target_pairs={{0,2},{2,0},{1,3},{3,1},{4,6},{6,4},{5,7},{7,5},{8,10},{10,8},{9,1... | collective-permute-start | bytes 147464 | tf_op jit(solution)/shard_map/ppermute | solution.py:537
  22.2 0.7 %shard_map.90 = (bf16[864,128]{1,0:T(8,128)(2,1)}, f32[3,2,16,128]{3,2,1,0:T(8,128)S(1)}) custom-call(bf16[54,16,128]{2,1,0:T(8,128)(2,1)S(1)} %bitcast.22, f32[3,2,16,128]{3,2,1,0:T(8,128)S(1)} %get-tuple-element.28.kept, f32[3,2,16,128]{3,2,1,0:T(8,128)S(1)} %slice_bitcast_fusion.1.arrived), custom_call_target="tpu_custom_call" | custom-call | flops 1000 | bytes 1000 | tf_op jit(solution)/shard_map/pallas_call | solution.py:538
  23.0 1.8 %collective-permute-done.5.other = f32[3,2,16,128]{3,2,1,0:T(8,128)S(1)} collective-permute-done((f32[3,2,16,128]{3,2,1,0:T(8,128)S(1)}, f32[3,2,16,128]{3,2,1,0:T(8,128)S(1)}, u32[]{:S(2)}, u32[]{:S(2)}) %collective-permute-start.5) | collective-permute-done | bytes 49184 | tf_op jit(solution)/shard_map/ppermute | solution.py:537
  24.8 0.9 %shard_map.91 = f32[8,3,2,16,16]{4,3,2,1,0:T(8,128)} custom-call(f32[3,2,16,128]{3,2,1,0:T(8,128)S(1)} %get-tuple-element.32.partial, f32[3,2,16,128]{3,2,1,0:T(8,128)S(1)} %collective-permute-done.5.other), custom_call_target="tpu_custom_call" | custom-call | flops 1000 | bytes 1000 | tf_op jit(solution)/shard_map/pallas_call | solution.py:542
  (3 shorter events, 0.0 us)
Async XLA Ops:
  1.9 15.5 %collective-permute-start = (bf16[880,128]{1,0:T(8,128)(2,1)S(1)}, bf16[880,128]{1,0:T(8,128)(2,1)S(1)}, u32[]{:S(2)}, u32[]{:S(2)}) collective-permute-start(bf16[880,128]{1,0:T(8,128)(2,1)S(1)} %get-tuple-element.18), channel_id=1, source_target_pairs={{4,8},{8,4},{12,0},{0,12},{5,9},{9,5},{13,1},{1,13},{6,10},{10,6},... | collective-permute-start | bytes 675848 | tf_op jit(solution)/shard_map/ppermute | solution.py:474
  7.0 1.5 %collective-permute-start.2 = (bf16[864,128]{1,0:T(8,128)(2,1)S(1)}, bf16[864,128]{1,0:T(8,128)(2,1)S(1)}, u32[]{:S(2)}, u32[]{:S(2)}) collective-permute-start(bf16[864,128]{1,0:T(8,128)(2,1)S(1)} %get-tuple-element.19.field_ref), channel_id=1, source_target_pairs={{0,1},{1,0},{2,3},{3,2},{4,5},{5,4},{6,7},{7,6},{8,9},{9,8},{10,11... | collective-permute-start | bytes 663560 | tf_op jit(solution)/shard_map/ppermute | solution.py:435
  7.0 7.8 %collective-permute-start.1 = (bf16[864,128]{1,0:T(8,128)(2,1)S(1)}, bf16[864,128]{1,0:T(8,128)(2,1)S(1)}, u32[]{:S(2)}, u32[]{:S(2)}) collective-permute-start(bf16[864,128]{1,0:T(8,128)(2,1)S(1)} %get-tuple-element.19.field_ref), channel_id=1, source_target_pairs={{0,2},{2,0},{1,3},{3,1},{4,6},{6,4},{5,7},{7,5},{8,10},{10,8},{9,1... | collective-permute-start | bytes 663560 | tf_op jit(solution)/shard_map/ppermute | solution.py:435
  8.5 8.9 %collective-permute-start.3 = (bf16[864,128]{1,0:T(8,128)(2,1)S(1)}, bf16[864,128]{1,0:T(8,128)(2,1)S(1)}, u32[]{:S(2)}, u32[]{:S(2)}) collective-permute-start(bf16[864,128]{1,0:T(8,128)(2,1)S(1)} %get-tuple-element.19.field_ref), channel_id=1, source_target_pairs={{0,4},{4,0},{8,12},{12,8},{1,5},{5,1},{9,13},{13,9},{2,6},{6,2},{1... | collective-permute-start | bytes 663560 | tf_op jit(solution)/shard_map/ppermute | solution.py:476
  19.3 1.4 %collective-permute-start.4 = (f32[2,3,2,16,128]{4,3,2,1,0:T(8,128)S(1)}, f32[2,3,2,16,128]{4,3,2,1,0:T(8,128)S(1)}, u32[]{:S(2)}, u32[]{:S(2)}) collective-permute-start(f32[2,3,2,16,128]{4,3,2,1,0:T(8,128)S(1)} %pad_maximum_fusion), channel_id=1, source_target_pairs={{0,1},{1,0},{2,3},{3,2},{4,5},{5,4},{6,7},{7,6},{8,9},{9,8},{10,11... | collective-permute-start | bytes 294920 | tf_op jit(solution)/shard_map/ppermute | solution.py:536
  20.7 4.2 %collective-permute-start.5 = (f32[3,2,16,128]{3,2,1,0:T(8,128)S(1)}, f32[3,2,16,128]{3,2,1,0:T(8,128)S(1)}, u32[]{:S(2)}, u32[]{:S(2)}) collective-permute-start(f32[3,2,16,128]{3,2,1,0:T(8,128)S(1)} %fusion), channel_id=1, source_target_pairs={{0,2},{2,0},{1,3},{3,1},{4,6},{6,4},{5,7},{7,5},{8,10},{10,8},{9,1... | collective-permute-start | bytes 147464 | tf_op jit(solution)/shard_map/ppermute | solution.py:537

commit v4 on v3

--- a/solution.py
+++ b/solution.py
@@ -34,18 +34,33 @@
     )
 
 
-def gather_kernel(vectors, chosen_hbm, store_hbm, far, out, chosen, store, wide, turned, sems):
-    copies = [
-        pltpu.make_async_copy(chosen_hbm, chosen, sems.at[0]),
-        pltpu.make_async_copy(store_hbm, store, sems.at[1]),
+PIECES = 5
+
+
+def gather_kernel(
+    vectors, chosen_hbm, store_hbm, fat_hbm, long_hbm,
+    far, out, fat, long,
+    chosen, store, wide, turned, sems,
+):
+    piece = store.shape[0] // PIECES
+    first = pltpu.make_async_copy(chosen_hbm, chosen, sems.at[PIECES])
+    first.start()
+    copies = []
+    for i in range(PIECES):
+        part = pl.ds(i * piece, piece)
+        copies.append(pltpu.make_async_copy(store_hbm.at[part], store.at[part], sems.at[i]))
+    later = [
+        pltpu.make_async_copy(fat_hbm, fat, sems.at[PIECES + 1]),
+        pltpu.make_async_copy(long_hbm, long, sems.at[PIECES + 2]),
     ]
-    for copy in copies:
+    for copy in copies + later:
         copy.start()
-    for copy in copies:
+    for i, copy in enumerate(copies):
         copy.wait()
+        wide[i * piece : (i + 1) * piece, :] = store[i * piece : (i + 1) * piece, :].astype(F32)
+    first.wait()
     size = out.shape[0]
     rows = size // vectors
-    wide[...] = store[...].astype(F32)
     full = rows // 8
     rest = rows - 8 * full
     for n in range(vectors):
@@ -63,6 +78,8 @@
         out[r : r + 16, :] = block
         far[r : r + 16, :] = block
     far[size:, :] = jnp.zeros((far.shape[0] - size, LANES), BF16)
+    for copy in later:
+        copy.wait()
 
 
 class Links:
@@ -174,18 +191,13 @@
 
 def local_kernel(
     times, depth, vectors, sizes,
-    momenta_hbm, fat_hbm, long_hbm, field_ref, y_ref,
+    momenta_hbm, fat, long, field_ref, y_ref,
     dacc, back_xy, weights, fatf, longf,
-    momenta, fat, long, x_perm, y_perm, sems,
+    momenta, x_perm, y_perm, sem,
 ):
     total_y, total_z, scale = sizes
-    copies = [
-        pltpu.make_async_copy(fat_hbm, fat, sems.at[0]),
-        pltpu.make_async_copy(long_hbm, long, sems.at[1]),
-        pltpu.make_async_copy(momenta_hbm, momenta, sems.at[2]),
-    ]
-    for copy in copies:
-        copy.start()
+    copy = pltpu.make_async_copy(momenta_hbm, momenta, sem)
+    copy.start()
     fat_l, long_l = Links(fatf, times, depth), Links(longf, times, depth)
     field = Field(field_ref, times, depth, vectors)
     y_field = Field(y_ref, times, depth, vectors)
@@ -193,8 +205,6 @@
     for e in range(2):
         x_perm[e] = x_permutation(origin + e)
     y_perm[...] = y_permutation()
-    for copy in copies:
-        copy.wait()
     fatf[...] = fat[...].astype(F32)
     longf[...] = long[...].astype(F32)
     for t in range(times):
@@ -226,6 +236,7 @@
             if z + 1 < depth:
                 add_hop(acc, fat_l, 0, 1, t, z, field.read(t, z + 1), False)
             write(dacc, t, z, acc)
+    copy.wait()
     count = momenta.shape[1]
     lane = lax.broadcasted_iota(jnp.int32, (count, LANES), 1)
     sub = lax.broadcasted_iota(jnp.int32, (count, LANES), 0)
@@ -342,22 +353,32 @@
 NT_DIMS = (((1,), (1,)), ((), ()))
 
 
-def last_kernel(
-    times, depth, vectors,
-    far_ref, dacc, near_ref, fatf, longf, weights, left,
-    dirac16, *pieces,
-):
-    fat_l, long_l = Links(fatf, times, depth), Links(longf, times, depth)
-    near = Field(near_ref, times, depth, vectors)
-    far = Field(far_ref, times, depth, vectors)
+def block_hops(acc, links, field, times, t, z, ahead):
+    fat_l, long_l = links
+    w = 0 if ahead else 1
+    add_hop(acc, long_l, w, 0, t, z, field.read(t, z), not ahead)
+    if ahead and t + 1 == times:
+        add_hop(acc, fat_l, 0, 0, t, z, field.read(0, z), False)
+    if not ahead and t == 0:
+        add_hop(acc, fat_l, 1, 0, t, z, field.read(times - 1, z), True)
+
+
+def time_kernel(times, depth, vectors, near, block_ref, fatf, longf, dacc_in, dacc):
+    links = Links(fatf, times, depth), Links(longf, times, depth)
+    block = Field(block_ref, times, depth, vectors)
     even = lax.axis_index("ta") % 2 == 0
-
-    def pick(first, second, t, z):
-        return [
-            [jnp.where(even, f, s) for f, s in zip(x, y)]
-            for x, y in zip(first.raw(t, z), second.raw(t, z))
-        ]
-
+    for ahead in (True, False):
+
+        @pl.when(even if ahead == near else jnp.logical_not(even))
+        def _(ahead=ahead):
+            for t in range(times):
+                for z in range(depth):
+                    acc = read(dacc_in, t, z)
+                    block_hops(acc, links, block, times, t, z, ahead)
+                    write(dacc, t, z, acc)
+
+
+def meson_kernel(times, depth, vectors, dacc, weights, left, dirac16, *pieces):
     rows = 2 * vectors
     left_rows = left.shape[1] // 2
     count = weights.shape[1] // 2
@@ -366,12 +387,6 @@
         parts = jnp.zeros((2 * left_rows, 2 * columns), F32)
         for z in range(depth):
             acc = read(dacc, t, z)
-            add_hop(acc, long_l, 0, 0, t, z, widen(pick(near, far, t, z)), False)
-            add_hop(acc, long_l, 1, 0, t, z, widen(pick(far, near, t, z)), True)
-            if t + 1 == times:
-                add_hop(acc, fat_l, 0, 0, t, z, widen(pick(near, far, 0, z)), False)
-            if t == 0:
-                add_hop(acc, fat_l, 1, 0, t, z, widen(pick(far, near, times - 1, z)), True)
             write(dirac16, t, z, acc)
             at = t * depth + z
             for a in range(3):
@@ -456,19 +471,19 @@
     def rows_of(n, dtype=BF16):
         return jax.ShapeDtypeStruct((n, LANES), dtype)
 
-    far_out, packed = call(
+    far_out, packed, fat_v, long_v = call(
         functools.partial(gather_kernel, vectors),
-        [rows_of(size + 16), rows_of(size)],
-        [HB] * 2,
+        [rows_of(size + 8), rows_of(size), rows_of(link_rows), rows_of(link_rows)],
+        [HB] * 4,
         [
             pltpu.SMEM(chosen.shape, jnp.int32),
             pltpu.VMEM(store.shape, BF16),
             pltpu.VMEM(store.shape, F32),
             pltpu.VMEM((size, LANES), F32),
-            pltpu.SemaphoreType.DMA((2,)),
+            pltpu.SemaphoreType.DMA((PIECES + 3,)),
         ],
-        1000,
-    )(pinned(chosen), pinned(store))
+        1,
+    )(*map(pinned, (chosen, store, fat, long)))
     near = [(i, i ^ 1) for i in range(n_ta)]
     far = [((i + 1) % n_ta, ((i ^ 1) + 1) % n_ta) for i in range(n_ta)]
     far_field = lax.ppermute(far_out, "ta", far)
@@ -491,17 +506,15 @@
             rows_of(link_rows, F32),
             rows_of(link_rows, F32),
         ],
-        [HB] * 3 + [VM] * 2,
+        [HB] + [VM] * 4,
         [
             pltpu.SMEM((3, count), jnp.int32),
-            pltpu.VMEM((link_rows, LANES), BF16),
-            pltpu.VMEM((link_rows, LANES), BF16),
             pltpu.VMEM((2, LANES, 4 * LANES), BF16),
             pltpu.VMEM((2 * LANES, 4 * LANES), BF16),
-            pltpu.SemaphoreType.DMA((3,)),
+            pltpu.SemaphoreType.DMA,
         ],
-        1000,
-    )(pinned(momenta.T), pinned(fat), pinned(long), packed, y_field)
+        1,
+    )(pinned(momenta.T), fat_v, long_v, packed, y_field)
     dacc, left = call(
         functools.partial(side_kernel, times, depth, vectors, rotate),
         [
@@ -515,18 +528,26 @@
             pltpu.VMEM((3,) + shape6, F32),
             pltpu.SemaphoreType.DMA((2,)),
         ],
-        1000,
+        1,
     )(
         pinned(current_dirs), pinned(taste_masks), packed, before_z, after_z, fatf, longf, dacc, back_xy
     )
     piece = jax.ShapeDtypeStruct((times, 2, vectors, count * vectors), F32)
+    for block, is_near in ((near_field, True), (far_field, False)):
+        (dacc,) = call(
+            functools.partial(time_kernel, times, depth, vectors, is_near),
+            [jax.ShapeDtypeStruct(shape6, F32)],
+            [VM] * 4,
+            [],
+            1000,
+        )(block, fatf, longf, dacc)
     dirac16, *pieces = call(
-        functools.partial(last_kernel, times, depth, vectors),
+        functools.partial(meson_kernel, times, depth, vectors),
         [jax.ShapeDtypeStruct(shape6, BF16)] + [piece] * slots,
-        [VM] * 7,
+        [VM] * 3,
         [],
-        1000,
-    )(far_field, dacc, near_field, fatf, longf, weights, left)
+        1,
+    )(dacc, weights, left)
 
     odd_shape = rows_of(size)
     turned = dirac16.reshape(per_vector, vectors, LANES)
@@ -536,12 +557,12 @@
         got = lax.ppermute(jnp.stack([pieces[1], pieces[3]]), "gy", swap)
         other = lax.ppermute(pieces[2] + got[1], "gz", swap)
         odd_rows, partial = call(
-            spread_kernel, [odd_shape, piece], [VM] * 3, scratch, 1000
+            spread_kernel, [odd_shape, piece], [VM] * 3, scratch, 1
         )(turned, pieces[0], got[0])
         meson_shape = jax.ShapeDtypeStruct((count, times, 2, vectors, vectors), F32)
-        (meson_fields,) = call(final_kernel, [meson_shape], [VM] * 2, [], 1000)(partial, other)
+        (meson_fields,) = call(final_kernel, [meson_shape], [VM] * 2, [], 1)(partial, other)
     else:
-        (odd_rows,) = call(turn_kernel, [odd_shape], [VM], scratch, 1000)(turned)
+        (odd_rows,) = call(turn_kernel, [odd_shape], [VM], scratch, 1)(turned)
         whole = jnp.stack(pieces).reshape(slots, times, 2, vectors, count, vectors)
         whole = whole.transpose(0, 4, 1, 2, 3, 5).reshape(
             slots * count, times, 2, vectors, vectors

time: 25.9 us -> 25.8 us (level)
  Pallas kernels: 9.74 us -> 8.61 us
  waiting for transfers between devices: 7.02 us -> 8.04 us
    pallas_call x1, Pallas kernels: 3.74 us -> 2.68 us  [on_device(): call(functools.partial(local_kernel, times, depth, vectors, (total_y, tot...]
    ppermute x2, waiting for transfers between devices: 2.59 us -> 3.65 us  [exchange(): before = lax.ppermute(value, axis, up)]
    pallas_call x4 -> x6, Pallas kernels: 4.79 us -> 4.72 us  [the longest x1 1.3 us: on_device(): call(functools.partial(gather_kernel, vectors), [rows_of(size + 8), rows_...]
  transfers between devices with their start and end apart: 6 -> 6, of which waited for: 4 -> 4; matrix products, arithmetic and copies ran while one was open for 0% -> 0% of each run, Pallas kernels for 22% -> 19%
where the time goes in v4:
time: 25.8 us; the launch traced here: 25.6 us
  Pallas kernels  8.61 us (33%)
  starting transfers between devices  8.24 us (32%)
  waiting for transfers between devices  8.04 us (31%)
  between operations  0.7 us (3%)
    ppermute x1, starting transfers between devices, on_device(): far_field = lax.ppermute(far_out, 'ta', far)  5.11 us
    ppermute x2, waiting for transfers between devices, exchange(): before = lax.ppermute(value, axis, up)  3.65 us
    pallas_call x1, Pallas kernels, on_device(): call(functools.partial(local_kernel, times, depth, vectors, (total_y, tot...  2.68 us
    ppermute x1, waiting for transfers between devices, on_device(): other = lax.ppermute(pieces[2] + got[1], 'gz', swap)  1.85 us
    ppermute x1, starting transfers between devices, on_device(): other = lax.ppermute(pieces[2] + got[1], 'gz', swap)  1.56 us
    ppermute x2, starting transfers between devices, exchange(): before = lax.ppermute(value, axis, up)  1.49 us
    pallas_call x1, Pallas kernels, on_device(): call(functools.partial(gather_kernel, vectors), [rows_of(size + 8), rows_...  1.3 us
    ppermute x1, waiting for transfers between devices, on_device(): got = lax.ppermute(jnp.stack([pieces[1], pieces[3]]), 'gy', swap)  1.29 us
  transfers between devices with their start and end apart: 6, of which 4 were waited for; matrix products, arithmetic and copies ran while one was open for 0% of the time, Pallas kernels for 19%

profile of v4, /device:TPU:0, one launch (start us, length us, event | category | flops | bytes accessed | tf_op | source)
XLA Modules:
  0.0 25.6 jit_solution(17640475382817245739)
XLA Ops:
  0.6 1.3 %shard_map.86 = (bf16[872,128]{1,0:T(8,128)(2,1)S(1)}, bf16[864,128]{1,0:T(8,128)(2,1)S(1)}, bf16[1296,128]{1,0:T(8,128)(2,1)S(1)}, bf16[1296,128]{1,0:T(8,128)(2,1)S(1)}) custom-call(s32[16]{0:T(128)} %chosen_hbm.1, bf16[1080,128]{1,0:T(8,128)(2,1)} %bitcast.27, bf16[1296,128]{1,0:T(8,128)(2,1)} %bitcast.25, bf16[1296,128]{1,0:T(8,128)(2,1)} %bitcast.26), custom_call_target="tpu_custom_call" | custom-call | flops 1 | bytes 1 | tf_op jit(solution)/shard_map/pallas_call | solution.py:474
  1.9 5.1 %collective-permute-start = (bf16[872,128]{1,0:T(8,128)(2,1)S(1)}, bf16[872,128]{1,0:T(8,128)(2,1)S(1)}, u32[]{:S(2)}, u32[]{:S(2)}) collective-permute-start(bf16[872,128]{1,0:T(8,128)(2,1)S(1)} %get-tuple-element.20), channel_id=1, source_target_pairs={{4,8},{8,4},{12,0},{0,12},{5,9},{9,5},{13,1},{1,13},{6,10},{10,6},... | collective-permute-start | bytes 669704 | tf_op jit(solution)/shard_map/ppermute | solution.py:489
  7.1 0.0 collective-permute-start.1
  7.1 1.5 %collective-permute-start.3 = (bf16[864,128]{1,0:T(8,128)(2,1)S(1)}, bf16[864,128]{1,0:T(8,128)(2,1)S(1)}, u32[]{:S(2)}, u32[]{:S(2)}) collective-permute-start(bf16[864,128]{1,0:T(8,128)(2,1)S(1)} %get-tuple-element.23.field_ref), channel_id=1, source_target_pairs={{0,2},{2,0},{1,3},{3,1},{4,6},{6,4},{5,7},{7,5},{8,10},{10,8},{9,1... | collective-permute-start | bytes 663560 | tf_op jit(solution)/shard_map/ppermute | solution.py:450
  8.5 0.0 collective-permute-start.2
  8.6 0.0 collective-permute-done.1.y_ref
  8.6 2.7 %shard_map.87 = (f32[3,3,3,2,16,128]{5,4,3,2,1,0:T(8,128)S(1)}, f32[2,3,3,3,2,16,128]{6,5,4,3,2,1,0:T(8,128)S(1)}, f32[9,16,128]{2,1,0:T(8,128)S(1)}, f32[1296,128]{1,0:T(8,128)S(1)}, f32[1296,128]{1,0:T(8,128)S(1)}) custom-call(s32[3,8]{1,0:T(4,128)} %bitcast.28, bf16[1296,128]{1,0:T(8,128)(2,1)S(1)} %get-tuple-element.21.fat, ...), custom_call_target="tpu_custom_call" | custom-call | flops 1 | bytes 1 | tf_op jit(solution)/shard_map/pallas_call | solution.py:500
  11.2 3.7 %collective-permute-done.3.before_ref.after_ref = bf16[864,128]{1,0:T(8,128)(2,1)S(1)} collective-permute-done((bf16[864,128]{1,0:T(8,128)(2,1)S(1)}, bf16[864,128]{1,0:T(8,128)(2,1)S(1)}, u32[]{:S(2)}, u32[]{:S(2)}) %collective-permute-start.3) | collective-permute-done | bytes 221216 | tf_op jit(solution)/shard_map/ppermute | solution.py:450
  14.9 1.2 %shard_map.88 = (f32[3,3,3,2,16,128]{5,4,3,2,1,0:T(8,128)S(1)}, bf16[3,256,2304]{2,1,0:T(8,128)(2,1)S(1)}) custom-call(s32[4]{0:T(128)} %dirs_hbm.1, s32[4]{0:T(128)} %masks_hbm.1, bf16[864,128]{1,0:T(8,128)(2,1)S(1)} %get-tuple-element.23.field_ref, bf16[864,128]{1,0:T(8,128)(2,1)S(1)} %collective-permute-done.3.before_ref.after_ref, ...), custom_call_target="tpu_custom_call" | custom-call | flops 1 | bytes 1 | tf_op jit(solution)/shard_map/pallas_call | solution.py:518
  16.1 1.3 %collective-permute-done.2.block_ref = bf16[864,128]{1,0:T(8,128)(2,1)S(1)} collective-permute-done((bf16[864,128]{1,0:T(8,128)(2,1)S(1)}, bf16[864,128]{1,0:T(8,128)(2,1)S(1)}, u32[]{:S(2)}, u32[]{:S(2)}) %collective-permute-start.2) | collective-permute-done | bytes 221216 | tf_op jit(solution)/shard_map/ppermute | solution.py:491
  17.4 0.3 %shard_map.89.dacc_in = f32[3,3,3,2,16,128]{5,4,3,2,1,0:T(8,128)S(1)} custom-call(bf16[864,128]{1,0:T(8,128)(2,1)S(1)} %collective-permute-done.2.block_ref, f32[1296,128]{1,0:T(8,128)S(1)} %get-tuple-element.24.fatf, f32[1296,128]{1,0:T(8,128)S(1)} %get-tuple-element.25.longf, f32[3,3,3,2,16,128]{5,4,3,2,1,0:T(8,128)S(1)} %get-tuple-element.28.dacc_in), custom_call_target="tpu_custom_call" | custom-call | flops 1000 | bytes 1000 | tf_op jit(solution)/shard_map/pallas_call | solution.py:537
  17.6 0.0 collective-permute-done.block_ref
  17.6 0.3 %shard_map.90.dacc = f32[3,3,3,2,16,128]{5,4,3,2,1,0:T(8,128)S(1)} custom-call(bf16[872,128]{1,0:T(8,128)(2,1)S(1)} %collective-permute-done.block_ref, f32[1296,128]{1,0:T(8,128)S(1)} %get-tuple-element.24.fatf, f32[1296,128]{1,0:T(8,128)S(1)} %get-tuple-element.25.longf, f32[3,3,3,2,16,128]{5,4,3,2,1,0:T(8,128)S(1)} %shard_map.89.dacc_in), custom_call_target="tpu_custom_call" | custom-call | flops 1000 | bytes 1000 | tf_op jit(solution)/shard_map/pallas_call | solution.py:537
  17.9 1.2 %shard_map.91 = (bf16[3,3,3,2,16,128]{5,4,3,2,1,0:T(8,128)(2,1)S(1)}, f32[3,2,16,128]{3,2,1,0:T(8,128)S(1)}, f32[3,2,16,128]{3,2,1,0:T(8,128)S(1)}, f32[3,2,16,128]{3,2,1,0:T(8,128)S(1)}, f32[3,2,16,128]{3,2,1,0:T(8,128)S(1)}) custom-call(f32[3,3,3,2,16,128]{5,4,3,2,1,0:T(8,128)S(1)} %shard_map.90.dacc, f32[9,16,128]{2,1,0:T(8,128)S(1)} %get-tuple-element.29.weights, ...), custom_call_target="tpu_custom_call" | custom-call | flops 1 | bytes 1 | tf_op jit(solution)/shard_map/pallas_call | solution.py:544
  19.2 0.1 collective-permute-start.4
  19.3 1.3 %collective-permute-done.4 = f32[2,3,2,16,128]{4,3,2,1,0:T(8,128)S(1)} collective-permute-done((f32[2,3,2,16,128]{4,3,2,1,0:T(8,128)S(1)}, f32[2,3,2,16,128]{4,3,2,1,0:T(8,128)S(1)}, u32[]{:S(2)}, u32[]{:S(2)}) %collective-permute-start.4) | collective-permute-done | bytes 98336 | tf_op jit(solution)/shard_map/ppermute | solution.py:557
  20.6 1.6 %collective-permute-start.5 = (f32[3,2,16,128]{3,2,1,0:T(8,128)S(1)}, f32[3,2,16,128]{3,2,1,0:T(8,128)S(1)}, u32[]{:S(2)}, u32[]{:S(2)}) collective-permute-start(f32[3,2,16,128]{3,2,1,0:T(8,128)S(1)} %fusion), channel_id=1, source_target_pairs={{0,2},{2,0},{1,3},{3,1},{4,6},{6,4},{5,7},{7,5},{8,10},{10,8},{9,1... | collective-permute-start | bytes 147464 | tf_op jit(solution)/shard_map/ppermute | solution.py:558
  22.1 0.7 %shard_map.92 = (bf16[864,128]{1,0:T(8,128)(2,1)}, f32[3,2,16,128]{3,2,1,0:T(8,128)S(1)}) custom-call(bf16[54,16,128]{2,1,0:T(8,128)(2,1)S(1)} %bitcast.22, f32[3,2,16,128]{3,2,1,0:T(8,128)S(1)} %get-tuple-element.32.kept, f32[3,2,16,128]{3,2,1,0:T(8,128)S(1)} %slice_bitcast_fusion.1.arrived), custom_call_target="tpu_custom_call" | custom-call | flops 1 | bytes 1 | tf_op jit(solution)/shard_map/pallas_call | solution.py:559
  22.9 1.8 %collective-permute-done.5.other = f32[3,2,16,128]{3,2,1,0:T(8,128)S(1)} collective-permute-done((f32[3,2,16,128]{3,2,1,0:T(8,128)S(1)}, f32[3,2,16,128]{3,2,1,0:T(8,128)S(1)}, u32[]{:S(2)}, u32[]{:S(2)}) %collective-permute-start.5) | collective-permute-done | bytes 49184 | tf_op jit(solution)/shard_map/ppermute | solution.py:558
  24.7 0.9 %shard_map.93 = f32[8,3,2,16,16]{4,3,2,1,0:T(8,128)} custom-call(f32[3,2,16,128]{3,2,1,0:T(8,128)S(1)} %get-tuple-element.36.partial, f32[3,2,16,128]{3,2,1,0:T(8,128)S(1)} %collective-permute-done.5.other), custom_call_target="tpu_custom_call" | custom-call | flops 1 | bytes 1 | tf_op jit(solution)/shard_map/pallas_call | solution.py:563
  (3 shorter events, 0.0 us)
Async XLA Ops:
  1.9 15.7 %collective-permute-start = (bf16[872,128]{1,0:T(8,128)(2,1)S(1)}, bf16[872,128]{1,0:T(8,128)(2,1)S(1)}, u32[]{:S(2)}, u32[]{:S(2)}) collective-permute-start(bf16[872,128]{1,0:T(8,128)(2,1)S(1)} %get-tuple-element.20), channel_id=1, source_target_pairs={{4,8},{8,4},{12,0},{0,12},{5,9},{9,5},{13,1},{1,13},{6,10},{10,6},... | collective-permute-start | bytes 669704 | tf_op jit(solution)/shard_map/ppermute | solution.py:489
  7.1 1.5 %collective-permute-start.1 = (bf16[864,128]{1,0:T(8,128)(2,1)S(1)}, bf16[864,128]{1,0:T(8,128)(2,1)S(1)}, u32[]{:S(2)}, u32[]{:S(2)}) collective-permute-start(bf16[864,128]{1,0:T(8,128)(2,1)S(1)} %get-tuple-element.23.field_ref), channel_id=1, source_target_pairs={{0,1},{1,0},{2,3},{3,2},{4,5},{5,4},{6,7},{7,6},{8,9},{9,8},{10,11... | collective-permute-start | bytes 663560 | tf_op jit(solution)/shard_map/ppermute | solution.py:450
  7.1 7.8 %collective-permute-start.3 = (bf16[864,128]{1,0:T(8,128)(2,1)S(1)}, bf16[864,128]{1,0:T(8,128)(2,1)S(1)}, u32[]{:S(2)}, u32[]{:S(2)}) collective-permute-start(bf16[864,128]{1,0:T(8,128)(2,1)S(1)} %get-tuple-element.23.field_ref), channel_id=1, source_target_pairs={{0,2},{2,0},{1,3},{3,1},{4,6},{6,4},{5,7},{7,5},{8,10},{10,8},{9,1... | collective-permute-start | bytes 663560 | tf_op jit(solution)/shard_map/ppermute | solution.py:450
  8.5 8.8 %collective-permute-start.2 = (bf16[864,128]{1,0:T(8,128)(2,1)S(1)}, bf16[864,128]{1,0:T(8,128)(2,1)S(1)}, u32[]{:S(2)}, u32[]{:S(2)}) collective-permute-start(bf16[864,128]{1,0:T(8,128)(2,1)S(1)} %get-tuple-element.23.field_ref), channel_id=1, source_target_pairs={{0,4},{4,0},{8,12},{12,8},{1,5},{5,1},{9,13},{13,9},{2,6},{6,2},{1... | collective-permute-start | bytes 663560 | tf_op jit(solution)/shard_map/ppermute | solution.py:491
  19.2 1.4 %collective-permute-start.4 = (f32[2,3,2,16,128]{4,3,2,1,0:T(8,128)S(1)}, f32[2,3,2,16,128]{4,3,2,1,0:T(8,128)S(1)}, u32[]{:S(2)}, u32[]{:S(2)}) collective-permute-start(f32[2,3,2,16,128]{4,3,2,1,0:T(8,128)S(1)} %pad_maximum_fusion), channel_id=1, source_target_pairs={{0,1},{1,0},{2,3},{3,2},{4,5},{5,4},{6,7},{7,6},{8,9},{9,8},{10,11... | collective-permute-start | bytes 294920 | tf_op jit(solution)/shard_map/ppermute | solution.py:557
  20.6 4.2 %collective-permute-start.5 = (f32[3,2,16,128]{3,2,1,0:T(8,128)S(1)}, f32[3,2,16,128]{3,2,1,0:T(8,128)S(1)}, u32[]{:S(2)}, u32[]{:S(2)}) collective-permute-start(f32[3,2,16,128]{3,2,1,0:T(8,128)S(1)} %fusion), channel_id=1, source_target_pairs={{0,2},{2,0},{1,3},{3,1},{4,6},{6,4},{5,7},{7,5},{8,10},{10,8},{9,1... | collective-permute-start | bytes 147464 | tf_op jit(solution)/shard_map/ppermute | solution.py:558

commit v5 on v4

--- a/solution.py
+++ b/solution.py
@@ -39,7 +39,7 @@
 
 def gather_kernel(
     vectors, chosen_hbm, store_hbm, fat_hbm, long_hbm,
-    far, out, fat, long,
+    up, down, out, fat, long,
     chosen, store, wide, turned, sems,
 ):
     piece = store.shape[0] // PIECES
@@ -76,8 +76,10 @@
     for r in range(0, size, 16):
         block = turned[r : r + 16, :].astype(BF16)
         out[r : r + 16, :] = block
-        far[r : r + 16, :] = block
-    far[size:, :] = jnp.zeros((far.shape[0] - size, LANES), BF16)
+        up[r : r + 16, :] = block
+        down[r : r + 16, :] = block
+    for ref in (up, down):
+        ref[size:, :] = jnp.zeros((ref.shape[0] - size, LANES), BF16)
     for copy in later:
         copy.wait()
 
@@ -363,19 +365,14 @@
         add_hop(acc, fat_l, 1, 0, t, z, field.read(times - 1, z), True)
 
 
-def time_kernel(times, depth, vectors, near, block_ref, fatf, longf, dacc_in, dacc):
+def time_kernel(times, depth, vectors, ahead, block_ref, fatf, longf, dacc_in, dacc):
     links = Links(fatf, times, depth), Links(longf, times, depth)
     block = Field(block_ref, times, depth, vectors)
-    even = lax.axis_index("ta") % 2 == 0
-    for ahead in (True, False):
-
-        @pl.when(even if ahead == near else jnp.logical_not(even))
-        def _(ahead=ahead):
-            for t in range(times):
-                for z in range(depth):
-                    acc = read(dacc_in, t, z)
-                    block_hops(acc, links, block, times, t, z, ahead)
-                    write(dacc, t, z, acc)
+    for t in range(times):
+        for z in range(depth):
+            acc = read(dacc_in, t, z)
+            block_hops(acc, links, block, times, t, z, ahead)
+            write(dacc, t, z, acc)
 
 
 def meson_kernel(times, depth, vectors, dacc, weights, left, dirac16, *pieces):
@@ -471,9 +468,12 @@
     def rows_of(n, dtype=BF16):
         return jax.ShapeDtypeStruct((n, LANES), dtype)
 
-    far_out, packed, fat_v, long_v = call(
+    up_out, down_out, packed, fat_v, long_v = call(
         functools.partial(gather_kernel, vectors),
-        [rows_of(size + 8), rows_of(size), rows_of(link_rows), rows_of(link_rows)],
+        [
+            rows_of(size + 16), rows_of(size + 8), rows_of(size),
+            rows_of(link_rows), rows_of(link_rows),
+        ],
         [HB] * 4,
         [
             pltpu.SMEM(chosen.shape, jnp.int32),
@@ -484,11 +484,11 @@
         ],
         1,
     )(*map(pinned, (chosen, store, fat, long)))
-    near = [(i, i ^ 1) for i in range(n_ta)]
-    far = [((i + 1) % n_ta, ((i ^ 1) + 1) % n_ta) for i in range(n_ta)]
-    far_field = lax.ppermute(far_out, "ta", far)
+    up = [(i, (i + 1) % n_ta) for i in range(n_ta)]
+    down = [(j, i) for i, j in up]
+    before_t = lax.ppermute(up_out, "ta", up)
+    after_t = lax.ppermute(down_out, "ta", down)
     before_z, after_z = exchange(packed, "gz")
-    near_field = lax.ppermute(packed, "ta", near)
     y_field, _ = exchange(packed, "gy")
 
     slots = current_dirs.shape[0]
@@ -533,9 +533,9 @@
         pinned(current_dirs), pinned(taste_masks), packed, before_z, after_z, fatf, longf, dacc, back_xy
     )
     piece = jax.ShapeDtypeStruct((times, 2, vectors, count * vectors), F32)
-    for block, is_near in ((near_field, True), (far_field, False)):
+    for block, ahead in ((before_t, False), (after_t, True)):
         (dacc,) = call(
-            functools.partial(time_kernel, times, depth, vectors, is_near),
+            functools.partial(time_kernel, times, depth, vectors, ahead),
             [jax.ShapeDtypeStruct(shape6, F32)],
             [VM] * 4,
             [],

time: 25.8 us -> 24.9 us (0.965)
  waiting for transfers between devices: 8.04 us -> 6.96 us
    ppermute x2, waiting for transfers between devices: 1.25 us -> 0.33 us  [the longest x1 0.33 us: on_device(): after_t = lax.ppermute(down_out, 'ta', down)]
  transfers between devices with their start and end apart: 6 -> 6, of which waited for: 4 -> 4; matrix products, arithmetic and copies ran while one was open for 0% -> 0% of each run, Pallas kernels for 19% -> 20%
where the time goes in v5:
time: 24.9 us; the launch traced here: 24.7 us
  Pallas kernels  8.59 us (34%)
  starting transfers between devices  8.45 us (34%)
  waiting for transfers between devices  6.96 us (28%)
  between operations  0.7 us (3%)
    ppermute x2, waiting for transfers between devices, exchange(): before = lax.ppermute(value, axis, up)  3.5 us
    ppermute x1, starting transfers between devices, on_device(): before_t = lax.ppermute(up_out, 'ta', up)  3.08 us
    pallas_call x1, Pallas kernels, on_device(): call(functools.partial(local_kernel, times, depth, vectors, (total_y, tot...  2.69 us
    ppermute x1, starting transfers between devices, on_device(): after_t = lax.ppermute(down_out, 'ta', down)  2.09 us
    ppermute x1, waiting for transfers between devices, on_device(): other = lax.ppermute(pieces[2] + got[1], 'gz', swap)  1.85 us
    ppermute x2, starting transfers between devices, exchange(): before = lax.ppermute(value, axis, up)  1.65 us
    ppermute x1, starting transfers between devices, on_device(): other = lax.ppermute(pieces[2] + got[1], 'gz', swap)  1.56 us
    pallas_call x1, Pallas kernels, on_device(): call(functools.partial(gather_kernel, vectors), [rows_of(size + 16), rows...  1.3 us
  transfers between devices with their start and end apart: 6, of which 4 were waited for; matrix products, arithmetic and copies ran while one was open for 0% of the time, Pallas kernels for 20%

profile of v5, /device:TPU:0, one launch (start us, length us, event | category | flops | bytes accessed | tf_op | source)
XLA Modules:
  0.0 24.7 jit_solution(15002132589839024797)
XLA Ops:
  0.6 1.3 %shard_map.86 = (bf16[880,128]{1,0:T(8,128)(2,1)S(1)}, bf16[872,128]{1,0:T(8,128)(2,1)S(1)}, bf16[864,128]{1,0:T(8,128)(2,1)S(1)}, bf16[1296,128]{1,0:T(8,128)(2,1)S(1)}, bf16[1296,128]{1,0:T(8,128)(2,1)S(1)}) custom-call(s32[16]{0:T(128)} %chosen_hbm.1, bf16[1080,128]{1,0:T(8,128)(2,1)} %bitcast.27, bf16[1296,128]{1,0:T(8,128)(2,1)} %bitcast.25, ...), custom_call_target="tpu_custom_call" | custom-call | flops 1 | bytes 1 | tf_op jit(solution)/shard_map/pallas_call | solution.py:471
  1.9 3.1 %collective-permute-start.2 = (bf16[880,128]{1,0:T(8,128)(2,1)S(1)}, bf16[880,128]{1,0:T(8,128)(2,1)S(1)}, u32[]{:S(2)}, u32[]{:S(2)}) collective-permute-start(bf16[880,128]{1,0:T(8,128)(2,1)S(1)} %get-tuple-element.27), channel_id=1, source_target_pairs={{0,4},{4,8},{8,12},{12,0},{1,5},{5,9},{9,13},{13,1},{2,6},{6,10},{... | collective-permute-start | bytes 675848 | tf_op jit(solution)/shard_map/ppermute | solution.py:489
  5.0 2.1 %collective-permute-start = (bf16[872,128]{1,0:T(8,128)(2,1)S(1)}, bf16[872,128]{1,0:T(8,128)(2,1)S(1)}, u32[]{:S(2)}, u32[]{:S(2)}) collective-permute-start(bf16[872,128]{1,0:T(8,128)(2,1)S(1)} %get-tuple-element.21), channel_id=1, source_target_pairs={{4,0},{8,4},{12,8},{0,12},{5,1},{9,5},{13,9},{1,13},{6,2},{10,6},{... | collective-permute-start | bytes 669704 | tf_op jit(solution)/shard_map/ppermute | solution.py:490
  7.1 0.0 collective-permute-start.1
  7.1 1.6 %collective-permute-start.3 = (bf16[864,128]{1,0:T(8,128)(2,1)S(1)}, bf16[864,128]{1,0:T(8,128)(2,1)S(1)}, u32[]{:S(2)}, u32[]{:S(2)}) collective-permute-start(bf16[864,128]{1,0:T(8,128)(2,1)S(1)} %get-tuple-element.24.field_ref), channel_id=1, source_target_pairs={{0,2},{2,0},{1,3},{3,1},{4,6},{6,4},{5,7},{7,5},{8,10},{10,8},{9,1... | collective-permute-start | bytes 663560 | tf_op jit(solution)/shard_map/ppermute | solution.py:447
  8.8 0.0 collective-permute-done.1.y_ref
  8.8 2.7 %shard_map.87 = (f32[3,3,3,2,16,128]{5,4,3,2,1,0:T(8,128)S(1)}, f32[2,3,3,3,2,16,128]{6,5,4,3,2,1,0:T(8,128)S(1)}, f32[9,16,128]{2,1,0:T(8,128)S(1)}, f32[1296,128]{1,0:T(8,128)S(1)}, f32[1296,128]{1,0:T(8,128)S(1)}) custom-call(s32[3,8]{1,0:T(4,128)} %bitcast.28, bf16[1296,128]{1,0:T(8,128)(2,1)S(1)} %get-tuple-element.22.fat, ...), custom_call_target="tpu_custom_call" | custom-call | flops 1 | bytes 1 | tf_op jit(solution)/shard_map/pallas_call | solution.py:500
  11.5 3.5 %collective-permute-done.3.before_ref.after_ref = bf16[864,128]{1,0:T(8,128)(2,1)S(1)} collective-permute-done((bf16[864,128]{1,0:T(8,128)(2,1)S(1)}, bf16[864,128]{1,0:T(8,128)(2,1)S(1)}, u32[]{:S(2)}, u32[]{:S(2)}) %collective-permute-start.3) | collective-permute-done | bytes 221216 | tf_op jit(solution)/shard_map/ppermute | solution.py:447
  15.0 1.2 %shard_map.88 = (f32[3,3,3,2,16,128]{5,4,3,2,1,0:T(8,128)S(1)}, bf16[3,256,2304]{2,1,0:T(8,128)(2,1)S(1)}) custom-call(s32[4]{0:T(128)} %dirs_hbm.1, s32[4]{0:T(128)} %masks_hbm.1, bf16[864,128]{1,0:T(8,128)(2,1)S(1)} %get-tuple-element.24.field_ref, bf16[864,128]{1,0:T(8,128)(2,1)S(1)} %collective-permute-done.3.before_ref.after_ref, ...), custom_call_target="tpu_custom_call" | custom-call | flops 1 | bytes 1 | tf_op jit(solution)/shard_map/pallas_call | solution.py:518
  16.2 0.0 collective-permute-done.2.block_ref
  16.2 0.3 %shard_map.89.dacc_in = f32[3,3,3,2,16,128]{5,4,3,2,1,0:T(8,128)S(1)} custom-call(bf16[880,128]{1,0:T(8,128)(2,1)S(1)} %collective-permute-done.2.block_ref, f32[1296,128]{1,0:T(8,128)S(1)} %get-tuple-element.25.fatf, f32[1296,128]{1,0:T(8,128)S(1)} %get-tuple-element.26.longf, f32[3,3,3,2,16,128]{5,4,3,2,1,0:T(8,128)S(1)} %get-tuple-element.30.dacc_in), custom_call_target="tpu_custom_call" | custom-call | flops 1000 | bytes 1000 | tf_op jit(solution)/shard_map/pallas_call | solution.py:537
  16.5 0.3 %collective-permute-done.block_ref = bf16[872,128]{1,0:T(8,128)(2,1)S(1)} collective-permute-done((bf16[872,128]{1,0:T(8,128)(2,1)S(1)}, bf16[872,128]{1,0:T(8,128)(2,1)S(1)}, u32[]{:S(2)}, u32[]{:S(2)}) %collective-permute-start) | collective-permute-done | bytes 223264 | tf_op jit(solution)/shard_map/ppermute | solution.py:490
  16.8 0.3 %shard_map.90.dacc = f32[3,3,3,2,16,128]{5,4,3,2,1,0:T(8,128)S(1)} custom-call(bf16[872,128]{1,0:T(8,128)(2,1)S(1)} %collective-permute-done.block_ref, f32[1296,128]{1,0:T(8,128)S(1)} %get-tuple-element.25.fatf, f32[1296,128]{1,0:T(8,128)S(1)} %get-tuple-element.26.longf, f32[3,3,3,2,16,128]{5,4,3,2,1,0:T(8,128)S(1)} %shard_map.89.dacc_in), custom_call_target="tpu_custom_call" | custom-call | flops 1000 | bytes 1000 | tf_op jit(solution)/shard_map/pallas_call | solution.py:537
  17.0 1.2 %shard_map.91 = (bf16[3,3,3,2,16,128]{5,4,3,2,1,0:T(8,128)(2,1)S(1)}, f32[3,2,16,128]{3,2,1,0:T(8,128)S(1)}, f32[3,2,16,128]{3,2,1,0:T(8,128)S(1)}, f32[3,2,16,128]{3,2,1,0:T(8,128)S(1)}, f32[3,2,16,128]{3,2,1,0:T(8,128)S(1)}) custom-call(f32[3,3,3,2,16,128]{5,4,3,2,1,0:T(8,128)S(1)} %shard_map.90.dacc, f32[9,16,128]{2,1,0:T(8,128)S(1)} %get-tuple-element.31.weights, ...), custom_call_target="tpu_custom_call" | custom-call | flops 1 | bytes 1 | tf_op jit(solution)/shard_map/pallas_call | solution.py:544
  18.3 0.1 collective-permute-start.4
  18.4 1.3 %collective-permute-done.4 = f32[2,3,2,16,128]{4,3,2,1,0:T(8,128)S(1)} collective-permute-done((f32[2,3,2,16,128]{4,3,2,1,0:T(8,128)S(1)}, f32[2,3,2,16,128]{4,3,2,1,0:T(8,128)S(1)}, u32[]{:S(2)}, u32[]{:S(2)}) %collective-permute-start.4) | collective-permute-done | bytes 98336 | tf_op jit(solution)/shard_map/ppermute | solution.py:557
  19.7 1.6 %collective-permute-start.5 = (f32[3,2,16,128]{3,2,1,0:T(8,128)S(1)}, f32[3,2,16,128]{3,2,1,0:T(8,128)S(1)}, u32[]{:S(2)}, u32[]{:S(2)}) collective-permute-start(f32[3,2,16,128]{3,2,1,0:T(8,128)S(1)} %fusion), channel_id=1, source_target_pairs={{0,2},{2,0},{1,3},{3,1},{4,6},{6,4},{5,7},{7,5},{8,10},{10,8},{9,1... | collective-permute-start | bytes 147464 | tf_op jit(solution)/shard_map/ppermute | solution.py:558
  21.2 0.7 %shard_map.92 = (bf16[864,128]{1,0:T(8,128)(2,1)}, f32[3,2,16,128]{3,2,1,0:T(8,128)S(1)}) custom-call(bf16[54,16,128]{2,1,0:T(8,128)(2,1)S(1)} %bitcast.22, f32[3,2,16,128]{3,2,1,0:T(8,128)S(1)} %get-tuple-element.34.kept, f32[3,2,16,128]{3,2,1,0:T(8,128)S(1)} %slice_bitcast_fusion.1.arrived), custom_call_target="tpu_custom_call" | custom-call | flops 1 | bytes 1 | tf_op jit(solution)/shard_map/pallas_call | solution.py:559
  22.0 1.8 %collective-permute-done.5.other = f32[3,2,16,128]{3,2,1,0:T(8,128)S(1)} collective-permute-done((f32[3,2,16,128]{3,2,1,0:T(8,128)S(1)}, f32[3,2,16,128]{3,2,1,0:T(8,128)S(1)}, u32[]{:S(2)}, u32[]{:S(2)}) %collective-permute-start.5) | collective-permute-done | bytes 49184 | tf_op jit(solution)/shard_map/ppermute | solution.py:558
  23.8 0.9 %shard_map.93 = f32[8,3,2,16,16]{4,3,2,1,0:T(8,128)} custom-call(f32[3,2,16,128]{3,2,1,0:T(8,128)S(1)} %get-tuple-element.38.partial, f32[3,2,16,128]{3,2,1,0:T(8,128)S(1)} %collective-permute-done.5.other), custom_call_target="tpu_custom_call" | custom-call | flops 1 | bytes 1 | tf_op jit(solution)/shard_map/pallas_call | solution.py:563
  (3 shorter events, 0.0 us)
Async XLA Ops:
  1.9 14.2 %collective-permute-start.2 = (bf16[880,128]{1,0:T(8,128)(2,1)S(1)}, bf16[880,128]{1,0:T(8,128)(2,1)S(1)}, u32[]{:S(2)}, u32[]{:S(2)}) collective-permute-start(bf16[880,128]{1,0:T(8,128)(2,1)S(1)} %get-tuple-element.27), channel_id=1, source_target_pairs={{0,4},{4,8},{8,12},{12,0},{1,5},{5,9},{9,13},{13,1},{2,6},{6,10},{... | collective-permute-start | bytes 675848 | tf_op jit(solution)/shard_map/ppermute | solution.py:489
  5.0 11.8 %collective-permute-start = (bf16[872,128]{1,0:T(8,128)(2,1)S(1)}, bf16[872,128]{1,0:T(8,128)(2,1)S(1)}, u32[]{:S(2)}, u32[]{:S(2)}) collective-permute-start(bf16[872,128]{1,0:T(8,128)(2,1)S(1)} %get-tuple-element.21), channel_id=1, source_target_pairs={{4,0},{8,4},{12,8},{0,12},{5,1},{9,5},{13,9},{1,13},{6,2},{10,6},{... | collective-permute-start | bytes 669704 | tf_op jit(solution)/shard_map/ppermute | solution.py:490
  7.1 1.7 %collective-permute-start.1 = (bf16[864,128]{1,0:T(8,128)(2,1)S(1)}, bf16[864,128]{1,0:T(8,128)(2,1)S(1)}, u32[]{:S(2)}, u32[]{:S(2)}) collective-permute-start(bf16[864,128]{1,0:T(8,128)(2,1)S(1)} %get-tuple-element.24.field_ref), channel_id=1, source_target_pairs={{0,1},{1,0},{2,3},{3,2},{4,5},{5,4},{6,7},{7,6},{8,9},{9,8},{10,11... | collective-permute-start | bytes 663560 | tf_op jit(solution)/shard_map/ppermute | solution.py:447
  7.1 7.8 %collective-permute-start.3 = (bf16[864,128]{1,0:T(8,128)(2,1)S(1)}, bf16[864,128]{1,0:T(8,128)(2,1)S(1)}, u32[]{:S(2)}, u32[]{:S(2)}) collective-permute-start(bf16[864,128]{1,0:T(8,128)(2,1)S(1)} %get-tuple-element.24.field_ref), channel_id=1, source_target_pairs={{0,2},{2,0},{1,3},{3,1},{4,6},{6,4},{5,7},{7,5},{8,10},{10,8},{9,1... | collective-permute-start | bytes 663560 | tf_op jit(solution)/shard_map/ppermute | solution.py:447
  18.3 1.4 %collective-permute-start.4 = (f32[2,3,2,16,128]{4,3,2,1,0:T(8,128)S(1)}, f32[2,3,2,16,128]{4,3,2,1,0:T(8,128)S(1)}, u32[]{:S(2)}, u32[]{:S(2)}) collective-permute-start(f32[2,3,2,16,128]{4,3,2,1,0:T(8,128)S(1)} %pad_maximum_fusion), channel_id=1, source_target_pairs={{0,1},{1,0},{2,3},{3,2},{4,5},{5,4},{6,7},{7,6},{8,9},{9,8},{10,11... | collective-permute-start | bytes 294920 | tf_op jit(solution)/shard_map/ppermute | solution.py:557
  19.7 4.2 %collective-permute-start.5 = (f32[3,2,16,128]{3,2,1,0:T(8,128)S(1)}, f32[3,2,16,128]{3,2,1,0:T(8,128)S(1)}, u32[]{:S(2)}, u32[]{:S(2)}) collective-permute-start(f32[3,2,16,128]{3,2,1,0:T(8,128)S(1)} %fusion), channel_id=1, source_target_pairs={{0,2},{2,0},{1,3},{3,1},{4,6},{6,4},{5,7},{7,5},{8,10},{10,8},{9,1... | collective-permute-start | bytes 147464 | tf_op jit(solution)/shard_map/ppermute | solution.py:558

commit v6 on v5

--- a/solution.py
+++ b/solution.py
@@ -38,8 +38,8 @@
 
 
 def gather_kernel(
-    vectors, chosen_hbm, store_hbm, fat_hbm, long_hbm,
-    up, down, out, fat, long,
+    times, depth, vectors, chosen_hbm, store_hbm, fat_hbm, long_hbm,
+    up, down, last, out, fat, long,
     chosen, store, wide, turned, sems,
 ):
     piece = store.shape[0] // PIECES
@@ -73,13 +73,19 @@
             turned[pl.ds(full * 8 * vectors + n, rest, stride=vectors), :] = wide[
                 pl.ds(start + 8 * full, rest), :
             ]
-    for r in range(0, size, 16):
-        block = turned[r : r + 16, :].astype(BF16)
-        out[r : r + 16, :] = block
-        up[r : r + 16, :] = block
-        down[r : r + 16, :] = block
-    for ref in (up, down):
-        ref[size:, :] = jnp.zeros((ref.shape[0] - size, LANES), BF16)
+    layer = depth * 2 * vectors
+    for a in range(3):
+        for t in range(times):
+            source = (a * times + t) * layer
+            block = turned[source : source + layer, :].astype(BF16)
+            out[source : source + layer, :] = block
+            up[source : source + layer, :] = block
+            if t + 1 < times:
+                target = (a * (times - 1) + t) * layer
+                down[target : target + layer, :] = block
+            else:
+                last[a * layer : (a + 1) * layer, :] = block
+    up[size:, :] = jnp.zeros((up.shape[0] - size, LANES), BF16)
     for copy in later:
         copy.wait()
 
@@ -355,66 +361,92 @@
 NT_DIMS = (((1,), (1,)), ((), ()))
 
 
-def block_hops(acc, links, field, times, t, z, ahead):
-    fat_l, long_l = links
-    w = 0 if ahead else 1
-    add_hop(acc, long_l, w, 0, t, z, field.read(t, z), not ahead)
-    if ahead and t + 1 == times:
-        add_hop(acc, fat_l, 0, 0, t, z, field.read(0, z), False)
-    if not ahead and t == 0:
-        add_hop(acc, fat_l, 1, 0, t, z, field.read(times - 1, z), True)
-
-
-def time_kernel(times, depth, vectors, ahead, block_ref, fatf, longf, dacc_in, dacc):
-    links = Links(fatf, times, depth), Links(longf, times, depth)
+def before_kernel(times, depth, vectors, block_ref, fatf, longf, dacc_in, dacc):
+    fat_l, long_l = Links(fatf, times, depth), Links(longf, times, depth)
     block = Field(block_ref, times, depth, vectors)
     for t in range(times):
         for z in range(depth):
             acc = read(dacc_in, t, z)
-            block_hops(acc, links, block, times, t, z, ahead)
+            add_hop(acc, long_l, 1, 0, t, z, block.read(t, z), True)
+            if t == 0:
+                add_hop(acc, fat_l, 1, 0, t, z, block.read(times - 1, z), True)
             write(dacc, t, z, acc)
 
 
-def meson_kernel(times, depth, vectors, dacc, weights, left, dirac16, *pieces):
+def meson_slice(t, layers, weights, left, pieces, vectors):
     rows = 2 * vectors
     left_rows = left.shape[1] // 2
     count = weights.shape[1] // 2
     columns = count * vectors
-    for t in range(times):
-        parts = jnp.zeros((2 * left_rows, 2 * columns), F32)
+    parts = jnp.zeros((2 * left_rows, 2 * columns), F32)
+    depth = len(layers)
+    for z, acc in enumerate(layers):
+        at = t * depth + z
+        for a in range(3):
+            real, imag = acc[a]
+            right = [[], []]
+            for p in range(count):
+                cosine = weights[at, p : p + 1, :]
+                sine = weights[at, count + p : count + p + 1, :]
+                right[0].append(halves(cosine * real + sine * imag))
+                right[1].append(halves(cosine * imag - sine * real))
+            right = jnp.concatenate(
+                [jnp.concatenate([h for h, _ in r] + [l for _, l in r], axis=0) for r in right],
+                axis=1,
+            )
+            col = (z * 3 + a) * 2 * LANES
+            parts = parts + lax.dot_general(
+                left[t, :, col : col + 2 * LANES], right, NT_DIMS, preferred_element_type=F32
+            )
+    total = (parts[:left_rows, :columns] + parts[left_rows:, columns:]) + (
+        parts[left_rows:, :columns] + parts[:left_rows, columns:]
+    )
+    for slot, piece in enumerate(pieces):
+        for ri in range(2):
+            top = slot * rows + ri * vectors
+            piece[t, ri] = total[top : top + vectors]
+
+
+def early_kernel(
+    times, depth, vectors,
+    block_ref, fatf, longf, dacc, weights, left,
+    edge, dirac16, *pieces,
+):
+    fat_l, long_l = Links(fatf, times, depth), Links(longf, times, depth)
+    block = Field(block_ref, times - 1, depth, vectors)
+    for z in range(depth):
+        acc = read(dacc, times - 1, z)
+        add_hop(acc, fat_l, 0, 0, times - 1, z, block.read(0, z), False)
+        write(edge, 0, z, acc)
+    for t in range(times - 1):
+        layers = []
         for z in range(depth):
             acc = read(dacc, t, z)
+            add_hop(acc, long_l, 0, 0, t, z, block.read(t, z), False)
             write(dirac16, t, z, acc)
-            at = t * depth + z
-            for a in range(3):
-                real, imag = acc[a]
-                right = [[], []]
-                for p in range(count):
-                    cosine = weights[at, p : p + 1, :]
-                    sine = weights[at, count + p : count + p + 1, :]
-                    right[0].append(halves(cosine * real + sine * imag))
-                    right[1].append(halves(cosine * imag - sine * real))
-                right = jnp.concatenate(
-                    [
-                        jnp.concatenate([h for h, _ in r] + [l for _, l in r], axis=0)
-                        for r in right
-                    ],
-                    axis=1,
-                )
-                col = (z * 3 + a) * 2 * LANES
-                parts = parts + lax.dot_general(
-                    left[t, :, col : col + 2 * LANES],
-                    right,
-                    NT_DIMS,
-                    preferred_element_type=F32,
-                )
-        total = (parts[:left_rows, :columns] + parts[left_rows:, columns:]) + (
-            parts[left_rows:, :columns] + parts[:left_rows, columns:]
-        )
-        for slot, piece in enumerate(pieces):
-            for ri in range(2):
-                top = slot * rows + ri * vectors
-                piece[t, ri] = total[top : top + vectors]
+            layers.append(acc)
+        meson_slice(t, layers, weights, left, pieces, vectors)
+
+
+def late_kernel(
+    times, depth, vectors,
+    block_ref, longf, edge, weights, left, dirac16_in, *rest,
+):
+    slots = len(rest) // 2
+    pieces_in, dirac16, pieces = rest[:slots], rest[slots], rest[slots + 1 :]
+    long_l = Links(longf, times, depth)
+    block = Field(block_ref, 1, depth, vectors)
+    layers = []
+    for z in range(depth):
+        acc = read(edge, 0, z)
+        add_hop(acc, long_l, 0, 0, times - 1, z, block.read(0, z), False)
+        write(dirac16, times - 1, z, acc)
+        layers.append(acc)
+    meson_slice(times - 1, layers, weights, left, pieces, vectors)
+    for t in range(times - 1):
+        dirac16[:, t] = dirac16_in[:, t]
+        for source, piece in zip(pieces_in, pieces):
+            piece[t] = source[t]
 
 
 def spread_kernel(dirac16, kept, arrived, out, partial, wide):
@@ -468,10 +500,11 @@
     def rows_of(n, dtype=BF16):
         return jax.ShapeDtypeStruct((n, LANES), dtype)
 
-    up_out, down_out, packed, fat_v, long_v = call(
-        functools.partial(gather_kernel, vectors),
+    last_size = size // times
+    up_out, down_out, last_out, packed, fat_v, long_v = call(
+        functools.partial(gather_kernel, times, depth, vectors),
         [
-            rows_of(size + 16), rows_of(size + 8), rows_of(size),
+            rows_of(size + 16), rows_of(size - last_size), rows_of(last_size), rows_of(size),
             rows_of(link_rows), rows_of(link_rows),
         ],
         [HB] * 4,
@@ -488,6 +521,7 @@
     down = [(j, i) for i, j in up]
     before_t = lax.ppermute(up_out, "ta", up)
     after_t = lax.ppermute(down_out, "ta", down)
+    after_last = lax.ppermute(last_out, "ta", down)
     before_z, after_z = exchange(packed, "gz")
     y_field, _ = exchange(packed, "gy")
 
@@ -533,21 +567,28 @@
         pinned(current_dirs), pinned(taste_masks), packed, before_z, after_z, fatf, longf, dacc, back_xy
     )
     piece = jax.ShapeDtypeStruct((times, 2, vectors, count * vectors), F32)
-    for block, ahead in ((before_t, False), (after_t, True)):
-        (dacc,) = call(
-            functools.partial(time_kernel, times, depth, vectors, ahead),
-            [jax.ShapeDtypeStruct(shape6, F32)],
-            [VM] * 4,
-            [],
-            1000,
-        )(block, fatf, longf, dacc)
-    dirac16, *pieces = call(
-        functools.partial(meson_kernel, times, depth, vectors),
-        [jax.ShapeDtypeStruct(shape6, BF16)] + [piece] * slots,
-        [VM] * 3,
+    (dacc,) = call(
+        functools.partial(before_kernel, times, depth, vectors),
+        [jax.ShapeDtypeStruct(shape6, F32)],
+        [VM] * 4,
         [],
         1,
-    )(dacc, weights, left)
+    )(before_t, fatf, longf, dacc)
+    finished = [jax.ShapeDtypeStruct(shape6, BF16)] + [piece] * slots
+    edge, *early = call(
+        functools.partial(early_kernel, times, depth, vectors),
+        [jax.ShapeDtypeStruct((3, 1) + shape6[2:], F32)] + finished,
+        [VM] * 6,
+        [],
+        1,
+    )(after_t, fatf, longf, dacc, weights, left)
+    dirac16, *pieces = call(
+        functools.partial(late_kernel, times, depth, vectors),
+        finished,
+        [VM] * (6 + slots),
+        [],
+        1,
+    )(after_last, longf, edge, weights, left, *early)
 
     odd_shape = rows_of(size)
     turned = dirac16.reshape(per_vector, vectors, LANES)

time: 24.9 us -> 24.5 us (0.984)
  waiting for transfers between devices: 6.96 us -> 4.67 us
  starting transfers between devices: 8.45 us -> 10.3 us
    ppermute x2, waiting for transfers between devices: 3.5 us -> 0.01 us  [exchange(): before = lax.ppermute(value, axis, up)]
    ppermute x0 -> x1, starting transfers between devices: none -> 1.8 us  [on_device(): after_last = lax.ppermute(last_out, 'ta', down)]
    ppermute x1, waiting for transfers between devices: 0.33 us -> 1 us  [on_device(): after_t = lax.ppermute(down_out, 'ta', down)]
    ppermute x0 -> x1, waiting for transfers between devices: none -> 0.55 us  [on_device(): after_last = lax.ppermute(last_out, 'ta', down)]
  transfers between devices with their start and end apart: 6 -> 7, of which waited for: 4 -> 4; matrix products, arithmetic and copies ran while one was open for 0% -> 0% of each run, Pallas kernels for 20% -> 24%
where the time goes in v6:
time: 24.5 us; the launch traced here: 24.3 us
  starting transfers between devices  10.3 us (42%)
  Pallas kernels  8.64 us (35%)
  waiting for transfers between devices  4.67 us (19%)
  between operations  0.7 us (3%)
    ppermute x1, starting transfers between devices, on_device(): before_t = lax.ppermute(up_out, 'ta', up)  3.08 us
    pallas_call x1, Pallas kernels, on_device(): call(functools.partial(local_kernel, times, depth, vectors, (total_y, tot...  2.71 us
    ppermute x1, starting transfers between devices, on_device(): after_t = lax.ppermute(down_out, 'ta', down)  2.25 us
    ppermute x1, waiting for transfers between devices, on_device(): other = lax.ppermute(pieces[2] + got[1], 'gz', swap)  1.85 us
    ppermute x1, starting transfers between devices, on_device(): after_last = lax.ppermute(last_out, 'ta', down)  1.8 us
    ppermute x1, starting transfers between devices, on_device(): other = lax.ppermute(pieces[2] + got[1], 'gz', swap)  1.55 us
    ppermute x2, starting transfers between devices, exchange(): before = lax.ppermute(value, axis, up)  1.49 us
    pallas_call x1, Pallas kernels, on_device(): call(functools.partial(gather_kernel, times, depth, vectors), [rows_of(si...  1.3 us
  transfers between devices with their start and end apart: 7, of which 4 were waited for; matrix products, arithmetic and copies ran while one was open for 0% of the time, Pallas kernels for 24%

profile of v6, /device:TPU:0, one launch (start us, length us, event | category | flops | bytes accessed | tf_op | source)
XLA Modules:
  0.0 24.3 jit_solution(16677104469696451222)
XLA Ops:
  0.6 1.3 %shard_map.86 = (bf16[880,128]{1,0:T(8,128)(2,1)S(1)}, bf16[576,128]{1,0:T(8,128)(2,1)S(1)}, bf16[288,128]{1,0:T(8,128)(2,1)S(1)}, bf16[864,128]{1,0:T(8,128)(2,...) custom-call(s32[16]{0:T(128)} %chosen_hbm.1, bf16[1080,128]{1,0:T(8,128)(2,1)} %bitcast.27, ...), custom_call_target="tpu_custom_call" | custom-call | flops 1 | bytes 1 | tf_op jit(solution)/shard_map/pallas_call | solution.py:504
  1.9 3.1 %collective-permute-start.3 = (bf16[880,128]{1,0:T(8,128)(2,1)S(1)}, bf16[880,128]{1,0:T(8,128)(2,1)S(1)}, u32[]{:S(2)}, u32[]{:S(2)}) collective-permute-start(bf16[880,128]{1,0:T(8,128)(2,1)S(1)} %get-tuple-element.35), channel_id=1, source_target_pairs={{0,4},{4,8},{8,12},{12,0},{1,5},{5,9},{9,13},{13,1},{2,6},{6,10},{... | collective-permute-start | bytes 675848 | tf_op jit(solution)/shard_map/ppermute | solution.py:522
  5.0 0.0 collective-permute-start.1
  5.0 1.5 %collective-permute-start.4 = (bf16[864,128]{1,0:T(8,128)(2,1)S(1)}, bf16[864,128]{1,0:T(8,128)(2,1)S(1)}, u32[]{:S(2)}, u32[]{:S(2)}) collective-permute-start(bf16[864,128]{1,0:T(8,128)(2,1)S(1)} %get-tuple-element.31.field_ref), channel_id=1, source_target_pairs={{0,2},{2,0},{1,3},{3,1},{4,6},{6,4},{5,7},{7,5},{8,10},{10,8},{9,1... | collective-permute-start | bytes 663560 | tf_op jit(solution)/shard_map/ppermute | solution.py:479
  6.5 2.2 %collective-permute-start.2 = (bf16[576,128]{1,0:T(8,128)(2,1)S(1)}, bf16[576,128]{1,0:T(8,128)(2,1)S(1)}, u32[]{:S(2)}, u32[]{:S(2)}) collective-permute-start(bf16[576,128]{1,0:T(8,128)(2,1)S(1)} %get-tuple-element.33), channel_id=1, source_target_pairs={{4,0},{8,4},{12,8},{0,12},{5,1},{9,5},{13,9},{1,13},{6,2},{10,6},{... | collective-permute-start | bytes 442376 | tf_op jit(solution)/shard_map/ppermute | solution.py:523
  8.8 1.8 %collective-permute-start = (bf16[288,128]{1,0:T(8,128)(2,1)S(1)}, bf16[288,128]{1,0:T(8,128)(2,1)S(1)}, u32[]{:S(2)}, u32[]{:S(2)}) collective-permute-start(bf16[288,128]{1,0:T(8,128)(2,1)S(1)} %get-tuple-element.28), channel_id=1, source_target_pairs={{4,0},{8,4},{12,8},{0,12},{5,1},{9,5},{13,9},{1,13},{6,2},{10,6},{... | collective-permute-start | bytes 221192 | tf_op jit(solution)/shard_map/ppermute | solution.py:524
  10.6 0.0 collective-permute-done.1.y_ref
  10.6 2.7 %shard_map.87 = (f32[3,3,3,2,16,128]{5,4,3,2,1,0:T(8,128)S(1)}, f32[2,3,3,3,2,16,128]{6,5,4,3,2,1,0:T(8,128)S(1)}, f32[9,16,128]{2,1,0:T(8,128)S(1)}, f32[1296,128]{1,0:T(8,128)S(1)}, f32[1296,128]{1,0:T(8,128)S(1)}) custom-call(s32[3,8]{1,0:T(4,128)} %bitcast.28, bf16[1296,128]{1,0:T(8,128)(2,1)S(1)} %get-tuple-element.29.fat, ...), custom_call_target="tpu_custom_call" | custom-call | flops 1 | bytes 1 | tf_op jit(solution)/shard_map/pallas_call | solution.py:534
  13.3 0.0 collective-permute-done.4.before_ref.after_ref
  13.3 1.2 %shard_map.88 = (f32[3,3,3,2,16,128]{5,4,3,2,1,0:T(8,128)S(1)}, bf16[3,256,2304]{2,1,0:T(8,128)(2,1)S(1)}) custom-call(s32[4]{0:T(128)} %dirs_hbm.1, s32[4]{0:T(128)} %masks_hbm.1, bf16[864,128]{1,0:T(8,128)(2,1)S(1)} %get-tuple-element.31.field_ref, bf16[864,128]{1,0:T(8,128)(2,1)S(1)} %collective-permute-done.4.before_ref.after_ref, ...), custom_call_target="tpu_custom_call" | custom-call | flops 1 | bytes 1 | tf_op jit(solution)/shard_map/pallas_call | solution.py:552
  14.5 0.0 collective-permute-done.3.block_ref
  14.5 0.3 %shard_map.89.dacc = f32[3,3,3,2,16,128]{5,4,3,2,1,0:T(8,128)S(1)} custom-call(bf16[880,128]{1,0:T(8,128)(2,1)S(1)} %collective-permute-done.3.block_ref, f32[1296,128]{1,0:T(8,128)S(1)} %get-tuple-element.34.fatf, f32[1296,128]{1,0:T(8,128)S(1)} %get-tuple-element.32.longf, f32[3,3,3,2,16,128]{5,4,3,2,1,0:T(8,128)S(1)} %get-tuple-element.38.dacc_in), custom_call_target="tpu_custom_call" | custom-call | flops 1 | bytes 1 | tf_op jit(solution)/shard_map/pallas_call | solution.py:570
  14.8 1.0 %collective-permute-done.2.block_ref = bf16[576,128]{1,0:T(8,128)(2,1)S(1)} collective-permute-done((bf16[576,128]{1,0:T(8,128)(2,1)S(1)}, bf16[576,128]{1,0:T(8,128)(2,1)S(1)}, u32[]{:S(2)}, u32[]{:S(2)}) %collective-permute-start.2) | collective-permute-done | bytes 147488 | tf_op jit(solution)/shard_map/ppermute | solution.py:523
  15.8 1.0 %shard_map.90 = (f32[3,1,3,2,16,128]{5,4,3,2,1,0:T(8,128)S(1)}, bf16[3,3,3,2,16,128]{5,4,3,2,1,0:T(8,128)(2,1)S(1)}, f32[3,2,16,128]{3,2,1,0:T(8,128)S(1)}, f32[...) custom-call(bf16[576,128]{1,0:T(8,128)(2,1)S(1)} %collective-permute-done.2.block_ref, ...), custom_call_target="tpu_custom_call" | custom-call | flops 1 | bytes 1 | tf_op jit(solution)/shard_map/pallas_call | solution.py:578
  16.8 0.5 %collective-permute-done.block_ref = bf16[288,128]{1,0:T(8,128)(2,1)S(1)} collective-permute-done((bf16[288,128]{1,0:T(8,128)(2,1)S(1)}, bf16[288,128]{1,0:T(8,128)(2,1)S(1)}, u32[]{:S(2)}, u32[]{:S(2)}) %collective-permute-start) | collective-permute-done | bytes 73760 | tf_op jit(solution)/shard_map/ppermute | solution.py:524
  17.3 0.6 %shard_map.91 = (bf16[3,3,3,2,16,128]{5,4,3,2,1,0:T(8,128)(2,1)S(1)}, f32[3,2,16,128]{3,2,1,0:T(8,128)S(1)}, f32[3,2,16,128]{3,2,1,0:T(8,128)S(1)}, f32[3,2,16,128]{3,2,1,0:T(8,128)S(1)}, f32[3,2,16,128]{3,2,1,0:T(8,128)S(1)}) custom-call(bf16[288,128]{1,0:T(8,128)(2,1)S(1)} %collective-permute-done.block_ref, f32[1296,128]{1,0:T(8,128)S(1)} %get-tuple-element.32.longf, ...), custom_call_target="tpu_custom_call" | custom-call | flops 1 | bytes 1 | tf_op jit(solution)/shard_map/pallas_call | solution.py:585
  17.9 0.1 collective-permute-start.5
  18.0 1.3 %collective-permute-done.5 = f32[2,3,2,16,128]{4,3,2,1,0:T(8,128)S(1)} collective-permute-done((f32[2,3,2,16,128]{4,3,2,1,0:T(8,128)S(1)}, f32[2,3,2,16,128]{4,3,2,1,0:T(8,128)S(1)}, u32[]{:S(2)}, u32[]{:S(2)}) %collective-permute-start.5) | collective-permute-done | bytes 98336 | tf_op jit(solution)/shard_map/ppermute | solution.py:598
  19.3 1.6 %collective-permute-start.6 = (f32[3,2,16,128]{3,2,1,0:T(8,128)S(1)}, f32[3,2,16,128]{3,2,1,0:T(8,128)S(1)}, u32[]{:S(2)}, u32[]{:S(2)}) collective-permute-start(f32[3,2,16,128]{3,2,1,0:T(8,128)S(1)} %fusion), channel_id=1, source_target_pairs={{0,2},{2,0},{1,3},{3,1},{4,6},{6,4},{5,7},{7,5},{8,10},{10,8},{9,1... | collective-permute-start | bytes 147464 | tf_op jit(solution)/shard_map/ppermute | solution.py:599
  20.8 0.7 %shard_map.92 = (bf16[864,128]{1,0:T(8,128)(2,1)}, f32[3,2,16,128]{3,2,1,0:T(8,128)S(1)}) custom-call(bf16[54,16,128]{2,1,0:T(8,128)(2,1)S(1)} %bitcast.22, f32[3,2,16,128]{3,2,1,0:T(8,128)S(1)} %get-tuple-element.48.kept, f32[3,2,16,128]{3,2,1,0:T(8,128)S(1)} %slice_bitcast_fusion.1.arrived), custom_call_target="tpu_custom_call" | custom-call | flops 1 | bytes 1 | tf_op jit(solution)/shard_map/pallas_call | solution.py:600
  21.6 1.9 %collective-permute-done.6.other = f32[3,2,16,128]{3,2,1,0:T(8,128)S(1)} collective-permute-done((f32[3,2,16,128]{3,2,1,0:T(8,128)S(1)}, f32[3,2,16,128]{3,2,1,0:T(8,128)S(1)}, u32[]{:S(2)}, u32[]{:S(2)}) %collective-permute-start.6) | collective-permute-done | bytes 49184 | tf_op jit(solution)/shard_map/ppermute | solution.py:599
  23.4 0.9 %shard_map.93 = f32[8,3,2,16,16]{4,3,2,1,0:T(8,128)} custom-call(f32[3,2,16,128]{3,2,1,0:T(8,128)S(1)} %get-tuple-element.52.partial, f32[3,2,16,128]{3,2,1,0:T(8,128)S(1)} %collective-permute-done.6.other), custom_call_target="tpu_custom_call" | custom-call | flops 1 | bytes 1 | tf_op jit(solution)/shard_map/pallas_call | solution.py:604
  (3 shorter events, 0.0 us)
Async XLA Ops:
  1.9 12.6 %collective-permute-start.3 = (bf16[880,128]{1,0:T(8,128)(2,1)S(1)}, bf16[880,128]{1,0:T(8,128)(2,1)S(1)}, u32[]{:S(2)}, u32[]{:S(2)}) collective-permute-start(bf16[880,128]{1,0:T(8,128)(2,1)S(1)} %get-tuple-element.35), channel_id=1, source_target_pairs={{0,4},{4,8},{8,12},{12,0},{1,5},{5,9},{9,13},{13,1},{2,6},{6,10},{... | collective-permute-start | bytes 675848 | tf_op jit(solution)/shard_map/ppermute | solution.py:522
  5.0 5.5 %collective-permute-start.1 = (bf16[864,128]{1,0:T(8,128)(2,1)S(1)}, bf16[864,128]{1,0:T(8,128)(2,1)S(1)}, u32[]{:S(2)}, u32[]{:S(2)}) collective-permute-start(bf16[864,128]{1,0:T(8,128)(2,1)S(1)} %get-tuple-element.31.field_ref), channel_id=1, source_target_pairs={{0,1},{1,0},{2,3},{3,2},{4,5},{5,4},{6,7},{7,6},{8,9},{9,8},{10,11... | collective-permute-start | bytes 663560 | tf_op jit(solution)/shard_map/ppermute | solution.py:479
  5.0 8.3 %collective-permute-start.4 = (bf16[864,128]{1,0:T(8,128)(2,1)S(1)}, bf16[864,128]{1,0:T(8,128)(2,1)S(1)}, u32[]{:S(2)}, u32[]{:S(2)}) collective-permute-start(bf16[864,128]{1,0:T(8,128)(2,1)S(1)} %get-tuple-element.31.field_ref), channel_id=1, source_target_pairs={{0,2},{2,0},{1,3},{3,1},{4,6},{6,4},{5,7},{7,5},{8,10},{10,8},{9,1... | collective-permute-start | bytes 663560 | tf_op jit(solution)/shard_map/ppermute | solution.py:479
  6.5 9.3 %collective-permute-start.2 = (bf16[576,128]{1,0:T(8,128)(2,1)S(1)}, bf16[576,128]{1,0:T(8,128)(2,1)S(1)}, u32[]{:S(2)}, u32[]{:S(2)}) collective-permute-start(bf16[576,128]{1,0:T(8,128)(2,1)S(1)} %get-tuple-element.33), channel_id=1, source_target_pairs={{4,0},{8,4},{12,8},{0,12},{5,1},{9,5},{13,9},{1,13},{6,2},{10,6},{... | collective-permute-start | bytes 442376 | tf_op jit(solution)/shard_map/ppermute | solution.py:523
  8.8 8.5 %collective-permute-start = (bf16[288,128]{1,0:T(8,128)(2,1)S(1)}, bf16[288,128]{1,0:T(8,128)(2,1)S(1)}, u32[]{:S(2)}, u32[]{:S(2)}) collective-permute-start(bf16[288,128]{1,0:T(8,128)(2,1)S(1)} %get-tuple-element.28), channel_id=1, source_target_pairs={{4,0},{8,4},{12,8},{0,12},{5,1},{9,5},{13,9},{1,13},{6,2},{10,6},{... | collective-permute-start | bytes 221192 | tf_op jit(solution)/shard_map/ppermute | solution.py:524
  17.9 1.4 %collective-permute-start.5 = (f32[2,3,2,16,128]{4,3,2,1,0:T(8,128)S(1)}, f32[2,3,2,16,128]{4,3,2,1,0:T(8,128)S(1)}, u32[]{:S(2)}, u32[]{:S(2)}) collective-permute-start(f32[2,3,2,16,128]{4,3,2,1,0:T(8,128)S(1)} %pad_maximum_fusion), channel_id=1, source_target_pairs={{0,1},{1,0},{2,3},{3,2},{4,5},{5,4},{6,7},{7,6},{8,9},{9,8},{10,11... | collective-permute-start | bytes 294920 | tf_op jit(solution)/shard_map/ppermute | solution.py:598
  19.3 4.2 %collective-permute-start.6 = (f32[3,2,16,128]{3,2,1,0:T(8,128)S(1)}, f32[3,2,16,128]{3,2,1,0:T(8,128)S(1)}, u32[]{:S(2)}, u32[]{:S(2)}) collective-permute-start(f32[3,2,16,128]{3,2,1,0:T(8,128)S(1)} %fusion), channel_id=1, source_target_pairs={{0,2},{2,0},{1,3},{3,1},{4,6},{6,4},{5,7},{7,5},{8,10},{10,8},{9,1... | collective-permute-start | bytes 147464 | tf_op jit(solution)/shard_map/ppermute | solution.py:599

commit v7 on v6

--- a/solution.py
+++ b/solution.py
@@ -373,7 +373,7 @@
             write(dacc, t, z, acc)
 
 
-def meson_slice(t, layers, weights, left, pieces, vectors):
+def meson_slice(t, layers, weights, left, pieces, vectors, first=0):
     rows = 2 * vectors
     left_rows = left.shape[1] // 2
     count = weights.shape[1] // 2
@@ -404,7 +404,7 @@
     for slot, piece in enumerate(pieces):
         for ri in range(2):
             top = slot * rows + ri * vectors
-            piece[t, ri] = total[top : top + vectors]
+            piece[t - first, ri] = total[top : top + vectors]
 
 
 def early_kernel(
@@ -430,10 +430,9 @@
 
 def late_kernel(
     times, depth, vectors,
-    block_ref, longf, edge, weights, left, dirac16_in, *rest,
+    block_ref, longf, edge, weights, left, dirac16_in,
+    dirac16, *pieces,
 ):
-    slots = len(rest) // 2
-    pieces_in, dirac16, pieces = rest[:slots], rest[slots], rest[slots + 1 :]
     long_l = Links(longf, times, depth)
     block = Field(block_ref, 1, depth, vectors)
     layers = []
@@ -442,34 +441,47 @@
         add_hop(acc, long_l, 0, 0, times - 1, z, block.read(0, z), False)
         write(dirac16, times - 1, z, acc)
         layers.append(acc)
-    meson_slice(times - 1, layers, weights, left, pieces, vectors)
+    meson_slice(times - 1, layers, weights, left, pieces, vectors, times - 1)
     for t in range(times - 1):
         dirac16[:, t] = dirac16_in[:, t]
-        for source, piece in zip(pieces_in, pieces):
-            piece[t] = source[t]
-
-
-def spread_kernel(dirac16, kept, arrived, out, partial, wide):
+
+
+def pair_kernel(*refs):
+    give, give_got, keep, keep_got = refs[:4]
+    send, partial = refs[-2:]
+    send[...] = give[...] + give_got[...]
+    partial[...] = keep[...] + keep_got[...]
+
+
+def spread_kernel(dirac16, *refs):
+    out, wide = refs[-2:]
     rows, vectors = dirac16.shape[0], dirac16.shape[1]
-    if partial is not None:
-        partial[...] = kept[...] + arrived[...]
     for r in range(rows):
         wide[pl.ds(r, vectors, stride=rows), :] = dirac16[r].astype(F32)
     out[...] = wide[...].astype(BF16)
 
 
-def turn_kernel(dirac16, out, wide):
-    spread_kernel(dirac16, None, None, out, None, wide)
-
-
-def final_kernel(partial, other, out):
-    times = partial.shape[0]
+def final_kernel(partial, other, partial_last, other_last, out):
+    early = partial.shape[0]
     width = out.shape[4]
-    for t in range(times):
+    for t in range(out.shape[1]):
         for ri in range(2):
-            total = partial[t, ri] + other[t, ri]
+            if t < early:
+                total = partial[t, ri] + other[t, ri]
+            else:
+                total = partial_last[t - early, ri] + other_last[t - early, ri]
             for p in range(out.shape[0]):
                 out[p, t, ri] = total[:, p * width : (p + 1) * width]
+
+
+def send_parts(pieces, after):
+    swap = [(0, 1), (1, 0)]
+    got = lax.ppermute(jnp.stack([pieces[1], pieces[3]]), "gy", swap)
+    shape = jax.ShapeDtypeStruct(pieces[0].shape, F32)
+    send, partial = call(pair_kernel, [shape] * 2, [VM] * (4 + len(after)), [], 1)(
+        pieces[2], got[1], pieces[0], got[0], *after
+    )
+    return send, partial, lax.ppermute(send, "gz", swap)
 
 
 def exchange(value, axis):
@@ -566,7 +578,10 @@
     )(
         pinned(current_dirs), pinned(taste_masks), packed, before_z, after_z, fatf, longf, dacc, back_xy
     )
-    piece = jax.ShapeDtypeStruct((times, 2, vectors, count * vectors), F32)
+
+    def piece_of(slices):
+        return jax.ShapeDtypeStruct((slices, 2, vectors, count * vectors), F32)
+
     (dacc,) = call(
         functools.partial(before_kernel, times, depth, vectors),
         [jax.ShapeDtypeStruct(shape6, F32)],
@@ -574,36 +589,36 @@
         [],
         1,
     )(before_t, fatf, longf, dacc)
-    finished = [jax.ShapeDtypeStruct(shape6, BF16)] + [piece] * slots
-    edge, *early = call(
+    odd16 = jax.ShapeDtypeStruct(shape6, BF16)
+    edge, dirac16, *early = call(
         functools.partial(early_kernel, times, depth, vectors),
-        [jax.ShapeDtypeStruct((3, 1) + shape6[2:], F32)] + finished,
+        [jax.ShapeDtypeStruct((3, 1) + shape6[2:], F32), odd16] + [piece_of(times - 1)] * slots,
         [VM] * 6,
         [],
         1,
     )(after_t, fatf, longf, dacc, weights, left)
-    dirac16, *pieces = call(
+    dirac16, *late = call(
         functools.partial(late_kernel, times, depth, vectors),
-        finished,
-        [VM] * (6 + slots),
+        [odd16] + [piece_of(1)] * slots,
+        [VM] * 6,
         [],
         1,
-    )(after_last, longf, edge, weights, left, *early)
+    )(after_last, longf, edge, weights, left, dirac16)
 
     odd_shape = rows_of(size)
     turned = dirac16.reshape(per_vector, vectors, LANES)
     scratch = [pltpu.VMEM((size, LANES), F32)]
     if rotate:
-        swap = [(0, 1), (1, 0)]
-        got = lax.ppermute(jnp.stack([pieces[1], pieces[3]]), "gy", swap)
-        other = lax.ppermute(pieces[2] + got[1], "gz", swap)
-        odd_rows, partial = call(
-            spread_kernel, [odd_shape, piece], [VM] * 3, scratch, 1
-        )(turned, pieces[0], got[0])
+        send, partial, other = send_parts(early, [])
+        _, partial_last, other_last = send_parts(late, [send])
+        (odd_rows,) = call(spread_kernel, [odd_shape], [VM] * 2, scratch, 1)(turned, partial_last)
         meson_shape = jax.ShapeDtypeStruct((count, times, 2, vectors, vectors), F32)
-        (meson_fields,) = call(final_kernel, [meson_shape], [VM] * 2, [], 1)(partial, other)
+        (meson_fields,) = call(final_kernel, [meson_shape], [VM] * 4, [], 1)(
+            partial, other, partial_last, other_last
+        )
     else:
-        (odd_rows,) = call(turn_kernel, [odd_shape], [VM], scratch, 1)(turned)
+        (odd_rows,) = call(spread_kernel, [odd_shape], [VM], scratch, 1)(turned)
+        pieces = [jnp.concatenate(pair, axis=0) for pair in zip(early, late)]
         whole = jnp.stack(pieces).reshape(slots, times, 2, vectors, count, vectors)
         whole = whole.transpose(0, 4, 1, 2, 3, 5).reshape(
             slots * count, times, 2, vectors, vectors

time: 24.5 us -> 24.6 us (level)
  starting transfers between devices: 10.3 us -> 11.4 us
  waiting for transfers between devices: 4.67 us -> 3.61 us
    ppermute x2 -> x4, starting transfers between devices: 1.66 us -> 2.78 us  [the longest x2 2.59 us: send_parts(): return (send, partial, lax.ppermute(send, 'gz', swap))]
    ppermute x2 -> x4, waiting for transfers between devices: 3.11 us -> 2.15 us  [the longest x2 2.04 us: send_parts(): return (send, partial, lax.ppermute(send, 'gz', swap))]
    pallas_call x3 -> x5, Pallas kernels: 2.2 us -> 2.21 us  [the longest x1 0.9 us: on_device(): call(final_kernel, [meson_shape], [VM] * 4, [], 1)]
  transfers between devices with their start and end apart: 7 -> 9, of which waited for: 4 -> 4; matrix products, arithmetic and copies ran while one was open for 0% -> 0% of each run, Pallas kernels for 24% -> 26%
where the time goes in v7:
time: 24.6 us; the launch traced here: 24.4 us
  starting transfers between devices  11.4 us (46%)
  Pallas kernels  8.65 us (35%)
  waiting for transfers between devices  3.61 us (15%)
  between operations  0.72 us (3%)
    ppermute x1, starting transfers between devices, on_device(): before_t = lax.ppermute(up_out, 'ta', up)  3.08 us
    pallas_call x1, Pallas kernels, on_device(): call(functools.partial(local_kernel, times, depth, vectors, (total_y, tot...  2.71 us
    ppermute x2, starting transfers between devices, send_parts(): return (send, partial, lax.ppermute(send, 'gz', swap))  2.59 us
    ppermute x1, starting transfers between devices, on_device(): after_t = lax.ppermute(down_out, 'ta', down)  2.25 us
    ppermute x2, waiting for transfers between devices, send_parts(): return (send, partial, lax.ppermute(send, 'gz', swap))  2.04 us
    ppermute x1, starting transfers between devices, on_device(): after_last = lax.ppermute(last_out, 'ta', down)  1.8 us
    ppermute x2, starting transfers between devices, exchange(): before = lax.ppermute(value, axis, up)  1.49 us
    pallas_call x1, Pallas kernels, on_device(): call(functools.partial(gather_kernel, times, depth, vectors), [rows_of(si...  1.3 us
  transfers between devices with their start and end apart: 9, of which 4 were waited for; matrix products, arithmetic and copies ran while one was open for 0% of the time, Pallas kernels for 26%

profile of v7, /device:TPU:0, one launch (start us, length us, event | category | flops | bytes accessed | tf_op | source)
XLA Modules:
  0.0 24.4 jit_solution(2785724840315999556)
XLA Ops:
  0.6 1.3 %shard_map.86 = (bf16[880,128]{1,0:T(8,128)(2,1)S(1)}, bf16[576,128]{1,0:T(8,128)(2,1)S(1)}, bf16[288,128]{1,0:T(8,128)(2,1)S(1)}, bf16[864,128]{1,0:T(8,128)(2,...) custom-call(s32[16]{0:T(128)} %chosen_hbm.1, bf16[1080,128]{1,0:T(8,128)(2,1)} %bitcast.33, ...), custom_call_target="tpu_custom_call" | custom-call | flops 1 | bytes 1 | tf_op jit(solution)/shard_map/pallas_call | solution.py:516
  1.9 3.1 %collective-permute-start.3 = (bf16[880,128]{1,0:T(8,128)(2,1)S(1)}, bf16[880,128]{1,0:T(8,128)(2,1)S(1)}, u32[]{:S(2)}, u32[]{:S(2)}) collective-permute-start(bf16[880,128]{1,0:T(8,128)(2,1)S(1)} %get-tuple-element.37), channel_id=1, source_target_pairs={{0,4},{4,8},{8,12},{12,0},{1,5},{5,9},{9,13},{13,1},{2,6},{6,10},{... | collective-permute-start | bytes 675848 | tf_op jit(solution)/shard_map/ppermute | solution.py:534
  5.0 0.0 collective-permute-start.1
  5.0 1.5 %collective-permute-start.4 = (bf16[864,128]{1,0:T(8,128)(2,1)S(1)}, bf16[864,128]{1,0:T(8,128)(2,1)S(1)}, u32[]{:S(2)}, u32[]{:S(2)}) collective-permute-start(bf16[864,128]{1,0:T(8,128)(2,1)S(1)} %get-tuple-element.33.field_ref), channel_id=1, source_target_pairs={{0,2},{2,0},{1,3},{3,1},{4,6},{6,4},{5,7},{7,5},{8,10},{10,8},{9,1... | collective-permute-start | bytes 663560 | tf_op jit(solution)/shard_map/ppermute | solution.py:491
  6.5 2.2 %collective-permute-start.2 = (bf16[576,128]{1,0:T(8,128)(2,1)S(1)}, bf16[576,128]{1,0:T(8,128)(2,1)S(1)}, u32[]{:S(2)}, u32[]{:S(2)}) collective-permute-start(bf16[576,128]{1,0:T(8,128)(2,1)S(1)} %get-tuple-element.35), channel_id=1, source_target_pairs={{4,0},{8,4},{12,8},{0,12},{5,1},{9,5},{13,9},{1,13},{6,2},{10,6},{... | collective-permute-start | bytes 442376 | tf_op jit(solution)/shard_map/ppermute | solution.py:535
  8.8 1.8 %collective-permute-start = (bf16[288,128]{1,0:T(8,128)(2,1)S(1)}, bf16[288,128]{1,0:T(8,128)(2,1)S(1)}, u32[]{:S(2)}, u32[]{:S(2)}) collective-permute-start(bf16[288,128]{1,0:T(8,128)(2,1)S(1)} %get-tuple-element.30), channel_id=1, source_target_pairs={{4,0},{8,4},{12,8},{0,12},{5,1},{9,5},{13,9},{1,13},{6,2},{10,6},{... | collective-permute-start | bytes 221192 | tf_op jit(solution)/shard_map/ppermute | solution.py:536
  10.6 0.0 collective-permute-done.1.y_ref
  10.6 2.7 %shard_map.87 = (f32[3,3,3,2,16,128]{5,4,3,2,1,0:T(8,128)S(1)}, f32[2,3,3,3,2,16,128]{6,5,4,3,2,1,0:T(8,128)S(1)}, f32[9,16,128]{2,1,0:T(8,128)S(1)}, f32[1296,128]{1,0:T(8,128)S(1)}, f32[1296,128]{1,0:T(8,128)S(1)}) custom-call(s32[3,8]{1,0:T(4,128)} %bitcast.35, bf16[1296,128]{1,0:T(8,128)(2,1)S(1)} %get-tuple-element.31.fat, ...), custom_call_target="tpu_custom_call" | custom-call | flops 1 | bytes 1 | tf_op jit(solution)/shard_map/pallas_call | solution.py:546
  13.3 0.0 collective-permute-done.4.before_ref.after_ref
  13.3 1.2 %shard_map.88 = (f32[3,3,3,2,16,128]{5,4,3,2,1,0:T(8,128)S(1)}, bf16[3,256,2304]{2,1,0:T(8,128)(2,1)S(1)}) custom-call(s32[4]{0:T(128)} %dirs_hbm.1, s32[4]{0:T(128)} %masks_hbm.1, bf16[864,128]{1,0:T(8,128)(2,1)S(1)} %get-tuple-element.33.field_ref, bf16[864,128]{1,0:T(8,128)(2,1)S(1)} %collective-permute-done.4.before_ref.after_ref, ...), custom_call_target="tpu_custom_call" | custom-call | flops 1 | bytes 1 | tf_op jit(solution)/shard_map/pallas_call | solution.py:564
  14.5 0.0 collective-permute-done.3.block_ref
  14.5 0.3 %shard_map.89.dacc = f32[3,3,3,2,16,128]{5,4,3,2,1,0:T(8,128)S(1)} custom-call(bf16[880,128]{1,0:T(8,128)(2,1)S(1)} %collective-permute-done.3.block_ref, f32[1296,128]{1,0:T(8,128)S(1)} %get-tuple-element.36.fatf, f32[1296,128]{1,0:T(8,128)S(1)} %get-tuple-element.34.longf, f32[3,3,3,2,16,128]{5,4,3,2,1,0:T(8,128)S(1)} %get-tuple-element.40.dacc_in), custom_call_target="tpu_custom_call" | custom-call | flops 1 | bytes 1 | tf_op jit(solution)/shard_map/pallas_call | solution.py:585
  14.8 1.0 %collective-permute-done.2.block_ref = bf16[576,128]{1,0:T(8,128)(2,1)S(1)} collective-permute-done((bf16[576,128]{1,0:T(8,128)(2,1)S(1)}, bf16[576,128]{1,0:T(8,128)(2,1)S(1)}, u32[]{:S(2)}, u32[]{:S(2)}) %collective-permute-start.2) | collective-permute-done | bytes 147488 | tf_op jit(solution)/shard_map/ppermute | solution.py:535
  15.8 1.0 %shard_map.90 = (f32[3,1,3,2,16,128]{5,4,3,2,1,0:T(8,128)S(1)}, bf16[3,3,3,2,16,128]{5,4,3,2,1,0:T(8,128)(2,1)S(1)}, f32[2,2,16,128]{3,2,1,0:T(8,128)S(1)}, f32[...) custom-call(bf16[576,128]{1,0:T(8,128)(2,1)S(1)} %collective-permute-done.2.block_ref, ...), custom_call_target="tpu_custom_call" | custom-call | flops 1 | bytes 1 | tf_op jit(solution)/shard_map/pallas_call | solution.py:593
  16.8 0.1 collective-permute-start.6
  16.8 0.5 %collective-permute-done.block_ref = bf16[288,128]{1,0:T(8,128)(2,1)S(1)} collective-permute-done((bf16[288,128]{1,0:T(8,128)(2,1)S(1)}, bf16[288,128]{1,0:T(8,128)(2,1)S(1)}, u32[]{:S(2)}, u32[]{:S(2)}) %collective-permute-start) | collective-permute-done | bytes 73760 | tf_op jit(solution)/shard_map/ppermute | solution.py:536
  17.3 0.6 %shard_map.91 = (bf16[3,3,3,2,16,128]{5,4,3,2,1,0:T(8,128)(2,1)S(1)}, f32[1,2,16,128]{3,2,1,0:T(8,128)S(1)}, f32[1,2,16,128]{3,2,1,0:T(8,128)S(1)}, f32[1,2,16,128]{3,2,1,0:T(8,128)S(1)}, f32[1,2,16,128]{3,2,1,0:T(8,128)S(1)}) custom-call(bf16[288,128]{1,0:T(8,128)(2,1)S(1)} %collective-permute-done.block_ref, f32[1296,128]{1,0:T(8,128)S(1)} %get-tuple-element.34.longf, ...), custom_call_target="tpu_custom_call" | custom-call | flops 1 | bytes 1 | tf_op jit(solution)/shard_map/pallas_call | solution.py:600
  17.9 0.1 collective-permute-start.5
  18.0 0.1 collective-permute-done.6
  18.1 1.6 %collective-permute-start.7 = (f32[2,2,16,128]{3,2,1,0:T(8,128)S(1)}, f32[2,2,16,128]{3,2,1,0:T(8,128)S(1)}, u32[]{:S(2)}, u32[]{:S(2)}) collective-permute-start(f32[2,2,16,128]{3,2,1,0:T(8,128)S(1)} %get-tuple-element.54.refs_4_), channel_id=1, source_target_pairs={{0,2},{2,0},{1,3},{3,1},{4,6},{6,4},{5,7},{7,5},{8,10},{10,8},{9,1... | collective-permute-start | bytes 98312 | tf_op jit(solution)/shard_map/ppermute | solution.py:484
  19.7 0.0 collective-permute-done.5
  19.7 1.0 %collective-permute-start.8 = (f32[1,2,16,128]{3,2,1,0:T(8,128)S(1)}, f32[1,2,16,128]{3,2,1,0:T(8,128)S(1)}, u32[]{:S(2)}, u32[]{:S(2)}) collective-permute-start(f32[1,2,16,128]{3,2,1,0:T(8,128)S(1)} %get-tuple-element.57), channel_id=1, source_target_pairs={{0,2},{2,0},{1,3},{3,1},{4,6},{6,4},{5,7},{7,5},{8,10},{10,8},{9,1... | collective-permute-start | bytes 49160 | tf_op jit(solution)/shard_map/ppermute | solution.py:484
  20.7 0.7 %shard_map.94 = bf16[864,128]{1,0:T(8,128)(2,1)} custom-call(bf16[54,16,128]{2,1,0:T(8,128)(2,1)S(1)} %bitcast.26, f32[1,2,16,128]{3,2,1,0:T(8,128)S(1)} %get-tuple-element.55.refs_0_.partial_last), custom_call_target="tpu_custom_call" | custom-call | flops 1 | bytes 1 | tf_op jit(solution)/shard_map/pallas_call | solution.py:614
  21.5 2.0 %collective-permute-done.8.other_last = f32[1,2,16,128]{3,2,1,0:T(8,128)S(1)} collective-permute-done((f32[1,2,16,128]{3,2,1,0:T(8,128)S(1)}, f32[1,2,16,128]{3,2,1,0:T(8,128)S(1)}, u32[]{:S(2)}, u32[]{:S(2)}) %collective-permute-start.8) | collective-permute-done | bytes 16416 | tf_op jit(solution)/shard_map/ppermute | solution.py:484
  23.5 0.0 collective-permute-done.7.other
  23.5 0.9 %shard_map.95 = f32[8,3,2,16,16]{4,3,2,1,0:T(8,128)} custom-call(f32[2,2,16,128]{3,2,1,0:T(8,128)S(1)} %get-tuple-element.56.partial, f32[2,2,16,128]{3,2,1,0:T(8,128)S(1)} %collective-permute-done.7.other, f32[1,2,16,128]{3,2,1,0:T(8,128)S(1)} %get-tuple-element.55.refs_0_.partial_last, f32[1,2,16,128]{3,2,1,0:T(8,128)S(1)} %collective-permute-done.8.other_last), custom_call_target="tpu_custom_call" | custom-call | flops 1 | bytes 1 | tf_op jit(solution)/shard_map/pallas_call | solution.py:616
  (6 shorter events, 0.0 us)
Async XLA Ops:
  1.9 12.6 %collective-permute-start.3 = (bf16[880,128]{1,0:T(8,128)(2,1)S(1)}, bf16[880,128]{1,0:T(8,128)(2,1)S(1)}, u32[]{:S(2)}, u32[]{:S(2)}) collective-permute-start(bf16[880,128]{1,0:T(8,128)(2,1)S(1)} %get-tuple-element.37), channel_id=1, source_target_pairs={{0,4},{4,8},{8,12},{12,0},{1,5},{5,9},{9,13},{13,1},{2,6},{6,10},{... | collective-permute-start | bytes 675848 | tf_op jit(solution)/shard_map/ppermute | solution.py:534
  5.0 5.5 %collective-permute-start.1 = (bf16[864,128]{1,0:T(8,128)(2,1)S(1)}, bf16[864,128]{1,0:T(8,128)(2,1)S(1)}, u32[]{:S(2)}, u32[]{:S(2)}) collective-permute-start(bf16[864,128]{1,0:T(8,128)(2,1)S(1)} %get-tuple-element.33.field_ref), channel_id=1, source_target_pairs={{0,1},{1,0},{2,3},{3,2},{4,5},{5,4},{6,7},{7,6},{8,9},{9,8},{10,11... | collective-permute-start | bytes 663560 | tf_op jit(solution)/shard_map/ppermute | solution.py:491
  5.0 8.3 %collective-permute-start.4 = (bf16[864,128]{1,0:T(8,128)(2,1)S(1)}, bf16[864,128]{1,0:T(8,128)(2,1)S(1)}, u32[]{:S(2)}, u32[]{:S(2)}) collective-permute-start(bf16[864,128]{1,0:T(8,128)(2,1)S(1)} %get-tuple-element.33.field_ref), channel_id=1, source_target_pairs={{0,2},{2,0},{1,3},{3,1},{4,6},{6,4},{5,7},{7,5},{8,10},{10,8},{9,1... | collective-permute-start | bytes 663560 | tf_op jit(solution)/shard_map/ppermute | solution.py:491
  6.5 9.3 %collective-permute-start.2 = (bf16[576,128]{1,0:T(8,128)(2,1)S(1)}, bf16[576,128]{1,0:T(8,128)(2,1)S(1)}, u32[]{:S(2)}, u32[]{:S(2)}) collective-permute-start(bf16[576,128]{1,0:T(8,128)(2,1)S(1)} %get-tuple-element.35), channel_id=1, source_target_pairs={{4,0},{8,4},{12,8},{0,12},{5,1},{9,5},{13,9},{1,13},{6,2},{10,6},{... | collective-permute-start | bytes 442376 | tf_op jit(solution)/shard_map/ppermute | solution.py:535
  8.8 8.5 %collective-permute-start = (bf16[288,128]{1,0:T(8,128)(2,1)S(1)}, bf16[288,128]{1,0:T(8,128)(2,1)S(1)}, u32[]{:S(2)}, u32[]{:S(2)}) collective-permute-start(bf16[288,128]{1,0:T(8,128)(2,1)S(1)} %get-tuple-element.30), channel_id=1, source_target_pairs={{4,0},{8,4},{12,8},{0,12},{5,1},{9,5},{13,9},{1,13},{6,2},{10,6},{... | collective-permute-start | bytes 221192 | tf_op jit(solution)/shard_map/ppermute | solution.py:536
  16.8 1.3 %collective-permute-start.6 = (f32[2,2,2,16,128]{4,3,2,1,0:T(8,128)S(1)}, f32[2,2,2,16,128]{4,3,2,1,0:T(8,128)S(1)}, u32[]{:S(2)}, u32[]{:S(2)}) collective-permute-start(f32[2,2,2,16,128]{4,3,2,1,0:T(8,128)S(1)} %pad_maximum_fusion), channel_id=1, source_target_pairs={{0,1},{1,0},{2,3},{3,2},{4,5},{5,4},{6,7},{7,6},{8,9},{9,8},{10,11... | collective-permute-start | bytes 196616 | tf_op jit(solution)/shard_map/ppermute | solution.py:479
  17.9 1.8 %collective-permute-start.5 = (f32[2,1,2,16,128]{4,3,2,1,0:T(8,128)S(1)}, f32[2,1,2,16,128]{4,3,2,1,0:T(8,128)S(1)}, u32[]{:S(2)}, u32[]{:S(2)}) collective-permute-start(f32[2,1,2,16,128]{4,3,2,1,0:T(8,128)S(1)} %pad_maximum_fusion.1), channel_id=1, source_target_pairs={{0,1},{1,0},{2,3},{3,2},{4,5},{5,4},{6,7},{7,6},{8,9},{9,8},{10,11... | collective-permute-start | bytes 98312 | tf_op jit(solution)/shard_map/ppermute | solution.py:479
  18.1 5.4 %collective-permute-start.7 = (f32[2,2,16,128]{3,2,1,0:T(8,128)S(1)}, f32[2,2,16,128]{3,2,1,0:T(8,128)S(1)}, u32[]{:S(2)}, u32[]{:S(2)}) collective-permute-start(f32[2,2,16,128]{3,2,1,0:T(8,128)S(1)} %get-tuple-element.54.refs_4_), channel_id=1, source_target_pairs={{0,2},{2,0},{1,3},{3,1},{4,6},{6,4},{5,7},{7,5},{8,10},{10,8},{9,1... | collective-permute-start | bytes 98312 | tf_op jit(solution)/shard_map/ppermute | solution.py:484
  19.7 3.8 %collective-permute-start.8 = (f32[1,2,16,128]{3,2,1,0:T(8,128)S(1)}, f32[1,2,16,128]{3,2,1,0:T(8,128)S(1)}, u32[]{:S(2)}, u32[]{:S(2)}) collective-permute-start(f32[1,2,16,128]{3,2,1,0:T(8,128)S(1)} %get-tuple-element.57), channel_id=1, source_target_pairs={{0,2},{2,0},{1,3},{3,1},{4,6},{6,4},{5,7},{7,5},{8,10},{10,8},{9,1... | collective-permute-start | bytes 49160 | tf_op jit(solution)/shard_map/ppermute | solution.py:484

commit v8 on v7

--- a/solution.py
+++ b/solution.py
@@ -461,17 +461,32 @@
     out[...] = wide[...].astype(BF16)
 
 
-def final_kernel(partial, other, partial_last, other_last, out):
-    early = partial.shape[0]
+def final_kernel(first, partial, other, *refs):
+    out, rows, sem = refs[-3:]
+    slices = partial.shape[0]
     width = out.shape[4]
-    for t in range(out.shape[1]):
+    for t in range(slices):
         for ri in range(2):
-            if t < early:
-                total = partial[t, ri] + other[t, ri]
-            else:
-                total = partial_last[t - early, ri] + other_last[t - early, ri]
+            total = partial[t, ri] + other[t, ri]
             for p in range(out.shape[0]):
-                out[p, t, ri] = total[:, p * width : (p + 1) * width]
+                rows[p, t, ri] = total[:, p * width : (p + 1) * width]
+    copy = pltpu.make_async_copy(rows, out.at[:, pl.ds(first, slices)], sem)
+    copy.start()
+    copy.wait()
+
+
+def finish(shape, first, partial, other, so_far):
+    rows = shape.shape[:1] + partial.shape[:1] + shape.shape[2:]
+    return pl.pallas_call(
+        functools.partial(final_kernel, first),
+        out_shape=shape,
+        in_specs=[VM] * 2 + [HB] * len(so_far),
+        out_specs=HB,
+        scratch_shapes=[pltpu.VMEM(rows, F32), pltpu.SemaphoreType.DMA],
+        input_output_aliases={2: 0} if so_far else {},
+        compiler_params=pltpu.CompilerParams(vmem_limit_bytes=40 * 1024 * 1024),
+        cost_estimate=pl.CostEstimate(flops=1, bytes_accessed=1, transcendentals=0),
+    )(partial, other, *so_far)
 
 
 def send_parts(pieces, after):
@@ -613,9 +628,8 @@
         _, partial_last, other_last = send_parts(late, [send])
         (odd_rows,) = call(spread_kernel, [odd_shape], [VM] * 2, scratch, 1)(turned, partial_last)
         meson_shape = jax.ShapeDtypeStruct((count, times, 2, vectors, vectors), F32)
-        (meson_fields,) = call(final_kernel, [meson_shape], [VM] * 4, [], 1)(
-            partial, other, partial_last, other_last
-        )
+        meson_fields = finish(meson_shape, 0, partial, other, [])
+        meson_fields = finish(meson_shape, times - 1, partial_last, other_last, [meson_fields])
     else:
         (odd_rows,) = call(spread_kernel, [odd_shape], [VM], scratch, 1)(turned)
         pieces = [jnp.concatenate(pair, axis=0) for pair in zip(early, late)]

time: 24.6 us -> 24.4 us (level)
  waiting for transfers between devices: 3.61 us -> 2.76 us
  Pallas kernels: 8.65 us -> 9.35 us
    ppermute x2, waiting for transfers between devices: 2.04 us -> 1.19 us  [send_parts(): return (send, partial, lax.ppermute(send, 'gz', swap))]
    pallas_call x1 -> x2, Pallas kernels: 0.9 us -> 1.6 us  [finish(): pl.pallas_call(functools.partial(final_kernel, first), out_shape=shape, i...]
  transfers between devices with their start and end apart: 9 -> 9, of which waited for: 4 -> 5; matrix products, arithmetic and copies ran while one was open for 0% -> 0% of each run, Pallas kernels for 26% -> 30%
where the time goes in v8:
time: 24.4 us; the launch traced here: 24.3 us
  starting transfers between devices  11.4 us (47%)
  Pallas kernels  9.35 us (38%)
  waiting for transfers between devices  2.76 us (11%)
  between operations  0.73 us (3%)
    ppermute x1, starting transfers between devices, on_device(): before_t = lax.ppermute(up_out, 'ta', up)  3.08 us
    pallas_call x1, Pallas kernels, on_device(): call(functools.partial(local_kernel, times, depth, vectors, (total_y, tot...  2.71 us
    ppermute x2, starting transfers between devices, send_parts(): return (send, partial, lax.ppermute(send, 'gz', swap))  2.59 us
    ppermute x1, starting transfers between devices, on_device(): after_t = lax.ppermute(down_out, 'ta', down)  2.25 us
    ppermute x1, starting transfers between devices, on_device(): after_last = lax.ppermute(last_out, 'ta', down)  1.8 us
    pallas_call x2, Pallas kernels, finish(): pl.pallas_call(functools.partial(final_kernel, first), out_shape=shape, i...  1.6 us
    ppermute x2, starting transfers between devices, exchange(): before = lax.ppermute(value, axis, up)  1.49 us
    pallas_call x1, Pallas kernels, on_device(): call(functools.partial(gather_kernel, times, depth, vectors), [rows_of(si...  1.3 us
  transfers between devices with their start and end apart: 9, of which 5 were waited for; matrix products, arithmetic and copies ran while one was open for 0% of the time, Pallas kernels for 30%

profile of v8, /device:TPU:0, one launch (start us, length us, event | category | flops | bytes accessed | tf_op | source)
XLA Modules:
  0.0 24.3 jit_solution(15352473709040854860)
XLA Ops:
  0.6 1.3 %shard_map.86 = (bf16[880,128]{1,0:T(8,128)(2,1)S(1)}, bf16[576,128]{1,0:T(8,128)(2,1)S(1)}, bf16[288,128]{1,0:T(8,128)(2,1)S(1)}, bf16[864,128]{1,0:T(8,128)(2,...) custom-call(s32[16]{0:T(128)} %chosen_hbm.1, bf16[1080,128]{1,0:T(8,128)(2,1)} %bitcast.33, ...), custom_call_target="tpu_custom_call" | custom-call | flops 1 | bytes 1 | tf_op jit(solution)/shard_map/pallas_call | solution.py:531
  1.9 3.1 %collective-permute-start.3 = (bf16[880,128]{1,0:T(8,128)(2,1)S(1)}, bf16[880,128]{1,0:T(8,128)(2,1)S(1)}, u32[]{:S(2)}, u32[]{:S(2)}) collective-permute-start(bf16[880,128]{1,0:T(8,128)(2,1)S(1)} %get-tuple-element.37), channel_id=1, source_target_pairs={{0,4},{4,8},{8,12},{12,0},{1,5},{5,9},{9,13},{13,1},{2,6},{6,10},{... | collective-permute-start | bytes 675848 | tf_op jit(solution)/shard_map/ppermute | solution.py:549
  5.0 0.0 collective-permute-start.1
  5.0 1.5 %collective-permute-start.4 = (bf16[864,128]{1,0:T(8,128)(2,1)S(1)}, bf16[864,128]{1,0:T(8,128)(2,1)S(1)}, u32[]{:S(2)}, u32[]{:S(2)}) collective-permute-start(bf16[864,128]{1,0:T(8,128)(2,1)S(1)} %get-tuple-element.33.field_ref), channel_id=1, source_target_pairs={{0,2},{2,0},{1,3},{3,1},{4,6},{6,4},{5,7},{7,5},{8,10},{10,8},{9,1... | collective-permute-start | bytes 663560 | tf_op jit(solution)/shard_map/ppermute | solution.py:506
  6.5 2.2 %collective-permute-start.2 = (bf16[576,128]{1,0:T(8,128)(2,1)S(1)}, bf16[576,128]{1,0:T(8,128)(2,1)S(1)}, u32[]{:S(2)}, u32[]{:S(2)}) collective-permute-start(bf16[576,128]{1,0:T(8,128)(2,1)S(1)} %get-tuple-element.35), channel_id=1, source_target_pairs={{4,0},{8,4},{12,8},{0,12},{5,1},{9,5},{13,9},{1,13},{6,2},{10,6},{... | collective-permute-start | bytes 442376 | tf_op jit(solution)/shard_map/ppermute | solution.py:550
  8.8 1.8 %collective-permute-start = (bf16[288,128]{1,0:T(8,128)(2,1)S(1)}, bf16[288,128]{1,0:T(8,128)(2,1)S(1)}, u32[]{:S(2)}, u32[]{:S(2)}) collective-permute-start(bf16[288,128]{1,0:T(8,128)(2,1)S(1)} %get-tuple-element.30), channel_id=1, source_target_pairs={{4,0},{8,4},{12,8},{0,12},{5,1},{9,5},{13,9},{1,13},{6,2},{10,6},{... | collective-permute-start | bytes 221192 | tf_op jit(solution)/shard_map/ppermute | solution.py:551
  10.6 0.0 collective-permute-done.1.y_ref
  10.6 2.7 %shard_map.87 = (f32[3,3,3,2,16,128]{5,4,3,2,1,0:T(8,128)S(1)}, f32[2,3,3,3,2,16,128]{6,5,4,3,2,1,0:T(8,128)S(1)}, f32[9,16,128]{2,1,0:T(8,128)S(1)}, f32[1296,128]{1,0:T(8,128)S(1)}, f32[1296,128]{1,0:T(8,128)S(1)}) custom-call(s32[3,8]{1,0:T(4,128)} %bitcast.35, bf16[1296,128]{1,0:T(8,128)(2,1)S(1)} %get-tuple-element.31.fat, ...), custom_call_target="tpu_custom_call" | custom-call | flops 1 | bytes 1 | tf_op jit(solution)/shard_map/pallas_call | solution.py:561
  13.3 0.0 collective-permute-done.4.before_ref.after_ref
  13.3 1.2 %shard_map.88 = (f32[3,3,3,2,16,128]{5,4,3,2,1,0:T(8,128)S(1)}, bf16[3,256,2304]{2,1,0:T(8,128)(2,1)S(1)}) custom-call(s32[4]{0:T(128)} %dirs_hbm.1, s32[4]{0:T(128)} %masks_hbm.1, bf16[864,128]{1,0:T(8,128)(2,1)S(1)} %get-tuple-element.33.field_ref, bf16[864,128]{1,0:T(8,128)(2,1)S(1)} %collective-permute-done.4.before_ref.after_ref, ...), custom_call_target="tpu_custom_call" | custom-call | flops 1 | bytes 1 | tf_op jit(solution)/shard_map/pallas_call | solution.py:579
  14.5 0.0 collective-permute-done.3.block_ref
  14.5 0.3 %shard_map.89.dacc = f32[3,3,3,2,16,128]{5,4,3,2,1,0:T(8,128)S(1)} custom-call(bf16[880,128]{1,0:T(8,128)(2,1)S(1)} %collective-permute-done.3.block_ref, f32[1296,128]{1,0:T(8,128)S(1)} %get-tuple-element.36.fatf, f32[1296,128]{1,0:T(8,128)S(1)} %get-tuple-element.34.longf, f32[3,3,3,2,16,128]{5,4,3,2,1,0:T(8,128)S(1)} %get-tuple-element.40.dacc_in), custom_call_target="tpu_custom_call" | custom-call | flops 1 | bytes 1 | tf_op jit(solution)/shard_map/pallas_call | solution.py:600
  14.8 1.0 %collective-permute-done.2.block_ref = bf16[576,128]{1,0:T(8,128)(2,1)S(1)} collective-permute-done((bf16[576,128]{1,0:T(8,128)(2,1)S(1)}, bf16[576,128]{1,0:T(8,128)(2,1)S(1)}, u32[]{:S(2)}, u32[]{:S(2)}) %collective-permute-start.2) | collective-permute-done | bytes 147488 | tf_op jit(solution)/shard_map/ppermute | solution.py:550
  15.8 1.0 %shard_map.90 = (f32[3,1,3,2,16,128]{5,4,3,2,1,0:T(8,128)S(1)}, bf16[3,3,3,2,16,128]{5,4,3,2,1,0:T(8,128)(2,1)S(1)}, f32[2,2,16,128]{3,2,1,0:T(8,128)S(1)}, f32[...) custom-call(bf16[576,128]{1,0:T(8,128)(2,1)S(1)} %collective-permute-done.2.block_ref, ...), custom_call_target="tpu_custom_call" | custom-call | flops 1 | bytes 1 | tf_op jit(solution)/shard_map/pallas_call | solution.py:608
  16.8 0.1 collective-permute-start.6
  16.8 0.5 %collective-permute-done.block_ref = bf16[288,128]{1,0:T(8,128)(2,1)S(1)} collective-permute-done((bf16[288,128]{1,0:T(8,128)(2,1)S(1)}, bf16[288,128]{1,0:T(8,128)(2,1)S(1)}, u32[]{:S(2)}, u32[]{:S(2)}) %collective-permute-start) | collective-permute-done | bytes 73760 | tf_op jit(solution)/shard_map/ppermute | solution.py:551
  17.3 0.6 %shard_map.91 = (bf16[3,3,3,2,16,128]{5,4,3,2,1,0:T(8,128)(2,1)S(1)}, f32[1,2,16,128]{3,2,1,0:T(8,128)S(1)}, f32[1,2,16,128]{3,2,1,0:T(8,128)S(1)}, f32[1,2,16,128]{3,2,1,0:T(8,128)S(1)}, f32[1,2,16,128]{3,2,1,0:T(8,128)S(1)}) custom-call(bf16[288,128]{1,0:T(8,128)(2,1)S(1)} %collective-permute-done.block_ref, f32[1296,128]{1,0:T(8,128)S(1)} %get-tuple-element.34.longf, ...), custom_call_target="tpu_custom_call" | custom-call | flops 1 | bytes 1 | tf_op jit(solution)/shard_map/pallas_call | solution.py:615
  17.9 0.1 collective-permute-start.5
  18.0 0.1 collective-permute-done.6
  18.1 1.6 %collective-permute-start.8 = (f32[2,2,16,128]{3,2,1,0:T(8,128)S(1)}, f32[2,2,16,128]{3,2,1,0:T(8,128)S(1)}, u32[]{:S(2)}, u32[]{:S(2)}) collective-permute-start(f32[2,2,16,128]{3,2,1,0:T(8,128)S(1)} %get-tuple-element.54.refs_4_), channel_id=1, source_target_pairs={{0,2},{2,0},{1,3},{3,1},{4,6},{6,4},{5,7},{7,5},{8,10},{10,8},{9,1... | collective-permute-start | bytes 98312 | tf_op jit(solution)/shard_map/ppermute | solution.py:499
  19.7 0.0 collective-permute-done.5
  19.7 1.0 %collective-permute-start.7 = (f32[1,2,16,128]{3,2,1,0:T(8,128)S(1)}, f32[1,2,16,128]{3,2,1,0:T(8,128)S(1)}, u32[]{:S(2)}, u32[]{:S(2)}) collective-permute-start(f32[1,2,16,128]{3,2,1,0:T(8,128)S(1)} %get-tuple-element.56), channel_id=1, source_target_pairs={{0,2},{2,0},{1,3},{3,1},{4,6},{6,4},{5,7},{7,5},{8,10},{10,8},{9,1... | collective-permute-start | bytes 49160 | tf_op jit(solution)/shard_map/ppermute | solution.py:499
  20.7 0.7 %shard_map.94 = bf16[864,128]{1,0:T(8,128)(2,1)} custom-call(bf16[54,16,128]{2,1,0:T(8,128)(2,1)S(1)} %bitcast.26, f32[1,2,16,128]{3,2,1,0:T(8,128)S(1)} %get-tuple-element.55.refs_0_.partial), custom_call_target="tpu_custom_call" | custom-call | flops 1 | bytes 1 | tf_op jit(solution)/shard_map/pallas_call | solution.py:629
  21.5 0.6 %collective-permute-done.8.other = f32[2,2,16,128]{3,2,1,0:T(8,128)S(1)} collective-permute-done((f32[2,2,16,128]{3,2,1,0:T(8,128)S(1)}, f32[2,2,16,128]{3,2,1,0:T(8,128)S(1)}, u32[]{:S(2)}, u32[]{:S(2)}) %collective-permute-start.8) | collective-permute-done | bytes 32800 | tf_op jit(solution)/shard_map/ppermute | solution.py:499
  22.1 0.8 %shard_map.95.refs_0_ = f32[8,3,2,16,16]{4,3,2,1,0:T(8,128)} custom-call(f32[2,2,16,128]{3,2,1,0:T(8,128)S(1)} %get-tuple-element.57.partial, f32[2,2,16,128]{3,2,1,0:T(8,128)S(1)} %collective-permute-done.8.other), custom_call_target="tpu_custom_call" | custom-call | flops 1 | bytes 1 | tf_op jit(solution)/shard_map/pallas_call | solution.py:480
  22.9 0.6 %collective-permute-done.7.other = f32[1,2,16,128]{3,2,1,0:T(8,128)S(1)} collective-permute-done((f32[1,2,16,128]{3,2,1,0:T(8,128)S(1)}, f32[1,2,16,128]{3,2,1,0:T(8,128)S(1)}, u32[]{:S(2)}, u32[]{:S(2)}) %collective-permute-start.7) | collective-permute-done | bytes 16416 | tf_op jit(solution)/shard_map/ppermute | solution.py:499
  23.5 0.8 %shard_map.96 = f32[8,3,2,16,16]{4,3,2,1,0:T(8,128)} custom-call(f32[1,2,16,128]{3,2,1,0:T(8,128)S(1)} %get-tuple-element.55.refs_0_.partial, f32[1,2,16,128]{3,2,1,0:T(8,128)S(1)} %collective-permute-done.7.other, f32[8,3,2,16,16]{4,3,2,1,0:T(8,128)} %shard_map.95.refs_0_), custom_call_target="tpu_custom_call", output_to_operand_aliasing={{}: (2, {})} | custom-call | flops 1 | bytes 1 | tf_op jit(solution)/shard_map/pallas_call | solution.py:480
  (6 shorter events, 0.0 us)
Async XLA Ops:
  1.9 12.6 %collective-permute-start.3 = (bf16[880,128]{1,0:T(8,128)(2,1)S(1)}, bf16[880,128]{1,0:T(8,128)(2,1)S(1)}, u32[]{:S(2)}, u32[]{:S(2)}) collective-permute-start(bf16[880,128]{1,0:T(8,128)(2,1)S(1)} %get-tuple-element.37), channel_id=1, source_target_pairs={{0,4},{4,8},{8,12},{12,0},{1,5},{5,9},{9,13},{13,1},{2,6},{6,10},{... | collective-permute-start | bytes 675848 | tf_op jit(solution)/shard_map/ppermute | solution.py:549
  5.0 5.5 %collective-permute-start.1 = (bf16[864,128]{1,0:T(8,128)(2,1)S(1)}, bf16[864,128]{1,0:T(8,128)(2,1)S(1)}, u32[]{:S(2)}, u32[]{:S(2)}) collective-permute-start(bf16[864,128]{1,0:T(8,128)(2,1)S(1)} %get-tuple-element.33.field_ref), channel_id=1, source_target_pairs={{0,1},{1,0},{2,3},{3,2},{4,5},{5,4},{6,7},{7,6},{8,9},{9,8},{10,11... | collective-permute-start | bytes 663560 | tf_op jit(solution)/shard_map/ppermute | solution.py:506
  5.0 8.3 %collective-permute-start.4 = (bf16[864,128]{1,0:T(8,128)(2,1)S(1)}, bf16[864,128]{1,0:T(8,128)(2,1)S(1)}, u32[]{:S(2)}, u32[]{:S(2)}) collective-permute-start(bf16[864,128]{1,0:T(8,128)(2,1)S(1)} %get-tuple-element.33.field_ref), channel_id=1, source_target_pairs={{0,2},{2,0},{1,3},{3,1},{4,6},{6,4},{5,7},{7,5},{8,10},{10,8},{9,1... | collective-permute-start | bytes 663560 | tf_op jit(solution)/shard_map/ppermute | solution.py:506
  6.5 9.3 %collective-permute-start.2 = (bf16[576,128]{1,0:T(8,128)(2,1)S(1)}, bf16[576,128]{1,0:T(8,128)(2,1)S(1)}, u32[]{:S(2)}, u32[]{:S(2)}) collective-permute-start(bf16[576,128]{1,0:T(8,128)(2,1)S(1)} %get-tuple-element.35), channel_id=1, source_target_pairs={{4,0},{8,4},{12,8},{0,12},{5,1},{9,5},{13,9},{1,13},{6,2},{10,6},{... | collective-permute-start | bytes 442376 | tf_op jit(solution)/shard_map/ppermute | solution.py:550
  8.8 8.5 %collective-permute-start = (bf16[288,128]{1,0:T(8,128)(2,1)S(1)}, bf16[288,128]{1,0:T(8,128)(2,1)S(1)}, u32[]{:S(2)}, u32[]{:S(2)}) collective-permute-start(bf16[288,128]{1,0:T(8,128)(2,1)S(1)} %get-tuple-element.30), channel_id=1, source_target_pairs={{4,0},{8,4},{12,8},{0,12},{5,1},{9,5},{13,9},{1,13},{6,2},{10,6},{... | collective-permute-start | bytes 221192 | tf_op jit(solution)/shard_map/ppermute | solution.py:551
  16.8 1.3 %collective-permute-start.6 = (f32[2,2,2,16,128]{4,3,2,1,0:T(8,128)S(1)}, f32[2,2,2,16,128]{4,3,2,1,0:T(8,128)S(1)}, u32[]{:S(2)}, u32[]{:S(2)}) collective-permute-start(f32[2,2,2,16,128]{4,3,2,1,0:T(8,128)S(1)} %pad_maximum_fusion), channel_id=1, source_target_pairs={{0,1},{1,0},{2,3},{3,2},{4,5},{5,4},{6,7},{7,6},{8,9},{9,8},{10,11... | collective-permute-start | bytes 196616 | tf_op jit(solution)/shard_map/ppermute | solution.py:494
  17.9 1.8 %collective-permute-start.5 = (f32[2,1,2,16,128]{4,3,2,1,0:T(8,128)S(1)}, f32[2,1,2,16,128]{4,3,2,1,0:T(8,128)S(1)}, u32[]{:S(2)}, u32[]{:S(2)}) collective-permute-start(f32[2,1,2,16,128]{4,3,2,1,0:T(8,128)S(1)} %pad_maximum_fusion.1), channel_id=1, source_target_pairs={{0,1},{1,0},{2,3},{3,2},{4,5},{5,4},{6,7},{7,6},{8,9},{9,8},{10,11... | collective-permute-start | bytes 98312 | tf_op jit(solution)/shard_map/ppermute | solution.py:494
  18.1 4.0 %collective-permute-start.8 = (f32[2,2,16,128]{3,2,1,0:T(8,128)S(1)}, f32[2,2,16,128]{3,2,1,0:T(8,128)S(1)}, u32[]{:S(2)}, u32[]{:S(2)}) collective-permute-start(f32[2,2,16,128]{3,2,1,0:T(8,128)S(1)} %get-tuple-element.54.refs_4_), channel_id=1, source_target_pairs={{0,2},{2,0},{1,3},{3,1},{4,6},{6,4},{5,7},{7,5},{8,10},{10,8},{9,1... | collective-permute-start | bytes 98312 | tf_op jit(solution)/shard_map/ppermute | solution.py:499
  19.7 3.8 %collective-permute-start.7 = (f32[1,2,16,128]{3,2,1,0:T(8,128)S(1)}, f32[1,2,16,128]{3,2,1,0:T(8,128)S(1)}, u32[]{:S(2)}, u32[]{:S(2)}) collective-permute-start(f32[1,2,16,128]{3,2,1,0:T(8,128)S(1)} %get-tuple-element.56), channel_id=1, source_target_pairs={{0,2},{2,0},{1,3},{3,1},{4,6},{6,4},{5,7},{7,5},{8,10},{10,8},{9,1... | collective-permute-start | bytes 49160 | tf_op jit(solution)/shard_map/ppermute | solution.py:499
